TPU v7x, 256 devices: a whole 4x4x8 slice. The times are simulated.
256 devices in a mesh: dp: 64 (over y_hi, z, x), tensor: 4 (over y_lo, core).
Axes of the slice: x: 4, y: 4 (y_hi: 2, y_lo: 2; y = y_hi * 2 + y_lo), z: 8, core: 2. Of those that a mesh axis runs over, the one named last changes fastest.
Arguments:
- image_feats: bfloat16 [12288, 1152], P('dp', 'tensor'), may hold values from -6 to 6
- text_feats: bfloat16 [12288, 1152], P('dp', 'tensor'), may hold values from -6 to 6
- image_proj: bfloat16 [1152, 1152], P('tensor'), may hold values from -0.1875 to 0.1875
- text_proj: bfloat16 [1152, 1152], P('tensor'), may hold values from -0.1875 to 0.1875
Outputs:
- grad_image_feats: bfloat16 [12288, 1152], P('dp', 'tensor')
- grad_text_feats: bfloat16 [12288, 1152], P('dp', 'tensor')
- grad_image_proj: float32 [1152, 1152], P('tensor')
- text_head_gradient: float32 [1152, 1152], P('tensor')
All inputs are finite; a program needn't handle non-finite values.
Results may differ from a plain program's by a relative error of at most 0.02.
Values may be sent and summed in bfloat16 or wider, within the bound.
No kernel may reach another device: no remote copies, remote signals or barrier semaphores. Data moves between devices by JAX's collectives and lax.ppermute only.
A program may use at most 64 MiB of HBM per device.

v0:
```python
import jax
import jax.numpy as jnp
from jax import lax
from jax.sharding import Mesh, PartitionSpec as P

SCALE = 10.0
OFFSET = -4.0
EPSILON = 1e-06
F32 = jnp.float32
BF16 = jnp.bfloat16

AXES = ("yhi", "z", "x", "ylo", "core")
PLANE = ("yhi", "x", "ylo")
TENSOR = ("ylo", "core")
LANES = 128


def shift(value, axis, by):
    n = lax.axis_size(axis)
    return lax.ppermute(value, axis, [(i, (i + by) % n) for i in range(n)])


def flip(value, axis, bit):
    n = lax.axis_size(axis)
    return lax.ppermute(value, axis, [(i, i ^ bit) for i in range(n)])


def broadcast_gather(value, axes, members):
    return lax.all_to_all(jnp.broadcast_to(value[None], (members,) + value.shape), axes, 0, 0)


def normalize(raw):
    radius = jnp.sqrt(jnp.sum(raw * raw, axis=1, keepdims=True) + EPSILON)
    return (raw / radius, radius)


def backnorm(unit, radius, grad):
    return ((grad - unit * jnp.sum(unit * grad, axis=1, keepdims=True)) / radius).astype(BF16)


def core_half(partial):
    core = lax.axis_index("core")
    rows, width = partial.shape
    parts = partial.reshape(2, 2, rows // 4, width)
    keep = lax.dynamic_index_in_dim(parts, core, 1, keepdims=False)
    send = lax.dynamic_index_in_dim(parts, 1 - core, 1, keepdims=False)
    return keep + flip(send.astype(BF16), "core", 1).astype(F32)


def quarter_rows(half):
    ylo = lax.axis_index("ylo")
    keep = lax.dynamic_index_in_dim(half, ylo, 0, keepdims=False)
    send = lax.dynamic_index_in_dim(half, 1 - ylo, 0, keepdims=False)
    return keep + flip(send.astype(BF16), "ylo", 1).astype(F32)


def column_shift(value, by):
    n = lax.axis_size("z")
    pairs = [(2 * z, (z + by) % n * 2) for z in range(n)]
    pairs += [(2 * z + 1, (z - by) % n * 2 + 1) for z in range(n)]
    return lax.ppermute(value, ("z", "core"), pairs)


def column_gather(value):
    first = lax.axis_index("core") == 0
    other = flip(value, "core", 1)
    pair = jnp.concatenate([jnp.where(first, value, other), jnp.where(first, other, value)], axis=0)
    far = column_shift(value, 4)
    got = {k: column_shift(pair, k) for k in (3, 2, 1)}
    mine = jnp.concatenate([got[1], got[2], got[3], far], axis=0)
    return jnp.concatenate([pair, mine, flip(mine, "core", 1)], axis=0)


def column_sum(parts, rows):
    first = lax.axis_index("core") == 0
    own = parts[: 2 * rows].astype(F32)
    far = 9 * rows
    mine = parts[2 * rows : far].astype(F32) + flip(parts[far:], "core", 1).astype(F32)
    mine = mine.astype(BF16)
    half = column_shift(mine[6 * rows :], -4).astype(F32)
    for k in (3, 2, 1):
        own = own + column_shift(mine[2 * rows * (k - 1) : 2 * rows * k], -k).astype(F32)
    send = jnp.where(first, own[rows:], own[:rows]).astype(BF16)
    return jnp.where(first, own[:rows], own[rows:]) + half + flip(send, "core", 1).astype(F32)


def to_tiles(grad, pieces):
    rows, width = grad.shape
    count = rows * width // (8 * LANES)
    each = -(-count // pieces)
    tiles = grad.reshape(rows // 8, 8, width // LANES, LANES).transpose(0, 2, 1, 3)
    tiles = tiles.reshape(count, 8, LANES)
    tiles = jnp.pad(tiles, ((0, pieces * each - count), (0, 0), (0, 0)))
    return tiles.reshape(pieces, each * 8, LANES)


def from_tiles(tiles, rows, width):
    count = rows * width // (8 * LANES)
    tiles = tiles.reshape(-1, 8, LANES)[:count].reshape(rows // 8, width // LANES, 8, LANES)
    return tiles.transpose(0, 2, 1, 3).reshape(rows, width)


def column_scatter_sum(tiles):
    z, n = lax.axis_index("z"), lax.axis_size("z")
    sign = 1 - 2 * lax.axis_index("core")

    def block(k):
        return lax.dynamic_index_in_dim(tiles, (z + n + k) % n, 0, keepdims=False)

    away = jnp.stack([block(-sign * k) for k in (1, 2, 3)]).astype(BF16)
    got = flip(away, "core", 1)
    mine = block(0) + column_shift(block(4).astype(BF16), 4).astype(F32)
    pairs = {
        k: column_shift(jnp.stack([block(sign * k).astype(BF16), got[k - 1]]), k) for k in (3, 2, 1)
    }
    theirs = sum(pairs[k][1].astype(F32) for k in (1, 2, 3)).astype(BF16)
    mine = mine + sum(pairs[k][0].astype(F32) for k in (1, 2, 3))
    return mine + flip(theirs, "core", 1).astype(F32)


def column_spread(value):
    z, n = lax.axis_index("z"), lax.axis_size("z")
    first = lax.axis_index("core") == 0
    pair = jnp.stack([value, flip(value, "core", 1)])
    far = column_shift(value, 4)
    got = {k: column_shift(pair, k) for k in (3, 2, 1)}
    far, got = lax.optimization_barrier((far, got))
    swapped = flip(jnp.stack([got[k][1] for k in (1, 2, 3)]), "core", 1)
    above = [jnp.where(first, swapped[k - 1], got[k][0]) for k in (1, 2, 3)]
    below = [jnp.where(first, got[k][0], swapped[k - 1]) for k in (3, 2, 1)]
    ring = [value] + above + [far] + below
    return lax.dynamic_slice_in_dim(jnp.stack(ring + ring), (n - z) % n, n, 0)


def dp_sum(grads):
    x = lax.axis_index("x")
    rows, width = grads[0].shape
    unit = rows // 4
    half = (unit + 8) // 16 * 8

    def part(k):
        start = (x + k) % 4 * unit
        return jnp.stack([lax.dynamic_slice_in_dim(g, start, unit, 0) for g in grads])

    far = part(2).astype(BF16)
    up = shift(far[:, :half], "x", 1)
    down = shift(far[:, half:], "x", -1)
    right, left = part(1), part(3)
    up = jnp.concatenate([right[:, :half] + up.astype(F32), right[:, half:]], axis=1)
    down = jnp.concatenate([left[:, :half], left[:, half:] + down.astype(F32)], axis=1)
    up = shift(up.astype(BF16), "x", 1)
    down = shift(down.astype(BF16), "x", -1)
    mine = part(0) + up.astype(F32) + down.astype(F32)
    tiles = to_tiles(mine.reshape(2 * unit, width), lax.axis_size("z"))
    sent = column_scatter_sum(tiles).astype(BF16)
    total = (sent.astype(F32) + flip(sent, "yhi", 1).astype(F32)).astype(BF16)
    mine = from_tiles(column_spread(total), 2 * unit, width).reshape(2, unit, width)
    from_left = shift(mine, "x", 1)
    from_right = shift(mine, "x", -1)
    up = shift(from_left[:, :half], "x", 1)
    down = shift(from_right[:, half:], "x", -1)
    out = []
    for h in range(2):
        whole = jnp.zeros((rows, width), F32)
        far = jnp.concatenate([up[h], down[h]], axis=0)
        for k, value in enumerate((mine[h], from_right[h], far, from_left[h])):
            place = (x + k) % 4 * unit
            whole = lax.dynamic_update_slice_in_dim(whole, value.astype(F32), place, 0)
        out.append(whole)
    return out


def per_device(image_feats, text_feats, image_proj, text_proj):
    width = image_proj.shape[1]
    quarter = image_feats.shape[0] // 4
    plane = 16

    image_half = core_half(jnp.dot(image_feats, image_proj, preferred_element_type=F32))
    text_half = core_half(jnp.dot(text_feats, text_proj, preferred_element_type=F32))
    image_unit, image_radius = normalize(quarter_rows(image_half))
    text_half, image_unit = lax.optimization_barrier((text_half, image_unit))
    text_unit, text_radius = normalize(quarter_rows(text_half))
    images = broadcast_gather(image_unit.astype(BF16), PLANE, plane).reshape(-1, width)
    texts = column_gather(text_unit.astype(BF16))
    own_image = lax.axis_index(PLANE) * quarter
    own_text = lax.axis_index("core") * quarter
    scores = lax.dot_general(images, texts, (((1,), (1,)), ((), ())), preferred_element_type=F32)
    row_id = lax.broadcasted_iota(jnp.int32, scores.shape, 0)
    col_id = lax.broadcasted_iota(jnp.int32, scores.shape, 1)
    label = (row_id - own_image == col_id - own_text) & (col_id // quarter == own_text // quarter)
    weights = (SCALE * (jax.nn.sigmoid(SCALE * scores + OFFSET) - label.astype(F32))).astype(BF16)

    image_part = jnp.dot(weights, texts, preferred_element_type=F32).astype(BF16)
    weights, image_part = lax.optimization_barrier((weights, image_part))
    text_part = lax.dot_general(
        weights, images, (((0,), (0,)), ((), ())), preferred_element_type=F32
    )
    image_sent = lax.all_to_all(image_part.reshape(plane, quarter, width), PLANE, 0, 0)
    grad_text_emb = column_sum(text_part.astype(BF16), quarter)
    text_grad_raw = backnorm(text_unit, text_radius, grad_text_emb)
    grad_image_emb = jnp.sum(image_sent.astype(F32), axis=0)
    image_grad_raw = backnorm(image_unit, image_radius, grad_image_emb)

    pieces = lax.all_gather(
        jnp.concatenate([image_grad_raw, text_grad_raw], axis=1), TENSOR, axis=0, tiled=True
    )
    piece_image, piece_text = pieces[:, :width], pieces[:, width:]

    def back(piece, proj):
        return lax.dot_general(
            piece, proj, (((1,), (1,)), ((), ())), preferred_element_type=F32
        ).astype(BF16)

    def outer(feats, piece):
        return lax.dot_general(feats, piece, (((0,), (0,)), ((), ())), preferred_element_type=F32)

    grad_image_w, grad_text_w = dp_sum(
        [outer(image_feats, piece_image), outer(text_feats, piece_text)]
    )
    return (
        back(piece_image, image_proj),
        back(piece_text, text_proj),
        grad_image_w,
        grad_text_w,
    )


def solution(mesh):
    fine = Mesh(mesh.devices.reshape(2, 8, 4, 2, 2), AXES)
    feats = P(("yhi", "z", "x"), TENSOR)
    proj = P(TENSOR, None)
    return jax.shard_map(
        per_device,
        mesh=fine,
        in_specs=(feats, feats, proj, proj),
        out_specs=(feats, feats, proj, proj),
        check_vma=False,
    )
```

profile of v0, /device:TPU:32, one launch (start us, length us, event | category | flops | bytes accessed | tf_op | source)
XLA Modules:
  0.0 198.3 jit_solution(2430087391118754752)
XLA Ops:
  5.7 3.5 %collective-permute-done.2 = bf16[48,1152]{1,0:T(8,128)(2,1)S(1)} collective-permute-done((bf16[48,1152]{1,0:T(8,128)(2,1)S(1)}, bf16[48,1152]{1,0:T(8,128)(2,1)S(1)}, u32[]{:S(2)}, u32[]{:S(2)}) %collective-permute-start.2) | collective-permute-done | bytes 110624 | tf_op jit(solution)/shard_map/ppermute | solution.py:25
  11.1 3.2 %collective-permute-done.3 = bf16[48,1152]{1,0:T(8,128)(2,1)S(1)} collective-permute-done((bf16[48,1152]{1,0:T(8,128)(2,1)S(1)}, bf16[48,1152]{1,0:T(8,128)(2,1)S(1)}, u32[]{:S(2)}, u32[]{:S(2)}) %collective-permute-start.3) | collective-permute-done | bytes 110624 | tf_op jit(solution)/shard_map/ppermute | solution.py:25
  16.5 7.0 %all-to-all-start = ((bf16[16,48,1152]{2,1,0:T(8,128)(2,1)}), bf16[16,48,1152]{2,1,0:T(8,128)(2,1)S(1)}, u32[]{:S(2)}, u32[]{:S(2)}) async-start(bf16[16,48,1152]{2,1,0:T(8,128)(2,1)} %broadcast_in_dim.2), calls=%async_computation | async-start | bytes 3538944 | tf_op jit(solution)/shard_map/all_to_all | solution.py:29
  24.9 2.0 %collective-permute-start.5 = (bf16[96,1152]{1,0:T(8,128)(2,1)S(1)}, bf16[96,1152]{1,0:T(8,128)(2,1)S(1)}, u32[]{:S(2)}, u32[]{:S(2)}) collective-permute-start(bf16[96,1152]{1,0:T(8,128)(2,1)S(1)} %pad_maximum_fusion.5), channel_id=1, source_target_pairs={{0,16},{16,32},{32,48},{48,64},{64,80},{80,96},{96,112},{112,0},{1... | collective-permute-start | bytes 663560 | tf_op jit(solution)/shard_map/ppermute | solution.py:61
  26.9 4.5 %collective-permute-start.6 = (bf16[96,1152]{1,0:T(8,128)(2,1)S(1)}, bf16[96,1152]{1,0:T(8,128)(2,1)S(1)}, u32[]{:S(2)}, u32[]{:S(2)}) collective-permute-start(bf16[96,1152]{1,0:T(8,128)(2,1)S(1)} %pad_maximum_fusion.5), channel_id=1, source_target_pairs={{0,32},{16,48},{32,64},{48,80},{64,96},{80,112},{96,0},{112,16},{1... | collective-permute-start | bytes 663560 | tf_op jit(solution)/shard_map/ppermute | solution.py:61
  31.4 1.9 collective-permute-start.7
  34.8 11.9 %collective-permute-done.8 = bf16[48,1152]{1,0:T(8,128)(2,1)S(1)} collective-permute-done((bf16[48,1152]{1,0:T(8,128)(2,1)S(1)}, bf16[48,1152]{1,0:T(8,128)(2,1)S(1)}, u32[]{:S(2)}, u32[]{:S(2)}) %collective-permute-start.8) | collective-permute-done | bytes 110624 | tf_op jit(solution)/shard_map/ppermute | solution.py:61
  47.1 5.2 %collective-permute-start.9 = (bf16[336,1152]{1,0:T(8,128)(2,1)S(1)}, bf16[336,1152]{1,0:T(8,128)(2,1)S(1)}, u32[]{:S(2)}, u32[]{:S(2)}) collective-permute-start(bf16[336,1152]{1,0:T(8,128)(2,1)S(1)} %pad_maximum_fusion), channel_id=1, source_target_pairs={{0,1},{1,0},{2,3},{3,2},{4,5},{5,4},{6,7},{7,6},{8,9},{9,8},{10,11... | collective-permute-start | bytes 2322440 | tf_op jit(solution)/shard_map/ppermute | solution.py:25
  56.0 3.5 %multiply_convert_fusion = bf16[768,768]{1,0:T(8,128)(2,1)S(1)} fusion(bf16[768,1152]{1,0:T(8,128)(2,1)S(1)} %bitcast.165, bf16[768,1152]{1,0:T(8,128)(2,1)} %constant_dynamic-update-slice_fusion, s32[]{:T(128)S(6)} %select_n.214, s32[768]{0:T(1024)S(1)} %iota_divide_fusion, s32[768]{0:T(1024)S(1)} %broadcast_add_fusion, s32[768]{0:T(1024)S(1)} %iota_subtract_fusion, ...), kind=kOutput, calls=%fused_computation.3 | convolution fusion | flops 1366622208 | bytes 4731652 | tf_op jit(solution)/shard_map/dot_general | solution.py:187
  59.5 4.4 %convolution_convert_fusion.1 = bf16[768,1152]{1,0:T(8,128)(2,1)} fusion(bf16[768,768]{1,0:T(8,128)(2,1)S(1)} %multiply_convert_fusion, bf16[768,1152]{1,0:T(8,128)(2,1)} %constant_dynamic-update-slice_fusion), kind=kOutput, calls=%fused_computation.2 | convolution fusion | flops 1359839232 | bytes 4718592 | tf_op jit(solution)/shard_map/dot_general | solution.py:193
  67.8 7.0 %all-to-all-start.1 = ((bf16[16,48,1152]{2,1,0:T(8,128)(2,1)}), bf16[16,48,1152]{2,1,0:T(8,128)(2,1)S(1)}, u32[]{:S(2)}, u32[]{:S(2)}) async-start(bf16[16,48,1152]{2,1,0:T(8,128)(2,1)} %bitcast.164), calls=%async_computation.1 | async-start | bytes 3538944 | tf_op jit(solution)/shard_map/all_to_all | solution.py:198
  78.1 4.3 %collective-permute-start.11 = (bf16[96,1152]{1,0:T(8,128)(2,1)}, bf16[96,1152]{1,0:T(8,128)(2,1)S(1)}, u32[]{:S(2)}, u32[]{:S(2)}) collective-permute-start(bf16[96,1152]{1,0:T(8,128)(2,1)} %get-tuple-element.34), channel_id=1, source_target_pairs={{0,80},{16,96},{32,112},{48,0},{64,16},{80,32},{96,48},{112,64},{1... | collective-permute-start | bytes 663560 | tf_op jit(solution)/shard_map/ppermute | solution.py:61
  84.5 2.9 %collective-permute-start.14 = (bf16[48,1152]{1,0:T(8,128)(2,1)}, bf16[48,1152]{1,0:T(8,128)(2,1)}, u32[]{:S(2)}, u32[]{:S(2)}) collective-permute-start(bf16[48,1152]{1,0:T(8,128)(2,1)} %slice.212), channel_id=1, source_target_pairs={{0,64},{16,80},{32,96},{48,112},{64,0},{80,16},{96,32},{112,48},{1... | collective-permute-start | bytes 331784 | tf_op jit(solution)/shard_map/ppermute | solution.py:61
  87.3 5.4 %collective-permute-done.11 = bf16[96,1152]{1,0:T(8,128)(2,1)S(1)} collective-permute-done((bf16[96,1152]{1,0:T(8,128)(2,1)}, bf16[96,1152]{1,0:T(8,128)(2,1)S(1)}, u32[]{:S(2)}, u32[]{:S(2)}) %collective-permute-start.11) | collective-permute-done | bytes 221216 | tf_op jit(solution)/shard_map/ppermute | solution.py:61
  92.8 3.8 %collective-permute-done.12 = bf16[96,1152]{1,0:T(8,128)(2,1)} collective-permute-done((bf16[96,1152]{1,0:T(8,128)(2,1)}, bf16[96,1152]{1,0:T(8,128)(2,1)}, u32[]{:S(2)}, u32[]{:S(2)}) %collective-permute-start.12) | collective-permute-done | bytes 221216 | tf_op jit(solution)/shard_map/ppermute | solution.py:61
  96.5 2.7 %collective-permute-done.13 = bf16[96,1152]{1,0:T(8,128)(2,1)} collective-permute-done((bf16[96,1152]{1,0:T(8,128)(2,1)S(1)}, bf16[96,1152]{1,0:T(8,128)(2,1)}, u32[]{:S(2)}, u32[]{:S(2)}) %collective-permute-start.13) | collective-permute-done | bytes 221216 | tf_op jit(solution)/shard_map/ppermute | solution.py:61
  104.9 9.1 %all_gather.3 = bf16[192,2304]{1,0:T(8,128)(2,1)S(1)} all-gather(bf16[48,2304]{1,0:T(8,128)(2,1)S(1)} %pad_maximum_fusion.6), channel_id=1, replica_groups=mesh['yhi'=2,'z'=8,'x'=4,'ylo'=2,'core'=2] {'ylo','core'}, dimensions={0}, use_global_device_ids=true | all-gather | bytes 1105920 | tf_op jit(solution)/shard_map/all_gather | solution.py:204
  118.6 4.0 %collective-permute-done.18 = bf16[2,32,1152]{2,1,0:T(8,128)(2,1)S(1)} collective-permute-done((bf16[2,32,1152]{2,1,0:T(8,128)(2,1)S(1)}, bf16[2,32,1152]{2,1,0:T(8,128)(2,1)S(1)}, u32[]{:S(2)}, u32[]{:S(2)}) %collective-permute-start.18) | collective-permute-done | bytes 147488 | tf_op jit(solution)/shard_map/ppermute | solution.py:20
  122.6 3.1 %collective-permute-start.19 = (bf16[2,72,1152]{2,1,0:T(8,128)(2,1)S(1)}, bf16[2,72,1152]{2,1,0:T(8,128)(2,1)S(1)}, u32[]{:S(2)}, u32[]{:S(2)}) collective-permute-start(bf16[2,72,1152]{2,1,0:T(8,128)(2,1)S(1)} %pad_maximum_fusion.2), channel_id=1, source_target_pairs={{0,12},{4,0},{8,4},{12,8},{1,13},{5,1},{9,5},{13,9},{2,14},{6,2},{... | collective-permute-start | bytes 995336 | tf_op jit(solution)/shard_map/ppermute | solution.py:20
  126.0 6.2 %collective-permute-done.19 = bf16[2,72,1152]{2,1,0:T(8,128)(2,1)S(1)} collective-permute-done((bf16[2,72,1152]{2,1,0:T(8,128)(2,1)S(1)}, bf16[2,72,1152]{2,1,0:T(8,128)(2,1)S(1)}, u32[]{:S(2)}, u32[]{:S(2)}) %collective-permute-start.19) | collective-permute-done | bytes 331808 | tf_op jit(solution)/shard_map/ppermute | solution.py:20
  132.2 3.6 %collective-permute-done.17 = bf16[2,72,1152]{2,1,0:T(8,128)(2,1)S(1)} collective-permute-done((bf16[2,72,1152]{2,1,0:T(8,128)(2,1)S(1)}, bf16[2,72,1152]{2,1,0:T(8,128)(2,1)S(1)}, u32[]{:S(2)}, u32[]{:S(2)}) %collective-permute-start.17) | collective-permute-done | bytes 331808 | tf_op jit(solution)/shard_map/ppermute | solution.py:20
  139.1 4.8 %collective-permute-start.23 = (bf16[2,168,128]{2,1,0:T(8,128)(2,1)S(1)}, bf16[2,168,128]{2,1,0:T(8,128)(2,1)S(1)}, u32[]{:S(2)}, u32[]{:S(2)}) collective-permute-start(bf16[2,168,128]{2,1,0:T(8,128)(2,1)S(1)} %pad_maximum_fusion.11), channel_id=1, source_target_pairs={{0,32},{16,48},{32,64},{48,80},{64,96},{80,112},{96,0},{112,16},{1... | collective-permute-start | bytes 258056 | tf_op jit(solution)/shard_map/ppermute | solution.py:61
  144.2 5.3 %collective-permute-start.20 = (bf16[168,128]{1,0:T(8,128)(2,1)S(1)}, bf16[168,128]{1,0:T(8,128)(2,1)S(1)}, u32[]{:S(2)}, u32[]{:S(2)}) collective-permute-start(bf16[168,128]{1,0:T(8,128)(2,1)S(1)} %get-tuple-element.37), channel_id=1, source_target_pairs={{0,64},{16,80},{32,96},{48,112},{64,0},{80,16},{96,32},{112,48},{1... | collective-permute-start | bytes 129032 | tf_op jit(solution)/shard_map/ppermute | solution.py:61
  149.5 3.5 %collective-permute-done.24 = bf16[2,168,128]{2,1,0:T(8,128)(2,1)S(1)} collective-permute-done((bf16[2,168,128]{2,1,0:T(8,128)(2,1)S(1)}, bf16[2,168,128]{2,1,0:T(8,128)(2,1)S(1)}, u32[]{:S(2)}, u32[]{:S(2)}) %collective-permute-start.24) | collective-permute-done | bytes 86048 | tf_op jit(solution)/shard_map/ppermute | solution.py:61
  156.3 3.7 %collective-permute-done.26 = bf16[168,128]{1,0:T(8,128)(2,1)S(1)} collective-permute-done((bf16[168,128]{1,0:T(8,128)(2,1)S(1)}, bf16[168,128]{1,0:T(8,128)(2,1)S(1)}, u32[]{:S(2)}, u32[]{:S(2)}) %collective-permute-start.26) | collective-permute-done | bytes 43040 | tf_op jit(solution)/shard_map/ppermute | solution.py:25
  160.1 3.4 %collective-permute-start.27 = (bf16[168,128]{1,0:T(8,128)(2,1)S(1)}, bf16[168,128]{1,0:T(8,128)(2,1)S(1)}, u32[]{:S(2)}, u32[]{:S(2)}) collective-permute-start(bf16[168,128]{1,0:T(8,128)(2,1)S(1)} %get-tuple-element.21), channel_id=1, source_target_pairs={{0,64},{16,80},{32,96},{48,112},{64,0},{80,16},{96,32},{112,48},{1... | collective-permute-start | bytes 129032 | tf_op jit(solution)/shard_map/ppermute | solution.py:61
  165.9 1.9 collective-permute-start.31
  169.0 3.4 %collective-permute-done.30 = bf16[2,168,128]{2,1,0:T(8,128)(2,1)S(1)} collective-permute-done((bf16[2,168,128]{2,1,0:T(8,128)(2,1)S(1)}, bf16[2,168,128]{2,1,0:T(8,128)(2,1)S(1)}, u32[]{:S(2)}, u32[]{:S(2)}) %collective-permute-start.30) | collective-permute-done | bytes 86048 | tf_op jit(solution)/shard_map/ppermute | solution.py:61
  172.4 3.3 %collective-permute-done.31 = bf16[2,168,128]{2,1,0:T(8,128)(2,1)S(1)} collective-permute-done((bf16[2,168,128]{2,1,0:T(8,128)(2,1)S(1)}, bf16[2,168,128]{2,1,0:T(8,128)(2,1)S(1)}, u32[]{:S(2)}, u32[]{:S(2)}) %collective-permute-start.31) | collective-permute-done | bytes 86048 | tf_op jit(solution)/shard_map/ppermute | solution.py:61
  180.3 9.0 %collective-permute-done.34 = bf16[2,72,1152]{2,1,0:T(8,128)(2,1)S(1)} collective-permute-done((bf16[2,72,1152]{2,1,0:T(8,128)(2,1)S(1)}, bf16[2,72,1152]{2,1,0:T(8,128)(2,1)S(1)}, u32[]{:S(2)}, u32[]{:S(2)}) %collective-permute-start.34) | collective-permute-done | bytes 331808 | tf_op jit(solution)/shard_map/ppermute | solution.py:20
  189.9 2.9 %collective-permute-start.36 = (bf16[2,32,1152]{2,1,0:T(8,128)(2,1)S(1)}, bf16[2,32,1152]{2,1,0:T(8,128)(2,1)S(1)}, u32[]{:S(2)}, u32[]{:S(2)}) collective-permute-start(bf16[2,32,1152]{2,1,0:T(8,128)(2,1)S(1)} %slice.238), channel_id=1, source_target_pairs={{0,12},{4,0},{8,4},{12,8},{1,13},{5,1},{9,5},{13,9},{2,14},{6,2},{... | collective-permute-start | bytes 442376 | tf_op jit(solution)/shard_map/ppermute | solution.py:20
  192.8 2.6 %collective-permute-done.36 = bf16[2,32,1152]{2,1,0:T(8,128)(2,1)S(1)} collective-permute-done((bf16[2,32,1152]{2,1,0:T(8,128)(2,1)S(1)}, bf16[2,32,1152]{2,1,0:T(8,128)(2,1)S(1)}, u32[]{:S(2)}, u32[]{:S(2)}) %collective-permute-start.36) | collective-permute-done | bytes 147488 | tf_op jit(solution)/shard_map/ppermute | solution.py:20
  (176 shorter events, 53.9 us)
Async XLA Ops:
  4.0 5.2 %collective-permute-start.2 = (bf16[48,1152]{1,0:T(8,128)(2,1)S(1)}, bf16[48,1152]{1,0:T(8,128)(2,1)S(1)}, u32[]{:S(2)}, u32[]{:S(2)}) collective-permute-start(bf16[48,1152]{1,0:T(8,128)(2,1)S(1)} %fusion.23), channel_id=1, source_target_pairs={{0,2},{2,0},{1,3},{3,1},{4,6},{6,4},{5,7},{7,5},{8,10},{10,8},{9,1... | collective-permute-start | bytes 331784 | tf_op jit(solution)/shard_map/ppermute | solution.py:25
  9.5 4.8 %collective-permute-start.3 = (bf16[48,1152]{1,0:T(8,128)(2,1)S(1)}, bf16[48,1152]{1,0:T(8,128)(2,1)S(1)}, u32[]{:S(2)}, u32[]{:S(2)}) collective-permute-start(bf16[48,1152]{1,0:T(8,128)(2,1)S(1)} %fusion.24), channel_id=1, source_target_pairs={{0,2},{2,0},{1,3},{3,1},{4,6},{6,4},{5,7},{7,5},{8,10},{10,8},{9,1... | collective-permute-start | bytes 331784 | tf_op jit(solution)/shard_map/ppermute | solution.py:25
  15.0 8.5 %collective-permute-start.4 = (bf16[48,1152]{1,0:T(8,128)(2,1)S(1)}, bf16[48,1152]{1,0:T(8,128)(2,1)S(1)}, u32[]{:S(2)}, u32[]{:S(2)}) collective-permute-start(bf16[48,1152]{1,0:T(8,128)(2,1)S(1)} %fusion.32), channel_id=1, source_target_pairs={{0,1},{1,0},{2,3},{3,2},{4,5},{5,4},{6,7},{7,6},{8,9},{9,8},{10,11... | collective-permute-start | bytes 331784 | tf_op jit(solution)/shard_map/ppermute | solution.py:25
  16.5 39.5 %all-to-all-start = ((bf16[16,48,1152]{2,1,0:T(8,128)(2,1)}), bf16[16,48,1152]{2,1,0:T(8,128)(2,1)S(1)}, u32[]{:S(2)}, u32[]{:S(2)}) async-start(bf16[16,48,1152]{2,1,0:T(8,128)(2,1)} %broadcast_in_dim.2), calls=%async_computation | async-start | bytes 3538944 | tf_op jit(solution)/shard_map/all_to_all | solution.py:29
  24.9 21.8 %collective-permute-start.5 = (bf16[96,1152]{1,0:T(8,128)(2,1)S(1)}, bf16[96,1152]{1,0:T(8,128)(2,1)S(1)}, u32[]{:S(2)}, u32[]{:S(2)}) collective-permute-start(bf16[96,1152]{1,0:T(8,128)(2,1)S(1)} %pad_maximum_fusion.5), channel_id=1, source_target_pairs={{0,16},{16,32},{32,48},{48,64},{64,80},{80,96},{96,112},{112,0},{1... | collective-permute-start | bytes 663560 | tf_op jit(solution)/shard_map/ppermute | solution.py:61
  26.9 19.8 %collective-permute-start.6 = (bf16[96,1152]{1,0:T(8,128)(2,1)S(1)}, bf16[96,1152]{1,0:T(8,128)(2,1)S(1)}, u32[]{:S(2)}, u32[]{:S(2)}) collective-permute-start(bf16[96,1152]{1,0:T(8,128)(2,1)S(1)} %pad_maximum_fusion.5), channel_id=1, source_target_pairs={{0,32},{16,48},{32,64},{48,80},{64,96},{80,112},{96,0},{112,16},{1... | collective-permute-start | bytes 663560 | tf_op jit(solution)/shard_map/ppermute | solution.py:61
  31.4 15.6 %collective-permute-start.7 = (bf16[96,1152]{1,0:T(8,128)(2,1)S(1)}, bf16[96,1152]{1,0:T(8,128)(2,1)S(1)}, u32[]{:S(2)}, u32[]{:S(2)}) collective-permute-start(bf16[96,1152]{1,0:T(8,128)(2,1)S(1)} %pad_maximum_fusion.5), channel_id=1, source_target_pairs={{0,48},{16,64},{32,80},{48,96},{64,112},{80,0},{96,16},{112,32},{1... | collective-permute-start | bytes 663560 | tf_op jit(solution)/shard_map/ppermute | solution.py:61
  33.3 13.3 %collective-permute-start.8 = (bf16[48,1152]{1,0:T(8,128)(2,1)S(1)}, bf16[48,1152]{1,0:T(8,128)(2,1)S(1)}, u32[]{:S(2)}, u32[]{:S(2)}) collective-permute-start(bf16[48,1152]{1,0:T(8,128)(2,1)S(1)} %fusion.32), channel_id=1, source_target_pairs={{0,64},{16,80},{32,96},{48,112},{64,0},{80,16},{96,32},{112,48},{1... | collective-permute-start | bytes 331784 | tf_op jit(solution)/shard_map/ppermute | solution.py:61
  47.1 8.0 %collective-permute-start.9 = (bf16[336,1152]{1,0:T(8,128)(2,1)S(1)}, bf16[336,1152]{1,0:T(8,128)(2,1)S(1)}, u32[]{:S(2)}, u32[]{:S(2)}) collective-permute-start(bf16[336,1152]{1,0:T(8,128)(2,1)S(1)} %pad_maximum_fusion), channel_id=1, source_target_pairs={{0,1},{1,0},{2,3},{3,2},{4,5},{5,4},{6,7},{7,6},{8,9},{9,8},{10,11... | collective-permute-start | bytes 2322440 | tf_op jit(solution)/shard_map/ppermute | solution.py:25
  67.8 7.0 %collective-permute-start.10 = (bf16[336,1152]{1,0:T(8,128)(2,1)}, bf16[336,1152]{1,0:T(8,128)(2,1)}, u32[]{:S(2)}, u32[]{:S(2)}) collective-permute-start(bf16[336,1152]{1,0:T(8,128)(2,1)} %slice.206), channel_id=1, source_target_pairs={{0,1},{1,0},{2,3},{3,2},{4,5},{5,4},{6,7},{7,6},{8,9},{9,8},{10,11... | collective-permute-start | bytes 2322440 | tf_op jit(solution)/shard_map/ppermute | solution.py:25
  67.8 34.8 %all-to-all-start.1 = ((bf16[16,48,1152]{2,1,0:T(8,128)(2,1)}), bf16[16,48,1152]{2,1,0:T(8,128)(2,1)S(1)}, u32[]{:S(2)}, u32[]{:S(2)}) async-start(bf16[16,48,1152]{2,1,0:T(8,128)(2,1)} %bitcast.164), calls=%async_computation.1 | async-start | bytes 3538944 | tf_op jit(solution)/shard_map/all_to_all | solution.py:198
  78.1 14.7 %collective-permute-start.11 = (bf16[96,1152]{1,0:T(8,128)(2,1)}, bf16[96,1152]{1,0:T(8,128)(2,1)S(1)}, u32[]{:S(2)}, u32[]{:S(2)}) collective-permute-start(bf16[96,1152]{1,0:T(8,128)(2,1)} %get-tuple-element.34), channel_id=1, source_target_pairs={{0,80},{16,96},{32,112},{48,0},{64,16},{80,32},{96,48},{112,64},{1... | collective-permute-start | bytes 663560 | tf_op jit(solution)/shard_map/ppermute | solution.py:61
  82.4 14.2 %collective-permute-start.12 = (bf16[96,1152]{1,0:T(8,128)(2,1)}, bf16[96,1152]{1,0:T(8,128)(2,1)}, u32[]{:S(2)}, u32[]{:S(2)}) collective-permute-start(bf16[96,1152]{1,0:T(8,128)(2,1)} %get-tuple-element.36), channel_id=1, source_target_pairs={{0,96},{16,112},{32,0},{48,16},{64,32},{80,48},{96,64},{112,80},{1... | collective-permute-start | bytes 663560 | tf_op jit(solution)/shard_map/ppermute | solution.py:61
  82.4 16.9 %collective-permute-start.13 = (bf16[96,1152]{1,0:T(8,128)(2,1)S(1)}, bf16[96,1152]{1,0:T(8,128)(2,1)}, u32[]{:S(2)}, u32[]{:S(2)}) collective-permute-start(bf16[96,1152]{1,0:T(8,128)(2,1)S(1)} %get-tuple-element.35), channel_id=1, source_target_pairs={{0,112},{16,0},{32,16},{48,32},{64,48},{80,64},{96,80},{112,96},{1... | collective-permute-start | bytes 663560 | tf_op jit(solution)/shard_map/ppermute | solution.py:61
  84.5 18.5 %collective-permute-start.14 = (bf16[48,1152]{1,0:T(8,128)(2,1)}, bf16[48,1152]{1,0:T(8,128)(2,1)}, u32[]{:S(2)}, u32[]{:S(2)}) collective-permute-start(bf16[48,1152]{1,0:T(8,128)(2,1)} %slice.212), channel_id=1, source_target_pairs={{0,64},{16,80},{32,96},{48,112},{64,0},{80,16},{96,32},{112,48},{1... | collective-permute-start | bytes 331784 | tf_op jit(solution)/shard_map/ppermute | solution.py:61
  115.2 10.5 %collective-permute-start.16 = (bf16[2,40,1152]{2,1,0:T(8,128)(2,1)S(1)}, bf16[2,40,1152]{2,1,0:T(8,128)(2,1)S(1)}, u32[]{:S(2)}, u32[]{:S(2)}) collective-permute-start(bf16[2,40,1152]{2,1,0:T(8,128)(2,1)S(1)} %fusion.18), channel_id=1, source_target_pairs={{0,4},{4,8},{8,12},{12,0},{1,5},{5,9},{9,13},{13,1},{2,6},{6,10},{... | collective-permute-start | bytes 552968 | tf_op jit(solution)/shard_map/ppermute | solution.py:20
  116.7 5.8 %collective-permute-start.18 = (bf16[2,32,1152]{2,1,0:T(8,128)(2,1)S(1)}, bf16[2,32,1152]{2,1,0:T(8,128)(2,1)S(1)}, u32[]{:S(2)}, u32[]{:S(2)}) collective-permute-start(bf16[2,32,1152]{2,1,0:T(8,128)(2,1)S(1)} %pad_maximum_fusion.7), channel_id=1, source_target_pairs={{0,12},{4,0},{8,4},{12,8},{1,13},{5,1},{9,5},{13,9},{2,14},{6,2},{... | collective-permute-start | bytes 442376 | tf_op jit(solution)/shard_map/ppermute | solution.py:20
  122.6 9.6 %collective-permute-start.19 = (bf16[2,72,1152]{2,1,0:T(8,128)(2,1)S(1)}, bf16[2,72,1152]{2,1,0:T(8,128)(2,1)S(1)}, u32[]{:S(2)}, u32[]{:S(2)}) collective-permute-start(bf16[2,72,1152]{2,1,0:T(8,128)(2,1)S(1)} %pad_maximum_fusion.2), channel_id=1, source_target_pairs={{0,12},{4,0},{8,4},{12,8},{1,13},{5,1},{9,5},{13,9},{2,14},{6,2},{... | collective-permute-start | bytes 995336 | tf_op jit(solution)/shard_map/ppermute | solution.py:20
  125.8 10.0 %collective-permute-start.17 = (bf16[2,72,1152]{2,1,0:T(8,128)(2,1)S(1)}, bf16[2,72,1152]{2,1,0:T(8,128)(2,1)S(1)}, u32[]{:S(2)}, u32[]{:S(2)}) collective-permute-start(bf16[2,72,1152]{2,1,0:T(8,128)(2,1)S(1)} %pad_maximum_fusion.1), channel_id=1, source_target_pairs={{0,4},{4,8},{8,12},{12,0},{1,5},{5,9},{9,13},{13,1},{2,6},{6,10},{... | collective-permute-start | bytes 995336 | tf_op jit(solution)/shard_map/ppermute | solution.py:20
  137.5 12.0 %collective-permute-start.22 = (bf16[2,168,128]{2,1,0:T(8,128)(2,1)S(1)}, bf16[2,168,128]{2,1,0:T(8,128)(2,1)S(1)}, u32[]{:S(2)}, u32[]{:S(2)}) collective-permute-start(bf16[2,168,128]{2,1,0:T(8,128)(2,1)S(1)} %pad_maximum_fusion.10), channel_id=1, source_target_pairs={{0,16},{16,32},{32,48},{48,64},{64,80},{80,96},{96,112},{112,0},{1... | collective-permute-start | bytes 258056 | tf_op jit(solution)/shard_map/ppermute | solution.py:61
  139.1 10.4 %collective-permute-start.23 = (bf16[2,168,128]{2,1,0:T(8,128)(2,1)S(1)}, bf16[2,168,128]{2,1,0:T(8,128)(2,1)S(1)}, u32[]{:S(2)}, u32[]{:S(2)}) collective-permute-start(bf16[2,168,128]{2,1,0:T(8,128)(2,1)S(1)} %pad_maximum_fusion.11), channel_id=1, source_target_pairs={{0,32},{16,48},{32,64},{48,80},{64,96},{80,112},{96,0},{112,16},{1... | collective-permute-start | bytes 258056 | tf_op jit(solution)/shard_map/ppermute | solution.py:61
  144.0 9.0 %collective-permute-start.24 = (bf16[2,168,128]{2,1,0:T(8,128)(2,1)S(1)}, bf16[2,168,128]{2,1,0:T(8,128)(2,1)S(1)}, u32[]{:S(2)}, u32[]{:S(2)}) collective-permute-start(bf16[2,168,128]{2,1,0:T(8,128)(2,1)S(1)} %pad_maximum_fusion.12), channel_id=1, source_target_pairs={{0,48},{16,64},{32,80},{48,96},{64,112},{80,0},{96,16},{112,32},{1... | collective-permute-start | bytes 258056 | tf_op jit(solution)/shard_map/ppermute | solution.py:61
  144.2 9.1 %collective-permute-start.20 = (bf16[168,128]{1,0:T(8,128)(2,1)S(1)}, bf16[168,128]{1,0:T(8,128)(2,1)S(1)}, u32[]{:S(2)}, u32[]{:S(2)}) collective-permute-start(bf16[168,128]{1,0:T(8,128)(2,1)S(1)} %get-tuple-element.37), channel_id=1, source_target_pairs={{0,64},{16,80},{32,96},{48,112},{64,0},{80,16},{96,32},{112,48},{1... | collective-permute-start | bytes 129032 | tf_op jit(solution)/shard_map/ppermute | solution.py:61
  154.4 5.6 %collective-permute-start.26 = (bf16[168,128]{1,0:T(8,128)(2,1)S(1)}, bf16[168,128]{1,0:T(8,128)(2,1)S(1)}, u32[]{:S(2)}, u32[]{:S(2)}) collective-permute-start(bf16[168,128]{1,0:T(8,128)(2,1)S(1)} %fusion.26), channel_id=1, source_target_pairs={{0,128},{128,0},{1,129},{129,1},{2,130},{130,2},{3,131},{131,3},{4... | collective-permute-start | bytes 129032 | tf_op jit(solution)/shard_map/ppermute | solution.py:25
  160.1 8.8 %collective-permute-start.27 = (bf16[168,128]{1,0:T(8,128)(2,1)S(1)}, bf16[168,128]{1,0:T(8,128)(2,1)S(1)}, u32[]{:S(2)}, u32[]{:S(2)}) collective-permute-start(bf16[168,128]{1,0:T(8,128)(2,1)S(1)} %get-tuple-element.21), channel_id=1, source_target_pairs={{0,64},{16,80},{32,96},{48,112},{64,0},{80,16},{96,32},{112,48},{1... | collective-permute-start | bytes 129032 | tf_op jit(solution)/shard_map/ppermute | solution.py:61
  163.5 5.5 %collective-permute-start.29 = (bf16[2,168,128]{2,1,0:T(8,128)(2,1)S(1)}, bf16[2,168,128]{2,1,0:T(8,128)(2,1)S(1)}, u32[]{:S(2)}, u32[]{:S(2)}) collective-permute-start(bf16[2,168,128]{2,1,0:T(8,128)(2,1)S(1)} %pad_maximum_fusion.13), channel_id=1, source_target_pairs={{0,16},{16,32},{32,48},{48,64},{64,80},{80,96},{96,112},{112,0},{1... | collective-permute-start | bytes 258056 | tf_op jit(solution)/shard_map/ppermute | solution.py:61
  164.8 7.6 %collective-permute-start.30 = (bf16[2,168,128]{2,1,0:T(8,128)(2,1)S(1)}, bf16[2,168,128]{2,1,0:T(8,128)(2,1)S(1)}, u32[]{:S(2)}, u32[]{:S(2)}) collective-permute-start(bf16[2,168,128]{2,1,0:T(8,128)(2,1)S(1)} %pad_maximum_fusion.13), channel_id=1, source_target_pairs={{0,32},{16,48},{32,64},{48,80},{64,96},{80,112},{96,0},{112,16},{1... | collective-permute-start | bytes 258056 | tf_op jit(solution)/shard_map/ppermute | solution.py:61
  165.9 9.9 %collective-permute-start.31 = (bf16[2,168,128]{2,1,0:T(8,128)(2,1)S(1)}, bf16[2,168,128]{2,1,0:T(8,128)(2,1)S(1)}, u32[]{:S(2)}, u32[]{:S(2)}) collective-permute-start(bf16[2,168,128]{2,1,0:T(8,128)(2,1)S(1)} %pad_maximum_fusion.13), channel_id=1, source_target_pairs={{0,48},{16,64},{32,80},{48,96},{64,112},{80,0},{96,16},{112,32},{1... | collective-permute-start | bytes 258056 | tf_op jit(solution)/shard_map/ppermute | solution.py:61
  177.7 12.2 %collective-permute-start.33 = (bf16[2,72,1152]{2,1,0:T(8,128)(2,1)S(1)}, bf16[2,72,1152]{2,1,0:T(8,128)(2,1)S(1)}, u32[]{:S(2)}, u32[]{:S(2)}) collective-permute-start(bf16[2,72,1152]{2,1,0:T(8,128)(2,1)S(1)} %bitcast.170), channel_id=1, source_target_pairs={{0,12},{4,0},{8,4},{12,8},{1,13},{5,1},{9,5},{13,9},{2,14},{6,2},{... | collective-permute-start | bytes 995336 | tf_op jit(solution)/shard_map/ppermute | solution.py:20
  178.1 11.2 %collective-permute-start.34 = (bf16[2,72,1152]{2,1,0:T(8,128)(2,1)S(1)}, bf16[2,72,1152]{2,1,0:T(8,128)(2,1)S(1)}, u32[]{:S(2)}, u32[]{:S(2)}) collective-permute-start(bf16[2,72,1152]{2,1,0:T(8,128)(2,1)S(1)} %bitcast.171), channel_id=1, source_target_pairs={{0,4},{4,8},{8,12},{12,0},{1,5},{5,9},{9,13},{13,1},{2,6},{6,10},{... | collective-permute-start | bytes 995336 | tf_op jit(solution)/shard_map/ppermute | solution.py:20
  189.3 7.3 %collective-permute-start.35 = (bf16[2,40,1152]{2,1,0:T(8,128)(2,1)S(1)}, bf16[2,40,1152]{2,1,0:T(8,128)(2,1)S(1)}, u32[]{:S(2)}, u32[]{:S(2)}) collective-permute-start(bf16[2,40,1152]{2,1,0:T(8,128)(2,1)S(1)} %slice.236), channel_id=1, source_target_pairs={{0,4},{4,8},{8,12},{12,0},{1,5},{5,9},{9,13},{13,1},{2,6},{6,10},{... | collective-permute-start | bytes 552968 | tf_op jit(solution)/shard_map/ppermute | solution.py:20
  189.9 5.5 %collective-permute-start.36 = (bf16[2,32,1152]{2,1,0:T(8,128)(2,1)S(1)}, bf16[2,32,1152]{2,1,0:T(8,128)(2,1)S(1)}, u32[]{:S(2)}, u32[]{:S(2)}) collective-permute-start(bf16[2,32,1152]{2,1,0:T(8,128)(2,1)S(1)} %slice.238), channel_id=1, source_target_pairs={{0,12},{4,0},{8,4},{12,8},{1,13},{5,1},{9,5},{13,9},{2,14},{6,2},{... | collective-permute-start | bytes 442376 | tf_op jit(solution)/shard_map/ppermute | solution.py:20
  (19 other events, 87.8 us)
where the time goes:
time: 199 us; the launch traced here: 198 us
  waiting for transfers between devices  75.8 us (38%)
  starting transfers between devices  75 us (38%)
  matrix products  14.7 us (7%)
  local copies, waits for them, and re-layouts  13.8 us (7%)
  blocking collectives  9.13 us (5%)
  other arithmetic  8.4 us (4%)
    ppermute x16, starting transfers between devices, column_shift(): return lax.ppermute(value, ('z', 'core'), pairs)  37.2 us
    ppermute x16, waiting for transfers between devices, column_shift(): return lax.ppermute(value, ('z', 'core'), pairs)  34.6 us
    ppermute x8, waiting for transfers between devices, shift(): return lax.ppermute(value, axis, [(i, (i + by) % n) for i in range(n)])  26.6 us
    ppermute x13, waiting for transfers between devices, flip(): return lax.ppermute(value, axis, [(i, i ^ bit) for i in range(n)])  13.4 us
    ppermute x8, starting transfers between devices, shift(): return lax.ppermute(value, axis, [(i, (i + by) % n) for i in range(n)])  12.2 us
    ppermute x13, starting transfers between devices, flip(): return lax.ppermute(value, axis, [(i, i ^ bit) for i in range(n)])  11.5 us
    all_gather x1, blocking collectives, per_device(): lax.all_gather(jnp.concatenate([image_grad_raw, text_grad_raw], axis=1),...  9.13 us
    unnamed x31, local copies, waits for them, and re-layouts  7.46 us
  transfers between devices with their start and end apart: 39, of which 24 were waited for; matrix products, arithmetic and copies ran while one was open for 8% of the time, Pallas kernels for 0%

commit v1 on v0

--- a/solution.py
+++ b/solution.py
@@ -23,10 +23,6 @@
 def flip(value, axis, bit):
     n = lax.axis_size(axis)
     return lax.ppermute(value, axis, [(i, i ^ bit) for i in range(n)])
-
-
-def broadcast_gather(value, axes, members):
-    return lax.all_to_all(jnp.broadcast_to(value[None], (members,) + value.shape), axes, 0, 0)
 
 
 def normalize(raw):
@@ -71,15 +67,17 @@
     return jnp.concatenate([pair, mine, flip(mine, "core", 1)], axis=0)
 
 
-def column_sum(parts, rows):
+def column_sum(parts, swapped, rows):
     first = lax.axis_index("core") == 0
     own = parts[: 2 * rows].astype(F32)
-    far = 9 * rows
-    mine = parts[2 * rows : far].astype(F32) + flip(parts[far:], "core", 1).astype(F32)
-    mine = mine.astype(BF16)
-    half = column_shift(mine[6 * rows :], -4).astype(F32)
+
+    def sent(start, stop):
+        mine = parts[2 * rows + start : 2 * rows + stop].astype(F32)
+        return (mine + swapped[start:stop].astype(F32)).astype(BF16)
+
+    half = column_shift(sent(6 * rows, 7 * rows), -4).astype(F32)
     for k in (3, 2, 1):
-        own = own + column_shift(mine[2 * rows * (k - 1) : 2 * rows * k], -k).astype(F32)
+        own = own + column_shift(sent(2 * rows * (k - 1), 2 * rows * k), -k).astype(F32)
     send = jnp.where(first, own[rows:], own[:rows]).astype(BF16)
     return jnp.where(first, own[:rows], own[rows:]) + half + flip(send, "core", 1).astype(F32)
 
@@ -178,10 +176,11 @@
     image_half = core_half(jnp.dot(image_feats, image_proj, preferred_element_type=F32))
     text_half = core_half(jnp.dot(text_feats, text_proj, preferred_element_type=F32))
     image_unit, image_radius = normalize(quarter_rows(image_half))
-    text_half, image_unit = lax.optimization_barrier((text_half, image_unit))
     text_unit, text_radius = normalize(quarter_rows(text_half))
-    images = broadcast_gather(image_unit.astype(BF16), PLANE, plane).reshape(-1, width)
-    texts = column_gather(text_unit.astype(BF16))
+    spread = jnp.broadcast_to(image_unit.astype(BF16)[None], (plane, quarter, width))
+    spread, text_emb = lax.optimization_barrier((spread, text_unit.astype(BF16)))
+    images = lax.all_to_all(spread, PLANE, 0, 0).reshape(-1, width)
+    texts = column_gather(text_emb)
     own_image = lax.axis_index(PLANE) * quarter
     own_text = lax.axis_index("core") * quarter
     scores = lax.dot_general(images, texts, (((1,), (1,)), ((), ())), preferred_element_type=F32)
@@ -190,13 +189,15 @@
     label = (row_id - own_image == col_id - own_text) & (col_id // quarter == own_text // quarter)
     weights = (SCALE * (jax.nn.sigmoid(SCALE * scores + OFFSET) - label.astype(F32))).astype(BF16)
 
-    image_part = jnp.dot(weights, texts, preferred_element_type=F32).astype(BF16)
-    weights, image_part = lax.optimization_barrier((weights, image_part))
     text_part = lax.dot_general(
         weights, images, (((0,), (0,)), ((), ())), preferred_element_type=F32
-    )
+    ).astype(BF16)
+    swapped = flip(text_part[9 * quarter :], "core", 1)
+    weights, text_part = lax.optimization_barrier((weights, text_part))
+    image_part = jnp.dot(weights, texts, preferred_element_type=F32).astype(BF16)
+    image_part, swapped = lax.optimization_barrier((image_part, swapped))
     image_sent = lax.all_to_all(image_part.reshape(plane, quarter, width), PLANE, 0, 0)
-    grad_text_emb = column_sum(text_part.astype(BF16), quarter)
+    grad_text_emb = column_sum(text_part, swapped, quarter)
     text_grad_raw = backnorm(text_unit, text_radius, grad_text_emb)
     grad_image_emb = jnp.sum(image_sent.astype(F32), axis=0)
     image_grad_raw = backnorm(image_unit, image_radius, grad_image_emb)

time: 199 us -> 197 us (0.990)
  other arithmetic: 8.4 us -> 14.7 us
  starting transfers between devices: 75 us -> 71.1 us
  local copies, waits for them, and re-layouts: 13.8 us -> 10.2 us
    ppermute x13, waiting for transfers between devices: 13.4 us -> 9.26 us  [flip(): return lax.ppermute(value, axis, [(i, i ^ bit) for i in range(n)])]
    slice x3 -> x1, local copies, waits for them, and re-layouts: 3.27 us -> 0.06 us  [per_device(): swapped = flip(text_part[9 * quarter:], 'core', 1)]
    ppermute x8, starting transfers between devices: 12.2 us -> 9.57 us  [shift(): return lax.ppermute(value, axis, [(i, (i + by) % n) for i in range(n)])]
    unnamed x14, other arithmetic: 1.67 us -> 4.11 us
    convert_element_type x3 -> x4, other arithmetic: 1.65 us -> 4.02 us  [the longest x2 3.18 us: sent(): return (mine + swapped[start:stop].astype(F32)).astype(BF16)]
    ppermute x8, waiting for transfers between devices: 26.6 us -> 28.8 us  [shift(): return lax.ppermute(value, axis, [(i, (i + by) % n) for i in range(n)])]
    unnamed x31 -> x33, local copies, waits for them, and re-layouts: 7.46 us -> 7 us
  transfers between devices with their start and end apart: 39 -> 39, of which waited for: 24 -> 21; matrix products, arithmetic and copies ran while one was open for 8% -> 11% of each run, Pallas kernels for 0% -> 0%
where the time goes in v1:
time: 197 us; the launch traced here: 196 us
  waiting for transfers between devices  75.3 us (38%)
  starting transfers between devices  71.1 us (36%)
  matrix products  15.1 us (8%)
  other arithmetic  14.7 us (7%)
  local copies, waits for them, and re-layouts  10.2 us (5%)
  blocking collectives  8.34 us (4%)
    ppermute x16, starting transfers between devices, column_shift(): return lax.ppermute(value, ('z', 'core'), pairs)  36.1 us
    ppermute x16, waiting for transfers between devices, column_shift(): return lax.ppermute(value, ('z', 'core'), pairs)  34.6 us
    ppermute x8, waiting for transfers between devices, shift(): return lax.ppermute(value, axis, [(i, (i + by) % n) for i in range(n)])  28.8 us
    ppermute x13, starting transfers between devices, flip(): return lax.ppermute(value, axis, [(i, i ^ bit) for i in range(n)])  11.4 us
    ppermute x8, starting transfers between devices, shift(): return lax.ppermute(value, axis, [(i, (i + by) % n) for i in range(n)])  9.57 us
    ppermute x13, waiting for transfers between devices, flip(): return lax.ppermute(value, axis, [(i, i ^ bit) for i in range(n)])  9.26 us
    all_gather x1, blocking collectives, per_device(): lax.all_gather(jnp.concatenate([image_grad_raw, text_grad_raw], axis=1),...  8.34 us
    all_to_all x1, starting transfers between devices, per_device(): images = lax.all_to_all(spread, PLANE, 0, 0).reshape(-1, width)  7.03 us
  transfers between devices with their start and end apart: 39, of which 21 were waited for; matrix products, arithmetic and copies ran while one was open for 11% of the time, Pallas kernels for 0%

profile of v1, /device:TPU:32, one launch (start us, length us, event | category | flops | bytes accessed | tf_op | source)
XLA Modules:
  0.0 196.2 jit_solution(17442636560174418582)
XLA Ops:
  7.0 3.7 %collective-permute-done.3 = bf16[48,1152]{1,0:T(8,128)(2,1)S(1)} collective-permute-done((bf16[48,1152]{1,0:T(8,128)(2,1)S(1)}, bf16[48,1152]{1,0:T(8,128)(2,1)S(1)}, u32[]{:S(2)}, u32[]{:S(2)}) %collective-permute-start.3) | collective-permute-done | bytes 110624 | tf_op jit(solution)/shard_map/ppermute | solution.py:25
  14.6 7.0 %all-to-all-start = ((bf16[16,48,1152]{2,1,0:T(8,128)(2,1)}), bf16[16,48,1152]{2,1,0:T(8,128)(2,1)S(1)}, u32[]{:S(2)}, u32[]{:S(2)}) async-start(bf16[16,48,1152]{2,1,0:T(8,128)(2,1)} %broadcast_in_dim.2), calls=%async_computation | async-start | bytes 3538944 | tf_op jit(solution)/shard_map/all_to_all | solution.py:182
  26.9 4.5 %collective-permute-start.6 = (bf16[96,1152]{1,0:T(8,128)(2,1)S(1)}, bf16[96,1152]{1,0:T(8,128)(2,1)S(1)}, u32[]{:S(2)}, u32[]{:S(2)}) collective-permute-start(bf16[96,1152]{1,0:T(8,128)(2,1)S(1)} %pad_maximum_fusion.5), channel_id=1, source_target_pairs={{0,32},{16,48},{32,64},{48,80},{64,96},{80,112},{96,0},{112,16},{1... | collective-permute-start | bytes 663560 | tf_op jit(solution)/shard_map/ppermute | solution.py:57
  35.3 11.4 %collective-permute-done.8 = bf16[48,1152]{1,0:T(8,128)(2,1)S(1)} collective-permute-done((bf16[48,1152]{1,0:T(8,128)(2,1)}, bf16[48,1152]{1,0:T(8,128)(2,1)S(1)}, u32[]{:S(2)}, u32[]{:S(2)}) %collective-permute-start.8) | collective-permute-done | bytes 110624 | tf_op jit(solution)/shard_map/ppermute | solution.py:57
  47.5 4.5 %collective-permute-start.9 = (bf16[336,1152]{1,0:T(8,128)(2,1)S(1)}, bf16[336,1152]{1,0:T(8,128)(2,1)S(1)}, u32[]{:S(2)}, u32[]{:S(2)}) collective-permute-start(bf16[336,1152]{1,0:T(8,128)(2,1)S(1)} %pad_maximum_fusion), channel_id=1, source_target_pairs={{0,1},{1,0},{2,3},{3,2},{4,5},{5,4},{6,7},{7,6},{8,9},{9,8},{10,11... | collective-permute-start | bytes 2322440 | tf_op jit(solution)/shard_map/ppermute | solution.py:25
  55.8 3.5 %multiply_convert_fusion = bf16[768,768]{1,0:T(8,128)(2,1)S(1)} fusion(bf16[768,1152]{1,0:T(8,128)(2,1)S(1)} %bitcast.170, bf16[768,1152]{1,0:T(8,128)(2,1)} %constant_dynamic-update-slice_fusion, s32[]{:T(128)S(6)} %select_n.214, s32[768]{0:T(1024)} %iota_divide_fusion, s32[768]{0:T(1024)} %broadcast_add_fusion, s32[768]{0:T(1024)S(1)} %iota_subtract_fusion, ...), kind=kOutput, calls=%fused_computation.3 | convolution fusion | flops 1366622208 | bytes 4731652 | tf_op jit(solution)/shard_map/dot_general | solution.py:186
  62.7 4.8 %convolution_convert_fusion = bf16[768,1152]{1,0:T(8,128)(2,1)} fusion(bf16[768,768]{1,0:T(8,128)(2,1)} %copy-done.12, bf16[768,1152]{1,0:T(8,128)(2,1)} %constant_dynamic-update-slice_fusion), kind=kOutput, calls=%fused_computation.1 | convolution fusion | flops 1359839232 | bytes 4718592 | tf_op jit(solution)/shard_map/dot_general | solution.py:197
  68.4 6.9 %all-to-all-start.1 = ((bf16[16,48,1152]{2,1,0:T(8,128)(2,1)}), bf16[16,48,1152]{2,1,0:T(8,128)(2,1)S(1)}, u32[]{:S(2)}, u32[]{:S(2)}) async-start(bf16[16,48,1152]{2,1,0:T(8,128)(2,1)} %bitcast.172), calls=%async_computation.1 | async-start | bytes 3538944 | tf_op jit(solution)/shard_map/all_to_all | solution.py:199
  77.6 4.2 %collective-permute-start.12 = (bf16[96,1152]{1,0:T(8,128)(2,1)S(1)}, bf16[96,1152]{1,0:T(8,128)(2,1)S(1)}, u32[]{:S(2)}, u32[]{:S(2)}) collective-permute-start(bf16[96,1152]{1,0:T(8,128)(2,1)S(1)} %get-tuple-element.34), channel_id=1, source_target_pairs={{0,96},{16,112},{32,0},{48,16},{64,32},{80,48},{96,64},{112,80},{1... | collective-permute-start | bytes 663560 | tf_op jit(solution)/shard_map/ppermute | solution.py:57
  83.4 2.9 %collective-permute-start.14 = (bf16[48,1152]{1,0:T(8,128)(2,1)}, bf16[48,1152]{1,0:T(8,128)(2,1)}, u32[]{:S(2)}, u32[]{:S(2)}) collective-permute-start(bf16[48,1152]{1,0:T(8,128)(2,1)} %add_convert_fusion.3), channel_id=1, source_target_pairs={{0,64},{16,80},{32,96},{48,112},{64,0},{80,16},{96,32},{112,48},{1... | collective-permute-start | bytes 331784 | tf_op jit(solution)/shard_map/ppermute | solution.py:57
  86.3 5.7 %collective-permute-done.12 = bf16[96,1152]{1,0:T(8,128)(2,1)S(1)} collective-permute-done((bf16[96,1152]{1,0:T(8,128)(2,1)S(1)}, bf16[96,1152]{1,0:T(8,128)(2,1)S(1)}, u32[]{:S(2)}, u32[]{:S(2)}) %collective-permute-start.12) | collective-permute-done | bytes 221216 | tf_op jit(solution)/shard_map/ppermute | solution.py:57
  92.0 6.2 %collective-permute-done.11 = bf16[96,1152]{1,0:T(8,128)(2,1)S(1)} collective-permute-done((bf16[96,1152]{1,0:T(8,128)(2,1)S(1)}, bf16[96,1152]{1,0:T(8,128)(2,1)S(1)}, u32[]{:S(2)}, u32[]{:S(2)}) %collective-permute-start.11) | collective-permute-done | bytes 221216 | tf_op jit(solution)/shard_map/ppermute | solution.py:57
  100.5 2.6 %all-to-all-done.1 = bf16[16,48,1152]{2,1,0:T(8,128)(2,1)S(1)} async-done(((bf16[16,48,1152]{2,1,0:T(8,128)(2,1)}), bf16[16,48,1152]{2,1,0:T(8,128)(2,1)S(1)}, u32[]{:S(2)}, u32[]{:S(2)}) %all-to-all-start.1) | async-done | bytes 1769504 | tf_op jit(solution)/shard_map/all_to_all | solution.py:199
  105.5 8.3 %all_gather.3 = bf16[192,2304]{1,0:T(8,128)(2,1)S(1)} all-gather(bf16[48,2304]{1,0:T(8,128)(2,1)S(1)} %pad_maximum_fusion.6), channel_id=1, replica_groups=mesh['yhi'=2,'z'=8,'x'=4,'ylo'=2,'core'=2] {'ylo','core'}, dimensions={0}, use_global_device_ids=true | all-gather | bytes 1105920 | tf_op jit(solution)/shard_map/all_gather | solution.py:205
  117.2 4.0 %collective-permute-done.18 = bf16[2,32,1152]{2,1,0:T(8,128)(2,1)S(1)} collective-permute-done((bf16[2,32,1152]{2,1,0:T(8,128)(2,1)S(1)}, bf16[2,32,1152]{2,1,0:T(8,128)(2,1)S(1)}, u32[]{:S(2)}, u32[]{:S(2)}) %collective-permute-start.18) | collective-permute-done | bytes 147488 | tf_op jit(solution)/shard_map/ppermute | solution.py:20
  121.3 3.1 %collective-permute-start.19 = (bf16[2,72,1152]{2,1,0:T(8,128)(2,1)S(1)}, bf16[2,72,1152]{2,1,0:T(8,128)(2,1)S(1)}, u32[]{:S(2)}, u32[]{:S(2)}) collective-permute-start(bf16[2,72,1152]{2,1,0:T(8,128)(2,1)S(1)} %pad_maximum_fusion.2), channel_id=1, source_target_pairs={{0,12},{4,0},{8,4},{12,8},{1,13},{5,1},{9,5},{13,9},{2,14},{6,2},{... | collective-permute-start | bytes 995336 | tf_op jit(solution)/shard_map/ppermute | solution.py:20
  125.0 6.1 %collective-permute-done.19 = bf16[2,72,1152]{2,1,0:T(8,128)(2,1)S(1)} collective-permute-done((bf16[2,72,1152]{2,1,0:T(8,128)(2,1)S(1)}, bf16[2,72,1152]{2,1,0:T(8,128)(2,1)S(1)}, u32[]{:S(2)}, u32[]{:S(2)}) %collective-permute-start.19) | collective-permute-done | bytes 331808 | tf_op jit(solution)/shard_map/ppermute | solution.py:20
  131.1 3.9 %collective-permute-done.17 = bf16[2,72,1152]{2,1,0:T(8,128)(2,1)S(1)} collective-permute-done((bf16[2,72,1152]{2,1,0:T(8,128)(2,1)S(1)}, bf16[2,72,1152]{2,1,0:T(8,128)(2,1)S(1)}, u32[]{:S(2)}, u32[]{:S(2)}) %collective-permute-start.17) | collective-permute-done | bytes 331808 | tf_op jit(solution)/shard_map/ppermute | solution.py:20
  136.8 5.0 %collective-permute-start.24 = (bf16[2,168,128]{2,1,0:T(8,128)(2,1)S(1)}, bf16[2,168,128]{2,1,0:T(8,128)(2,1)S(1)}, u32[]{:S(2)}, u32[]{:S(2)}) collective-permute-start(bf16[2,168,128]{2,1,0:T(8,128)(2,1)S(1)} %pad_maximum_fusion.12), channel_id=1, source_target_pairs={{0,48},{16,64},{32,80},{48,96},{64,112},{80,0},{96,16},{112,32},{1... | collective-permute-start | bytes 258056 | tf_op jit(solution)/shard_map/ppermute | solution.py:57
  143.3 3.4 %collective-permute-start.20 = (bf16[168,128]{1,0:T(8,128)(2,1)S(1)}, bf16[168,128]{1,0:T(8,128)(2,1)S(1)}, u32[]{:S(2)}, u32[]{:S(2)}) collective-permute-start(bf16[168,128]{1,0:T(8,128)(2,1)S(1)} %get-tuple-element.41), channel_id=1, source_target_pairs={{0,64},{16,80},{32,96},{48,112},{64,0},{80,16},{96,32},{112,48},{1... | collective-permute-start | bytes 129032 | tf_op jit(solution)/shard_map/ppermute | solution.py:57
  146.7 2.8 %collective-permute-done.23 = bf16[2,168,128]{2,1,0:T(8,128)(2,1)S(1)} collective-permute-done((bf16[2,168,128]{2,1,0:T(8,128)(2,1)S(1)}, bf16[2,168,128]{2,1,0:T(8,128)(2,1)S(1)}, u32[]{:S(2)}, u32[]{:S(2)}) %collective-permute-start.23) | collective-permute-done | bytes 86048 | tf_op jit(solution)/shard_map/ppermute | solution.py:57
  149.6 2.3 %collective-permute-done.20 = bf16[168,128]{1,0:T(8,128)(2,1)S(1)} collective-permute-done((bf16[168,128]{1,0:T(8,128)(2,1)S(1)}, bf16[168,128]{1,0:T(8,128)(2,1)S(1)}, u32[]{:S(2)}, u32[]{:S(2)}) %collective-permute-start.20) | collective-permute-done | bytes 43040 | tf_op jit(solution)/shard_map/ppermute | solution.py:57
  151.9 3.0 %collective-permute-start.26 = (bf16[168,128]{1,0:T(8,128)(2,1)S(1)}, bf16[168,128]{1,0:T(8,128)(2,1)S(1)}, u32[]{:S(2)}, u32[]{:S(2)}) collective-permute-start(bf16[168,128]{1,0:T(8,128)(2,1)S(1)} %fusion.26), channel_id=1, source_target_pairs={{0,128},{128,0},{1,129},{129,1},{2,130},{130,2},{3,131},{131,3},{4... | collective-permute-start | bytes 129032 | tf_op jit(solution)/shard_map/ppermute | solution.py:25
  154.9 2.6 %collective-permute-done.26 = bf16[168,128]{1,0:T(8,128)(2,1)S(1)} collective-permute-done((bf16[168,128]{1,0:T(8,128)(2,1)S(1)}, bf16[168,128]{1,0:T(8,128)(2,1)S(1)}, u32[]{:S(2)}, u32[]{:S(2)}) %collective-permute-start.26) | collective-permute-done | bytes 43040 | tf_op jit(solution)/shard_map/ppermute | solution.py:25
  158.2 2.8 %collective-permute-start.27 = (bf16[168,128]{1,0:T(8,128)(2,1)S(1)}, bf16[168,128]{1,0:T(8,128)(2,1)S(1)}, u32[]{:S(2)}, u32[]{:S(2)}) collective-permute-start(bf16[168,128]{1,0:T(8,128)(2,1)S(1)} %get-tuple-element.25), channel_id=1, source_target_pairs={{0,64},{16,80},{32,96},{48,112},{64,0},{80,16},{96,32},{112,48},{1... | collective-permute-start | bytes 129032 | tf_op jit(solution)/shard_map/ppermute | solution.py:57
  160.9 2.8 %collective-permute-start.29 = (bf16[2,168,128]{2,1,0:T(8,128)(2,1)S(1)}, bf16[2,168,128]{2,1,0:T(8,128)(2,1)S(1)}, u32[]{:S(2)}, u32[]{:S(2)}) collective-permute-start(bf16[2,168,128]{2,1,0:T(8,128)(2,1)S(1)} %pad_maximum_fusion.13), channel_id=1, source_target_pairs={{0,16},{16,32},{32,48},{48,64},{64,80},{80,96},{96,112},{112,0},{1... | collective-permute-start | bytes 258056 | tf_op jit(solution)/shard_map/ppermute | solution.py:57
  164.1 2.7 %collective-permute-start.31 = (bf16[2,168,128]{2,1,0:T(8,128)(2,1)S(1)}, bf16[2,168,128]{2,1,0:T(8,128)(2,1)S(1)}, u32[]{:S(2)}, u32[]{:S(2)}) collective-permute-start(bf16[2,168,128]{2,1,0:T(8,128)(2,1)S(1)} %pad_maximum_fusion.13), channel_id=1, source_target_pairs={{0,48},{16,64},{32,80},{48,96},{64,112},{80,0},{96,16},{112,32},{1... | collective-permute-start | bytes 258056 | tf_op jit(solution)/shard_map/ppermute | solution.py:57
  168.0 2.4 %collective-permute-done.30 = bf16[2,168,128]{2,1,0:T(8,128)(2,1)S(1)} collective-permute-done((bf16[2,168,128]{2,1,0:T(8,128)(2,1)S(1)}, bf16[2,168,128]{2,1,0:T(8,128)(2,1)S(1)}, u32[]{:S(2)}, u32[]{:S(2)}) %collective-permute-start.30) | collective-permute-done | bytes 86048 | tf_op jit(solution)/shard_map/ppermute | solution.py:57
  170.3 3.2 %collective-permute-done.31 = bf16[2,168,128]{2,1,0:T(8,128)(2,1)S(1)} collective-permute-done((bf16[2,168,128]{2,1,0:T(8,128)(2,1)S(1)}, bf16[2,168,128]{2,1,0:T(8,128)(2,1)S(1)}, u32[]{:S(2)}, u32[]{:S(2)}) %collective-permute-start.31) | collective-permute-done | bytes 86048 | tf_op jit(solution)/shard_map/ppermute | solution.py:57
  177.9 7.7 %collective-permute-done.33 = bf16[2,72,1152]{2,1,0:T(8,128)(2,1)S(1)} collective-permute-done((bf16[2,72,1152]{2,1,0:T(8,128)(2,1)S(1)}, bf16[2,72,1152]{2,1,0:T(8,128)(2,1)S(1)}, u32[]{:S(2)}, u32[]{:S(2)}) %collective-permute-start.33) | collective-permute-done | bytes 331808 | tf_op jit(solution)/shard_map/ppermute | solution.py:20
  187.8 3.0 %collective-permute-done.36 = bf16[2,32,1152]{2,1,0:T(8,128)(2,1)S(1)} collective-permute-done((bf16[2,32,1152]{2,1,0:T(8,128)(2,1)S(1)}, bf16[2,32,1152]{2,1,0:T(8,128)(2,1)S(1)}, u32[]{:S(2)}, u32[]{:S(2)}) %collective-permute-start.36) | collective-permute-done | bytes 147488 | tf_op jit(solution)/shard_map/ppermute | solution.py:20
  190.9 3.6 %collective-permute-done.35 = bf16[2,40,1152]{2,1,0:T(8,128)(2,1)S(1)} collective-permute-done((bf16[2,40,1152]{2,1,0:T(8,128)(2,1)S(1)}, bf16[2,40,1152]{2,1,0:T(8,128)(2,1)S(1)}, u32[]{:S(2)}, u32[]{:S(2)}) %collective-permute-start.35) | collective-permute-done | bytes 184352 | tf_op jit(solution)/shard_map/ppermute | solution.py:20
  (176 shorter events, 54.0 us)
Async XLA Ops:
  4.8 6.0 %collective-permute-start.3 = (bf16[48,1152]{1,0:T(8,128)(2,1)S(1)}, bf16[48,1152]{1,0:T(8,128)(2,1)S(1)}, u32[]{:S(2)}, u32[]{:S(2)}) collective-permute-start(bf16[48,1152]{1,0:T(8,128)(2,1)S(1)} %fusion.24), channel_id=1, source_target_pairs={{0,2},{2,0},{1,3},{3,1},{4,6},{6,4},{5,7},{7,5},{8,10},{10,8},{9,1... | collective-permute-start | bytes 331784 | tf_op jit(solution)/shard_map/ppermute | solution.py:25
  6.5 5.7 %collective-permute-start.1 = (bf16[48,1152]{1,0:T(8,128)(2,1)S(1)}, bf16[48,1152]{1,0:T(8,128)(2,1)S(1)}, u32[]{:S(2)}, u32[]{:S(2)}) collective-permute-start(bf16[48,1152]{1,0:T(8,128)(2,1)S(1)} %fusion.23), channel_id=1, source_target_pairs={{0,2},{2,0},{1,3},{3,1},{4,6},{6,4},{5,7},{7,5},{8,10},{10,8},{9,1... | collective-permute-start | bytes 331784 | tf_op jit(solution)/shard_map/ppermute | solution.py:25
  14.6 7.0 %collective-permute-start.4 = (bf16[48,1152]{1,0:T(8,128)(2,1)}, bf16[48,1152]{1,0:T(8,128)(2,1)}, u32[]{:S(2)}, u32[]{:S(2)}) collective-permute-start(bf16[48,1152]{1,0:T(8,128)(2,1)} %fusion.32), channel_id=1, source_target_pairs={{0,1},{1,0},{2,3},{3,2},{4,5},{5,4},{6,7},{7,6},{8,9},{9,8},{10,11... | collective-permute-start | bytes 331784 | tf_op jit(solution)/shard_map/ppermute | solution.py:25
  14.6 41.2 %all-to-all-start = ((bf16[16,48,1152]{2,1,0:T(8,128)(2,1)}), bf16[16,48,1152]{2,1,0:T(8,128)(2,1)S(1)}, u32[]{:S(2)}, u32[]{:S(2)}) async-start(bf16[16,48,1152]{2,1,0:T(8,128)(2,1)} %broadcast_in_dim.2), calls=%async_computation | async-start | bytes 3538944 | tf_op jit(solution)/shard_map/all_to_all | solution.py:182
  24.9 21.8 %collective-permute-start.5 = (bf16[96,1152]{1,0:T(8,128)(2,1)S(1)}, bf16[96,1152]{1,0:T(8,128)(2,1)S(1)}, u32[]{:S(2)}, u32[]{:S(2)}) collective-permute-start(bf16[96,1152]{1,0:T(8,128)(2,1)S(1)} %pad_maximum_fusion.5), channel_id=1, source_target_pairs={{0,16},{16,32},{32,48},{48,64},{64,80},{80,96},{96,112},{112,0},{1... | collective-permute-start | bytes 663560 | tf_op jit(solution)/shard_map/ppermute | solution.py:57
  26.9 19.8 %collective-permute-start.6 = (bf16[96,1152]{1,0:T(8,128)(2,1)S(1)}, bf16[96,1152]{1,0:T(8,128)(2,1)S(1)}, u32[]{:S(2)}, u32[]{:S(2)}) collective-permute-start(bf16[96,1152]{1,0:T(8,128)(2,1)S(1)} %pad_maximum_fusion.5), channel_id=1, source_target_pairs={{0,32},{16,48},{32,64},{48,80},{64,96},{80,112},{96,0},{112,16},{1... | collective-permute-start | bytes 663560 | tf_op jit(solution)/shard_map/ppermute | solution.py:57
  31.3 16.1 %collective-permute-start.7 = (bf16[96,1152]{1,0:T(8,128)(2,1)S(1)}, bf16[96,1152]{1,0:T(8,128)(2,1)S(1)}, u32[]{:S(2)}, u32[]{:S(2)}) collective-permute-start(bf16[96,1152]{1,0:T(8,128)(2,1)S(1)} %pad_maximum_fusion.5), channel_id=1, source_target_pairs={{0,48},{16,64},{32,80},{48,96},{64,112},{80,0},{96,16},{112,32},{1... | collective-permute-start | bytes 663560 | tf_op jit(solution)/shard_map/ppermute | solution.py:57
  33.3 13.4 %collective-permute-start.8 = (bf16[48,1152]{1,0:T(8,128)(2,1)}, bf16[48,1152]{1,0:T(8,128)(2,1)S(1)}, u32[]{:S(2)}, u32[]{:S(2)}) collective-permute-start(bf16[48,1152]{1,0:T(8,128)(2,1)} %fusion.32), channel_id=1, source_target_pairs={{0,64},{16,80},{32,96},{48,112},{64,0},{80,16},{96,32},{112,48},{1... | collective-permute-start | bytes 331784 | tf_op jit(solution)/shard_map/ppermute | solution.py:57
  47.5 7.3 %collective-permute-start.9 = (bf16[336,1152]{1,0:T(8,128)(2,1)S(1)}, bf16[336,1152]{1,0:T(8,128)(2,1)S(1)}, u32[]{:S(2)}, u32[]{:S(2)}) collective-permute-start(bf16[336,1152]{1,0:T(8,128)(2,1)S(1)} %pad_maximum_fusion), channel_id=1, source_target_pairs={{0,1},{1,0},{2,3},{3,2},{4,5},{5,4},{6,7},{7,6},{8,9},{9,8},{10,11... | collective-permute-start | bytes 2322440 | tf_op jit(solution)/shard_map/ppermute | solution.py:25
  62.4 5.1 %collective-permute-start.10 = (bf16[336,1152]{1,0:T(8,128)(2,1)S(1)}, bf16[336,1152]{1,0:T(8,128)(2,1)S(1)}, u32[]{:S(2)}, u32[]{:S(2)}) collective-permute-start(bf16[336,1152]{1,0:T(8,128)(2,1)S(1)} %slice.216), channel_id=1, source_target_pairs={{0,1},{1,0},{2,3},{3,2},{4,5},{5,4},{6,7},{7,6},{8,9},{9,8},{10,11... | collective-permute-start | bytes 2322440 | tf_op jit(solution)/shard_map/ppermute | solution.py:25
  68.4 34.7 %all-to-all-start.1 = ((bf16[16,48,1152]{2,1,0:T(8,128)(2,1)}), bf16[16,48,1152]{2,1,0:T(8,128)(2,1)S(1)}, u32[]{:S(2)}, u32[]{:S(2)}) async-start(bf16[16,48,1152]{2,1,0:T(8,128)(2,1)} %bitcast.172), calls=%async_computation.1 | async-start | bytes 3538944 | tf_op jit(solution)/shard_map/all_to_all | solution.py:199
  76.9 9.4 %collective-permute-start.13 = (bf16[96,1152]{1,0:T(8,128)(2,1)S(1)}, bf16[96,1152]{1,0:T(8,128)(2,1)S(1)}, u32[]{:S(2)}, u32[]{:S(2)}) collective-permute-start(bf16[96,1152]{1,0:T(8,128)(2,1)S(1)} %get-tuple-element.33), channel_id=1, source_target_pairs={{0,112},{16,0},{32,16},{48,32},{64,48},{80,64},{96,80},{112,96},{1... | collective-permute-start | bytes 663560 | tf_op jit(solution)/shard_map/ppermute | solution.py:57
  77.6 14.5 %collective-permute-start.12 = (bf16[96,1152]{1,0:T(8,128)(2,1)S(1)}, bf16[96,1152]{1,0:T(8,128)(2,1)S(1)}, u32[]{:S(2)}, u32[]{:S(2)}) collective-permute-start(bf16[96,1152]{1,0:T(8,128)(2,1)S(1)} %get-tuple-element.34), channel_id=1, source_target_pairs={{0,96},{16,112},{32,0},{48,16},{64,32},{80,48},{96,64},{112,80},{1... | collective-permute-start | bytes 663560 | tf_op jit(solution)/shard_map/ppermute | solution.py:57
  81.8 16.4 %collective-permute-start.11 = (bf16[96,1152]{1,0:T(8,128)(2,1)S(1)}, bf16[96,1152]{1,0:T(8,128)(2,1)S(1)}, u32[]{:S(2)}, u32[]{:S(2)}) collective-permute-start(bf16[96,1152]{1,0:T(8,128)(2,1)S(1)} %get-tuple-element.32), channel_id=1, source_target_pairs={{0,80},{16,96},{32,112},{48,0},{64,16},{80,32},{96,48},{112,64},{1... | collective-permute-start | bytes 663560 | tf_op jit(solution)/shard_map/ppermute | solution.py:57
  83.4 20.2 %collective-permute-start.14 = (bf16[48,1152]{1,0:T(8,128)(2,1)}, bf16[48,1152]{1,0:T(8,128)(2,1)}, u32[]{:S(2)}, u32[]{:S(2)}) collective-permute-start(bf16[48,1152]{1,0:T(8,128)(2,1)} %add_convert_fusion.3), channel_id=1, source_target_pairs={{0,64},{16,80},{32,96},{48,112},{64,0},{80,16},{96,32},{112,48},{1... | collective-permute-start | bytes 331784 | tf_op jit(solution)/shard_map/ppermute | solution.py:57
  115.0 6.2 %collective-permute-start.18 = (bf16[2,32,1152]{2,1,0:T(8,128)(2,1)S(1)}, bf16[2,32,1152]{2,1,0:T(8,128)(2,1)S(1)}, u32[]{:S(2)}, u32[]{:S(2)}) collective-permute-start(bf16[2,32,1152]{2,1,0:T(8,128)(2,1)S(1)} %pad_maximum_fusion.7), channel_id=1, source_target_pairs={{0,12},{4,0},{8,4},{12,8},{1,13},{5,1},{9,5},{13,9},{2,14},{6,2},{... | collective-permute-start | bytes 442376 | tf_op jit(solution)/shard_map/ppermute | solution.py:20
  116.9 7.8 %collective-permute-start.16 = (bf16[2,40,1152]{2,1,0:T(8,128)(2,1)S(1)}, bf16[2,40,1152]{2,1,0:T(8,128)(2,1)S(1)}, u32[]{:S(2)}, u32[]{:S(2)}) collective-permute-start(bf16[2,40,1152]{2,1,0:T(8,128)(2,1)S(1)} %fusion.18), channel_id=1, source_target_pairs={{0,4},{4,8},{8,12},{12,0},{1,5},{5,9},{9,13},{13,1},{2,6},{6,10},{... | collective-permute-start | bytes 552968 | tf_op jit(solution)/shard_map/ppermute | solution.py:20
  121.3 9.9 %collective-permute-start.19 = (bf16[2,72,1152]{2,1,0:T(8,128)(2,1)S(1)}, bf16[2,72,1152]{2,1,0:T(8,128)(2,1)S(1)}, u32[]{:S(2)}, u32[]{:S(2)}) collective-permute-start(bf16[2,72,1152]{2,1,0:T(8,128)(2,1)S(1)} %pad_maximum_fusion.2), channel_id=1, source_target_pairs={{0,12},{4,0},{8,4},{12,8},{1,13},{5,1},{9,5},{13,9},{2,14},{6,2},{... | collective-permute-start | bytes 995336 | tf_op jit(solution)/shard_map/ppermute | solution.py:20
  124.8 10.2 %collective-permute-start.17 = (bf16[2,72,1152]{2,1,0:T(8,128)(2,1)S(1)}, bf16[2,72,1152]{2,1,0:T(8,128)(2,1)S(1)}, u32[]{:S(2)}, u32[]{:S(2)}) collective-permute-start(bf16[2,72,1152]{2,1,0:T(8,128)(2,1)S(1)} %pad_maximum_fusion.1), channel_id=1, source_target_pairs={{0,4},{4,8},{8,12},{12,0},{1,5},{5,9},{9,13},{13,1},{2,6},{6,10},{... | collective-permute-start | bytes 995336 | tf_op jit(solution)/shard_map/ppermute | solution.py:20
  136.8 9.9 %collective-permute-start.24 = (bf16[2,168,128]{2,1,0:T(8,128)(2,1)S(1)}, bf16[2,168,128]{2,1,0:T(8,128)(2,1)S(1)}, u32[]{:S(2)}, u32[]{:S(2)}) collective-permute-start(bf16[2,168,128]{2,1,0:T(8,128)(2,1)S(1)} %pad_maximum_fusion.12), channel_id=1, source_target_pairs={{0,48},{16,64},{32,80},{48,96},{64,112},{80,0},{96,16},{112,32},{1... | collective-permute-start | bytes 258056 | tf_op jit(solution)/shard_map/ppermute | solution.py:57
  141.8 7.6 %collective-permute-start.23 = (bf16[2,168,128]{2,1,0:T(8,128)(2,1)S(1)}, bf16[2,168,128]{2,1,0:T(8,128)(2,1)S(1)}, u32[]{:S(2)}, u32[]{:S(2)}) collective-permute-start(bf16[2,168,128]{2,1,0:T(8,128)(2,1)S(1)} %pad_maximum_fusion.11), channel_id=1, source_target_pairs={{0,32},{16,48},{32,64},{48,80},{64,96},{80,112},{96,0},{112,16},{1... | collective-permute-start | bytes 258056 | tf_op jit(solution)/shard_map/ppermute | solution.py:57
  142.5 7.0 %collective-permute-start.22 = (bf16[2,168,128]{2,1,0:T(8,128)(2,1)S(1)}, bf16[2,168,128]{2,1,0:T(8,128)(2,1)S(1)}, u32[]{:S(2)}, u32[]{:S(2)}) collective-permute-start(bf16[2,168,128]{2,1,0:T(8,128)(2,1)S(1)} %pad_maximum_fusion.10), channel_id=1, source_target_pairs={{0,16},{16,32},{32,48},{48,64},{64,80},{80,96},{96,112},{112,0},{1... | collective-permute-start | bytes 258056 | tf_op jit(solution)/shard_map/ppermute | solution.py:57
  143.3 8.6 %collective-permute-start.20 = (bf16[168,128]{1,0:T(8,128)(2,1)S(1)}, bf16[168,128]{1,0:T(8,128)(2,1)S(1)}, u32[]{:S(2)}, u32[]{:S(2)}) collective-permute-start(bf16[168,128]{1,0:T(8,128)(2,1)S(1)} %get-tuple-element.41), channel_id=1, source_target_pairs={{0,64},{16,80},{32,96},{48,112},{64,0},{80,16},{96,32},{112,48},{1... | collective-permute-start | bytes 129032 | tf_op jit(solution)/shard_map/ppermute | solution.py:57
  151.9 5.6 %collective-permute-start.26 = (bf16[168,128]{1,0:T(8,128)(2,1)S(1)}, bf16[168,128]{1,0:T(8,128)(2,1)S(1)}, u32[]{:S(2)}, u32[]{:S(2)}) collective-permute-start(bf16[168,128]{1,0:T(8,128)(2,1)S(1)} %fusion.26), channel_id=1, source_target_pairs={{0,128},{128,0},{1,129},{129,1},{2,130},{130,2},{3,131},{131,3},{4... | collective-permute-start | bytes 129032 | tf_op jit(solution)/shard_map/ppermute | solution.py:25
  158.2 9.8 %collective-permute-start.27 = (bf16[168,128]{1,0:T(8,128)(2,1)S(1)}, bf16[168,128]{1,0:T(8,128)(2,1)S(1)}, u32[]{:S(2)}, u32[]{:S(2)}) collective-permute-start(bf16[168,128]{1,0:T(8,128)(2,1)S(1)} %get-tuple-element.25), channel_id=1, source_target_pairs={{0,64},{16,80},{32,96},{48,112},{64,0},{80,16},{96,32},{112,48},{1... | collective-permute-start | bytes 129032 | tf_op jit(solution)/shard_map/ppermute | solution.py:57
  160.9 7.0 %collective-permute-start.29 = (bf16[2,168,128]{2,1,0:T(8,128)(2,1)S(1)}, bf16[2,168,128]{2,1,0:T(8,128)(2,1)S(1)}, u32[]{:S(2)}, u32[]{:S(2)}) collective-permute-start(bf16[2,168,128]{2,1,0:T(8,128)(2,1)S(1)} %pad_maximum_fusion.13), channel_id=1, source_target_pairs={{0,16},{16,32},{32,48},{48,64},{64,80},{80,96},{96,112},{112,0},{1... | collective-permute-start | bytes 258056 | tf_op jit(solution)/shard_map/ppermute | solution.py:57
  163.7 6.6 %collective-permute-start.30 = (bf16[2,168,128]{2,1,0:T(8,128)(2,1)S(1)}, bf16[2,168,128]{2,1,0:T(8,128)(2,1)S(1)}, u32[]{:S(2)}, u32[]{:S(2)}) collective-permute-start(bf16[2,168,128]{2,1,0:T(8,128)(2,1)S(1)} %pad_maximum_fusion.13), channel_id=1, source_target_pairs={{0,32},{16,48},{32,64},{48,80},{64,96},{80,112},{96,0},{112,16},{1... | collective-permute-start | bytes 258056 | tf_op jit(solution)/shard_map/ppermute | solution.py:57
  164.1 9.4 %collective-permute-start.31 = (bf16[2,168,128]{2,1,0:T(8,128)(2,1)S(1)}, bf16[2,168,128]{2,1,0:T(8,128)(2,1)S(1)}, u32[]{:S(2)}, u32[]{:S(2)}) collective-permute-start(bf16[2,168,128]{2,1,0:T(8,128)(2,1)S(1)} %pad_maximum_fusion.13), channel_id=1, source_target_pairs={{0,48},{16,64},{32,80},{48,96},{64,112},{80,0},{96,16},{112,32},{1... | collective-permute-start | bytes 258056 | tf_op jit(solution)/shard_map/ppermute | solution.py:57
  175.5 10.1 %collective-permute-start.33 = (bf16[2,72,1152]{2,1,0:T(8,128)(2,1)S(1)}, bf16[2,72,1152]{2,1,0:T(8,128)(2,1)S(1)}, u32[]{:S(2)}, u32[]{:S(2)}) collective-permute-start(bf16[2,72,1152]{2,1,0:T(8,128)(2,1)S(1)} %bitcast.176), channel_id=1, source_target_pairs={{0,12},{4,0},{8,4},{12,8},{1,13},{5,1},{9,5},{13,9},{2,14},{6,2},{... | collective-permute-start | bytes 995336 | tf_op jit(solution)/shard_map/ppermute | solution.py:20
  175.6 11.6 %collective-permute-start.34 = (bf16[2,72,1152]{2,1,0:T(8,128)(2,1)S(1)}, bf16[2,72,1152]{2,1,0:T(8,128)(2,1)S(1)}, u32[]{:S(2)}, u32[]{:S(2)}) collective-permute-start(bf16[2,72,1152]{2,1,0:T(8,128)(2,1)S(1)} %bitcast.177), channel_id=1, source_target_pairs={{0,4},{4,8},{8,12},{12,0},{1,5},{5,9},{9,13},{13,1},{2,6},{6,10},{... | collective-permute-start | bytes 995336 | tf_op jit(solution)/shard_map/ppermute | solution.py:20
  185.6 5.3 %collective-permute-start.36 = (bf16[2,32,1152]{2,1,0:T(8,128)(2,1)S(1)}, bf16[2,32,1152]{2,1,0:T(8,128)(2,1)S(1)}, u32[]{:S(2)}, u32[]{:S(2)}) collective-permute-start(bf16[2,32,1152]{2,1,0:T(8,128)(2,1)S(1)} %slice.244), channel_id=1, source_target_pairs={{0,12},{4,0},{8,4},{12,8},{1,13},{5,1},{9,5},{13,9},{2,14},{6,2},{... | collective-permute-start | bytes 442376 | tf_op jit(solution)/shard_map/ppermute | solution.py:20
  187.2 7.3 %collective-permute-start.35 = (bf16[2,40,1152]{2,1,0:T(8,128)(2,1)S(1)}, bf16[2,40,1152]{2,1,0:T(8,128)(2,1)S(1)}, u32[]{:S(2)}, u32[]{:S(2)}) collective-permute-start(bf16[2,40,1152]{2,1,0:T(8,128)(2,1)S(1)} %slice.242), channel_id=1, source_target_pairs={{0,4},{4,8},{8,12},{12,0},{1,5},{5,9},{9,13},{13,1},{2,6},{6,10},{... | collective-permute-start | bytes 552968 | tf_op jit(solution)/shard_map/ppermute | solution.py:20
  (20 other events, 100.9 us)

commit v2 on v1

--- a/solution.py
+++ b/solution.py
@@ -63,7 +63,7 @@
     pair = jnp.concatenate([jnp.where(first, value, other), jnp.where(first, other, value)], axis=0)
     far = column_shift(value, 4)
     got = {k: column_shift(pair, k) for k in (3, 2, 1)}
-    mine = jnp.concatenate([got[1], got[2], got[3], far], axis=0)
+    mine = lax.optimization_barrier(jnp.concatenate([got[1], got[2], got[3], far], axis=0))
     return jnp.concatenate([pair, mine, flip(mine, "core", 1)], axis=0)
 
 
@@ -186,7 +186,8 @@
     scores = lax.dot_general(images, texts, (((1,), (1,)), ((), ())), preferred_element_type=F32)
     row_id = lax.broadcasted_iota(jnp.int32, scores.shape, 0)
     col_id = lax.broadcasted_iota(jnp.int32, scores.shape, 1)
-    label = (row_id - own_image == col_id - own_text) & (col_id // quarter == own_text // quarter)
+    own_id = col_id - own_text
+    label = (row_id == own_id + own_image) & (own_id >= 0) & (own_id < quarter)
     weights = (SCALE * (jax.nn.sigmoid(SCALE * scores + OFFSET) - label.astype(F32))).astype(BF16)
 
     text_part = lax.dot_general(

time: 197 us -> 198 us (level)
  waiting for transfers between devices: 75.3 us -> 79.2 us
    ppermute x13, starting transfers between devices: 11.4 us -> 7.19 us  [flip(): return lax.ppermute(value, axis, [(i, i ^ bit) for i in range(n)])]
    unnamed x14 -> x12, other arithmetic: 4.11 us -> 0.32 us
    ppermute x16, waiting for transfers between devices: 34.6 us -> 38 us  [column_shift(): return lax.ppermute(value, ('z', 'core'), pairs)]
    ppermute x8, starting transfers between devices: 9.57 us -> 12.7 us  [shift(): return lax.ppermute(value, axis, [(i, (i + by) % n) for i in range(n)])]
    ppermute x8, waiting for transfers between devices: 28.8 us -> 25.8 us  [shift(): return lax.ppermute(value, axis, [(i, (i + by) % n) for i in range(n)])]
    ppermute x13, waiting for transfers between devices: 9.26 us -> 11.9 us  [flip(): return lax.ppermute(value, axis, [(i, i ^ bit) for i in range(n)])]
  transfers between devices with their start and end apart: 39 -> 39, of which waited for: 21 -> 24; matrix products, arithmetic and copies ran while one was open for 11% -> 9% of each run, Pallas kernels for 0% -> 0%
where the time goes in v2:
time: 198 us; the launch traced here: 197 us
  waiting for transfers between devices  79.2 us (40%)
  starting transfers between devices  70.9 us (36%)
  matrix products  14.9 us (8%)
  other arithmetic  13.5 us (7%)
  local copies, waits for them, and re-layouts  8.84 us (4%)
  blocking collectives  8.45 us (4%)
    ppermute x16, waiting for transfers between devices, column_shift(): return lax.ppermute(value, ('z', 'core'), pairs)  38 us
    ppermute x16, starting transfers between devices, column_shift(): return lax.ppermute(value, ('z', 'core'), pairs)  37.2 us
    ppermute x8, waiting for transfers between devices, shift(): return lax.ppermute(value, axis, [(i, (i + by) % n) for i in range(n)])  25.8 us
    ppermute x8, starting transfers between devices, shift(): return lax.ppermute(value, axis, [(i, (i + by) % n) for i in range(n)])  12.7 us
    ppermute x13, waiting for transfers between devices, flip(): return lax.ppermute(value, axis, [(i, i ^ bit) for i in range(n)])  11.9 us
    all_gather x1, blocking collectives, per_device(): lax.all_gather(jnp.concatenate([image_grad_raw, text_grad_raw], axis=1),...  8.45 us
    ppermute x13, starting transfers between devices, flip(): return lax.ppermute(value, axis, [(i, i ^ bit) for i in range(n)])  7.19 us
    all_to_all x1, starting transfers between devices, per_device(): images = lax.all_to_all(spread, PLANE, 0, 0).reshape(-1, width)  7 us
  transfers between devices with their start and end apart: 39, of which 24 were waited for; matrix products, arithmetic and copies ran while one was open for 9% of the time, Pallas kernels for 0%

profile of v2, /device:TPU:32, one launch (start us, length us, event | category | flops | bytes accessed | tf_op | source)
XLA Modules:
  0.0 197.2 jit_solution(4584641895349688150)
XLA Ops:
  16.6 7.0 %all-to-all-start = ((bf16[16,48,1152]{2,1,0:T(8,128)(2,1)}), bf16[16,48,1152]{2,1,0:T(8,128)(2,1)S(1)}, u32[]{:S(2)}, u32[]{:S(2)}) async-start(bf16[16,48,1152]{2,1,0:T(8,128)(2,1)} %broadcast_in_dim.2), calls=%async_computation | async-start | bytes 3538944 | tf_op jit(solution)/shard_map/all_to_all | solution.py:182
  27.3 4.5 %collective-permute-start.6 = (bf16[96,1152]{1,0:T(8,128)(2,1)S(1)}, bf16[96,1152]{1,0:T(8,128)(2,1)S(1)}, u32[]{:S(2)}, u32[]{:S(2)}) collective-permute-start(bf16[96,1152]{1,0:T(8,128)(2,1)S(1)} %pad_maximum_fusion.8), channel_id=1, source_target_pairs={{0,32},{16,48},{32,64},{48,80},{64,96},{80,112},{96,0},{112,16},{1... | collective-permute-start | bytes 663560 | tf_op jit(solution)/shard_map/ppermute | solution.py:57
  35.1 11.9 %collective-permute-done.8 = bf16[48,1152]{1,0:T(8,128)(2,1)S(1)} collective-permute-done((bf16[48,1152]{1,0:T(8,128)(2,1)}, bf16[48,1152]{1,0:T(8,128)(2,1)S(1)}, u32[]{:S(2)}, u32[]{:S(2)}) %collective-permute-start.8) | collective-permute-done | bytes 110624 | tf_op jit(solution)/shard_map/ppermute | solution.py:57
  47.0 4.5 %collective-permute-done.7 = bf16[96,1152]{1,0:T(8,128)(2,1)S(1)} collective-permute-done((bf16[96,1152]{1,0:T(8,128)(2,1)S(1)}, bf16[96,1152]{1,0:T(8,128)(2,1)S(1)}, u32[]{:S(2)}, u32[]{:S(2)}) %collective-permute-start.7) | collective-permute-done | bytes 221216 | tf_op jit(solution)/shard_map/ppermute | solution.py:57
  55.4 3.7 %multiply_convert_fusion = bf16[768,768]{1,0:T(8,128)(2,1)S(1)} fusion(bf16[768,1152]{1,0:T(8,128)(2,1)S(1)} %bitcast.168, s32[768]{0:T(1024)S(1)} %fusion.32, pred[768]{0:T(1024)(128)(4,1)S(1)} %fusion.30, pred[768]{0:T(1024)(128)(4,1)} %fusion.31, bf16[336,1152]{1,0:T(8,128)(2,1)} %collective-permute-done.9, bf16[336,1152]{1,0:T(8,128)(2,1)} %pad_maximum_fusion.1, ...), kind=kOutput, calls=%fused_computation.3 | convolution fusion | flops 1373110272 | bytes 4723200 | tf_op jit(solution)/shard_map/dot_general | solution.py:186
  62.8 4.7 %convolution_convert_fusion = bf16[768,1152]{1,0:T(8,128)(2,1)} fusion(bf16[768,768]{1,0:T(8,128)(2,1)} %copy-done.14, bf16[336,1152]{1,0:T(8,128)(2,1)} %collective-permute-done.9, bf16[336,1152]{1,0:T(8,128)(2,1)} %pad_maximum_fusion.1, bf16[48,1152]{1,0:T(8,128)(2,1)} %copy-done.13, bf16[48,1152]{1,0:T(8,128)(2,1)} %copy-done.12), kind=kOutput, calls=%fused_computation.1 | convolution fusion | flops 1366917120 | bytes 4718592 | tf_op jit(solution)/shard_map/dot_general | solution.py:198
  68.4 6.9 %all-to-all-start.1 = ((bf16[16,48,1152]{2,1,0:T(8,128)(2,1)}), bf16[16,48,1152]{2,1,0:T(8,128)(2,1)S(1)}, u32[]{:S(2)}, u32[]{:S(2)}) async-start(bf16[16,48,1152]{2,1,0:T(8,128)(2,1)} %bitcast.170), calls=%async_computation.1 | async-start | bytes 3538944 | tf_op jit(solution)/shard_map/all_to_all | solution.py:200
  76.9 4.0 %collective-permute-start.11 = (bf16[96,1152]{1,0:T(8,128)(2,1)S(1)}, bf16[96,1152]{1,0:T(8,128)(2,1)S(1)}, u32[]{:S(2)}, u32[]{:S(2)}) collective-permute-start(bf16[96,1152]{1,0:T(8,128)(2,1)S(1)} %get-tuple-element.28), channel_id=1, source_target_pairs={{0,80},{16,96},{32,112},{48,0},{64,16},{80,32},{96,48},{112,64},{1... | collective-permute-start | bytes 663560 | tf_op jit(solution)/shard_map/ppermute | solution.py:57
  83.2 2.9 %collective-permute-start.14 = (bf16[48,1152]{1,0:T(8,128)(2,1)}, bf16[48,1152]{1,0:T(8,128)(2,1)}, u32[]{:S(2)}, u32[]{:S(2)}) collective-permute-start(bf16[48,1152]{1,0:T(8,128)(2,1)} %add_convert_fusion.3), channel_id=1, source_target_pairs={{0,64},{16,80},{32,96},{48,112},{64,0},{80,16},{96,32},{112,48},{1... | collective-permute-start | bytes 331784 | tf_op jit(solution)/shard_map/ppermute | solution.py:57
  86.1 5.5 %collective-permute-done.11 = bf16[96,1152]{1,0:T(8,128)(2,1)S(1)} collective-permute-done((bf16[96,1152]{1,0:T(8,128)(2,1)S(1)}, bf16[96,1152]{1,0:T(8,128)(2,1)S(1)}, u32[]{:S(2)}, u32[]{:S(2)}) %collective-permute-start.11) | collective-permute-done | bytes 221216 | tf_op jit(solution)/shard_map/ppermute | solution.py:57
  91.7 3.0 %collective-permute-done.12 = bf16[96,1152]{1,0:T(8,128)(2,1)S(1)} collective-permute-done((bf16[96,1152]{1,0:T(8,128)(2,1)S(1)}, bf16[96,1152]{1,0:T(8,128)(2,1)S(1)}, u32[]{:S(2)}, u32[]{:S(2)}) %collective-permute-start.12) | collective-permute-done | bytes 221216 | tf_op jit(solution)/shard_map/ppermute | solution.py:57
  94.6 2.9 %collective-permute-done.13 = bf16[96,1152]{1,0:T(8,128)(2,1)S(1)} collective-permute-done((bf16[96,1152]{1,0:T(8,128)(2,1)S(1)}, bf16[96,1152]{1,0:T(8,128)(2,1)S(1)}, u32[]{:S(2)}, u32[]{:S(2)}) %collective-permute-start.13) | collective-permute-done | bytes 221216 | tf_op jit(solution)/shard_map/ppermute | solution.py:57
  99.4 3.5 %all-to-all-done.1 = bf16[16,48,1152]{2,1,0:T(8,128)(2,1)S(1)} async-done(((bf16[16,48,1152]{2,1,0:T(8,128)(2,1)}), bf16[16,48,1152]{2,1,0:T(8,128)(2,1)S(1)}, u32[]{:S(2)}, u32[]{:S(2)}) %all-to-all-start.1) | async-done | bytes 1769504 | tf_op jit(solution)/shard_map/all_to_all | solution.py:200
  105.3 8.5 %all_gather.3 = bf16[192,2304]{1,0:T(8,128)(2,1)S(1)} all-gather(bf16[48,2304]{1,0:T(8,128)(2,1)S(1)} %pad_maximum_fusion.9), channel_id=1, replica_groups=mesh['yhi'=2,'z'=8,'x'=4,'ylo'=2,'core'=2] {'ylo','core'}, dimensions={0}, use_global_device_ids=true | all-gather | bytes 1105920 | tf_op jit(solution)/shard_map/all_gather | solution.py:206
  115.0 3.2 %collective-permute-start.18 = (bf16[2,32,1152]{2,1,0:T(8,128)(2,1)S(1)}, bf16[2,32,1152]{2,1,0:T(8,128)(2,1)S(1)}, u32[]{:S(2)}, u32[]{:S(2)}) collective-permute-start(bf16[2,32,1152]{2,1,0:T(8,128)(2,1)S(1)} %pad_maximum_fusion.10), channel_id=1, source_target_pairs={{0,12},{4,0},{8,4},{12,8},{1,13},{5,1},{9,5},{13,9},{2,14},{6,2},{... | collective-permute-start | bytes 442376 | tf_op jit(solution)/shard_map/ppermute | solution.py:20
  118.2 3.3 %collective-permute-done.18 = bf16[2,32,1152]{2,1,0:T(8,128)(2,1)S(1)} collective-permute-done((bf16[2,32,1152]{2,1,0:T(8,128)(2,1)S(1)}, bf16[2,32,1152]{2,1,0:T(8,128)(2,1)S(1)}, u32[]{:S(2)}, u32[]{:S(2)}) %collective-permute-start.18) | collective-permute-done | bytes 147488 | tf_op jit(solution)/shard_map/ppermute | solution.py:20
  121.6 3.8 %collective-permute-start.19 = (bf16[2,72,1152]{2,1,0:T(8,128)(2,1)S(1)}, bf16[2,72,1152]{2,1,0:T(8,128)(2,1)S(1)}, u32[]{:S(2)}, u32[]{:S(2)}) collective-permute-start(bf16[2,72,1152]{2,1,0:T(8,128)(2,1)S(1)} %pad_maximum_fusion.3), channel_id=1, source_target_pairs={{0,12},{4,0},{8,4},{12,8},{1,13},{5,1},{9,5},{13,9},{2,14},{6,2},{... | collective-permute-start | bytes 995336 | tf_op jit(solution)/shard_map/ppermute | solution.py:20
  125.7 6.2 %collective-permute-done.19 = bf16[2,72,1152]{2,1,0:T(8,128)(2,1)S(1)} collective-permute-done((bf16[2,72,1152]{2,1,0:T(8,128)(2,1)S(1)}, bf16[2,72,1152]{2,1,0:T(8,128)(2,1)S(1)}, u32[]{:S(2)}, u32[]{:S(2)}) %collective-permute-start.19) | collective-permute-done | bytes 331808 | tf_op jit(solution)/shard_map/ppermute | solution.py:20
  131.8 3.6 %collective-permute-done.17 = bf16[2,72,1152]{2,1,0:T(8,128)(2,1)S(1)} collective-permute-done((bf16[2,72,1152]{2,1,0:T(8,128)(2,1)S(1)}, bf16[2,72,1152]{2,1,0:T(8,128)(2,1)S(1)}, u32[]{:S(2)}, u32[]{:S(2)}) %collective-permute-start.17) | collective-permute-done | bytes 331808 | tf_op jit(solution)/shard_map/ppermute | solution.py:20
  137.1 2.6 %collective-permute-start.22 = (bf16[2,168,128]{2,1,0:T(8,128)(2,1)S(1)}, bf16[2,168,128]{2,1,0:T(8,128)(2,1)S(1)}, u32[]{:S(2)}, u32[]{:S(2)}) collective-permute-start(bf16[2,168,128]{2,1,0:T(8,128)(2,1)S(1)} %pad_maximum_fusion.13), channel_id=1, source_target_pairs={{0,16},{16,32},{32,48},{48,64},{64,80},{80,96},{96,112},{112,0},{1... | collective-permute-start | bytes 258056 | tf_op jit(solution)/shard_map/ppermute | solution.py:57
  139.7 2.4 %collective-permute-start.23 = (bf16[2,168,128]{2,1,0:T(8,128)(2,1)S(1)}, bf16[2,168,128]{2,1,0:T(8,128)(2,1)S(1)}, u32[]{:S(2)}, u32[]{:S(2)}) collective-permute-start(bf16[2,168,128]{2,1,0:T(8,128)(2,1)S(1)} %pad_maximum_fusion.14), channel_id=1, source_target_pairs={{0,32},{16,48},{32,64},{48,80},{64,96},{80,112},{96,0},{112,16},{1... | collective-permute-start | bytes 258056 | tf_op jit(solution)/shard_map/ppermute | solution.py:57
  143.2 4.9 %collective-permute-start.20 = (bf16[168,128]{1,0:T(8,128)(2,1)S(1)}, bf16[168,128]{1,0:T(8,128)(2,1)S(1)}, u32[]{:S(2)}, u32[]{:S(2)}) collective-permute-start(bf16[168,128]{1,0:T(8,128)(2,1)S(1)} %get-tuple-element.37), channel_id=1, source_target_pairs={{0,64},{16,80},{32,96},{48,112},{64,0},{80,16},{96,32},{112,48},{1... | collective-permute-start | bytes 129032 | tf_op jit(solution)/shard_map/ppermute | solution.py:57
  148.1 2.8 %collective-permute-done.24 = bf16[2,168,128]{2,1,0:T(8,128)(2,1)S(1)} collective-permute-done((bf16[2,168,128]{2,1,0:T(8,128)(2,1)S(1)}, bf16[2,168,128]{2,1,0:T(8,128)(2,1)S(1)}, u32[]{:S(2)}, u32[]{:S(2)}) %collective-permute-start.24) | collective-permute-done | bytes 86048 | tf_op jit(solution)/shard_map/ppermute | solution.py:57
  152.3 2.7 %collective-permute-start.26 = (bf16[168,128]{1,0:T(8,128)(2,1)S(1)}, bf16[168,128]{1,0:T(8,128)(2,1)S(1)}, u32[]{:S(2)}, u32[]{:S(2)}) collective-permute-start(bf16[168,128]{1,0:T(8,128)(2,1)S(1)} %fusion.27), channel_id=1, source_target_pairs={{0,128},{128,0},{1,129},{129,1},{2,130},{130,2},{3,131},{131,3},{4... | collective-permute-start | bytes 129032 | tf_op jit(solution)/shard_map/ppermute | solution.py:25
  154.9 2.9 %collective-permute-done.26 = bf16[168,128]{1,0:T(8,128)(2,1)S(1)} collective-permute-done((bf16[168,128]{1,0:T(8,128)(2,1)S(1)}, bf16[168,128]{1,0:T(8,128)(2,1)S(1)}, u32[]{:S(2)}, u32[]{:S(2)}) %collective-permute-start.26) | collective-permute-done | bytes 43040 | tf_op jit(solution)/shard_map/ppermute | solution.py:25
  158.0 4.1 %collective-permute-start.27 = (bf16[168,128]{1,0:T(8,128)(2,1)S(1)}, bf16[168,128]{1,0:T(8,128)(2,1)S(1)}, u32[]{:S(2)}, u32[]{:S(2)}) collective-permute-start(bf16[168,128]{1,0:T(8,128)(2,1)S(1)} %get-tuple-element.25), channel_id=1, source_target_pairs={{0,64},{16,80},{32,96},{48,112},{64,0},{80,16},{96,32},{112,48},{1... | collective-permute-start | bytes 129032 | tf_op jit(solution)/shard_map/ppermute | solution.py:57
  163.3 3.0 %collective-permute-start.30 = (bf16[2,168,128]{2,1,0:T(8,128)(2,1)S(1)}, bf16[2,168,128]{2,1,0:T(8,128)(2,1)S(1)}, u32[]{:S(2)}, u32[]{:S(2)}) collective-permute-start(bf16[2,168,128]{2,1,0:T(8,128)(2,1)S(1)} %pad_maximum_fusion.16), channel_id=1, source_target_pairs={{0,32},{16,48},{32,64},{48,80},{64,96},{80,112},{96,0},{112,16},{1... | collective-permute-start | bytes 258056 | tf_op jit(solution)/shard_map/ppermute | solution.py:57
  168.0 3.1 %collective-permute-done.30 = bf16[2,168,128]{2,1,0:T(8,128)(2,1)S(1)} collective-permute-done((bf16[2,168,128]{2,1,0:T(8,128)(2,1)S(1)}, bf16[2,168,128]{2,1,0:T(8,128)(2,1)S(1)}, u32[]{:S(2)}, u32[]{:S(2)}) %collective-permute-start.30) | collective-permute-done | bytes 86048 | tf_op jit(solution)/shard_map/ppermute | solution.py:57
  171.1 3.9 %collective-permute-done.31 = bf16[2,168,128]{2,1,0:T(8,128)(2,1)S(1)} collective-permute-done((bf16[2,168,128]{2,1,0:T(8,128)(2,1)S(1)}, bf16[2,168,128]{2,1,0:T(8,128)(2,1)S(1)}, u32[]{:S(2)}, u32[]{:S(2)}) %collective-permute-start.31) | collective-permute-done | bytes 86048 | tf_op jit(solution)/shard_map/ppermute | solution.py:57
  179.3 9.0 %collective-permute-done.34 = bf16[2,72,1152]{2,1,0:T(8,128)(2,1)S(1)} collective-permute-done((bf16[2,72,1152]{2,1,0:T(8,128)(2,1)S(1)}, bf16[2,72,1152]{2,1,0:T(8,128)(2,1)S(1)}, u32[]{:S(2)}, u32[]{:S(2)}) %collective-permute-start.34) | collective-permute-done | bytes 331808 | tf_op jit(solution)/shard_map/ppermute | solution.py:20
  188.8 2.9 %collective-permute-start.36 = (bf16[2,32,1152]{2,1,0:T(8,128)(2,1)S(1)}, bf16[2,32,1152]{2,1,0:T(8,128)(2,1)S(1)}, u32[]{:S(2)}, u32[]{:S(2)}) collective-permute-start(bf16[2,32,1152]{2,1,0:T(8,128)(2,1)S(1)} %slice.244), channel_id=1, source_target_pairs={{0,12},{4,0},{8,4},{12,8},{1,13},{5,1},{9,5},{13,9},{2,14},{6,2},{... | collective-permute-start | bytes 442376 | tf_op jit(solution)/shard_map/ppermute | solution.py:20
  191.7 2.6 %collective-permute-done.36 = bf16[2,32,1152]{2,1,0:T(8,128)(2,1)S(1)} collective-permute-done((bf16[2,32,1152]{2,1,0:T(8,128)(2,1)S(1)}, bf16[2,32,1152]{2,1,0:T(8,128)(2,1)S(1)}, u32[]{:S(2)}, u32[]{:S(2)}) %collective-permute-start.36) | collective-permute-done | bytes 147488 | tf_op jit(solution)/shard_map/ppermute | solution.py:20
  (172 shorter events, 55.5 us)
Async XLA Ops:
  6.6 5.2 %collective-permute-start.3 = (bf16[48,1152]{1,0:T(8,128)(2,1)S(1)}, bf16[48,1152]{1,0:T(8,128)(2,1)S(1)}, u32[]{:S(2)}, u32[]{:S(2)}) collective-permute-start(bf16[48,1152]{1,0:T(8,128)(2,1)S(1)} %fusion.25), channel_id=1, source_target_pairs={{0,2},{2,0},{1,3},{3,1},{4,6},{6,4},{5,7},{7,5},{8,10},{10,8},{9,1... | collective-permute-start | bytes 331784 | tf_op jit(solution)/shard_map/ppermute | solution.py:25
  9.3 4.9 %collective-permute-start.1 = (bf16[48,1152]{1,0:T(8,128)(2,1)S(1)}, bf16[48,1152]{1,0:T(8,128)(2,1)S(1)}, u32[]{:S(2)}, u32[]{:S(2)}) collective-permute-start(bf16[48,1152]{1,0:T(8,128)(2,1)S(1)} %fusion.24), channel_id=1, source_target_pairs={{0,2},{2,0},{1,3},{3,1},{4,6},{6,4},{5,7},{7,5},{8,10},{10,8},{9,1... | collective-permute-start | bytes 331784 | tf_op jit(solution)/shard_map/ppermute | solution.py:25
  16.6 7.0 %collective-permute-start.4 = (bf16[48,1152]{1,0:T(8,128)(2,1)}, bf16[48,1152]{1,0:T(8,128)(2,1)}, u32[]{:S(2)}, u32[]{:S(2)}) collective-permute-start(bf16[48,1152]{1,0:T(8,128)(2,1)} %fusion.35), channel_id=1, source_target_pairs={{0,1},{1,0},{2,3},{3,2},{4,5},{5,4},{6,7},{7,6},{8,9},{9,8},{10,11... | collective-permute-start | bytes 331784 | tf_op jit(solution)/shard_map/ppermute | solution.py:25
  16.6 38.9 %all-to-all-start = ((bf16[16,48,1152]{2,1,0:T(8,128)(2,1)}), bf16[16,48,1152]{2,1,0:T(8,128)(2,1)S(1)}, u32[]{:S(2)}, u32[]{:S(2)}) async-start(bf16[16,48,1152]{2,1,0:T(8,128)(2,1)} %broadcast_in_dim.2), calls=%async_computation | async-start | bytes 3538944 | tf_op jit(solution)/shard_map/all_to_all | solution.py:182
  25.3 21.8 %collective-permute-start.5 = (bf16[96,1152]{1,0:T(8,128)(2,1)S(1)}, bf16[96,1152]{1,0:T(8,128)(2,1)S(1)}, u32[]{:S(2)}, u32[]{:S(2)}) collective-permute-start(bf16[96,1152]{1,0:T(8,128)(2,1)S(1)} %pad_maximum_fusion.8), channel_id=1, source_target_pairs={{0,16},{16,32},{32,48},{48,64},{64,80},{80,96},{96,112},{112,0},{1... | collective-permute-start | bytes 663560 | tf_op jit(solution)/shard_map/ppermute | solution.py:57
  27.3 19.8 %collective-permute-start.6 = (bf16[96,1152]{1,0:T(8,128)(2,1)S(1)}, bf16[96,1152]{1,0:T(8,128)(2,1)S(1)}, u32[]{:S(2)}, u32[]{:S(2)}) collective-permute-start(bf16[96,1152]{1,0:T(8,128)(2,1)S(1)} %pad_maximum_fusion.8), channel_id=1, source_target_pairs={{0,32},{16,48},{32,64},{48,80},{64,96},{80,112},{96,0},{112,16},{1... | collective-permute-start | bytes 663560 | tf_op jit(solution)/shard_map/ppermute | solution.py:57
  31.7 19.8 %collective-permute-start.7 = (bf16[96,1152]{1,0:T(8,128)(2,1)S(1)}, bf16[96,1152]{1,0:T(8,128)(2,1)S(1)}, u32[]{:S(2)}, u32[]{:S(2)}) collective-permute-start(bf16[96,1152]{1,0:T(8,128)(2,1)S(1)} %pad_maximum_fusion.8), channel_id=1, source_target_pairs={{0,48},{16,64},{32,80},{48,96},{64,112},{80,0},{96,16},{112,32},{1... | collective-permute-start | bytes 663560 | tf_op jit(solution)/shard_map/ppermute | solution.py:57
  33.7 13.4 %collective-permute-start.8 = (bf16[48,1152]{1,0:T(8,128)(2,1)}, bf16[48,1152]{1,0:T(8,128)(2,1)S(1)}, u32[]{:S(2)}, u32[]{:S(2)}) collective-permute-start(bf16[48,1152]{1,0:T(8,128)(2,1)} %fusion.35), channel_id=1, source_target_pairs={{0,64},{16,80},{32,96},{48,112},{64,0},{80,16},{96,32},{112,48},{1... | collective-permute-start | bytes 331784 | tf_op jit(solution)/shard_map/ppermute | solution.py:57
  62.2 5.3 %collective-permute-start.10 = (bf16[336,1152]{1,0:T(8,128)(2,1)S(1)}, bf16[336,1152]{1,0:T(8,128)(2,1)S(1)}, u32[]{:S(2)}, u32[]{:S(2)}) collective-permute-start(bf16[336,1152]{1,0:T(8,128)(2,1)S(1)} %slice.216), channel_id=1, source_target_pairs={{0,1},{1,0},{2,3},{3,2},{4,5},{5,4},{6,7},{7,6},{8,9},{9,8},{10,11... | collective-permute-start | bytes 2322440 | tf_op jit(solution)/shard_map/ppermute | solution.py:25
  68.4 34.5 %all-to-all-start.1 = ((bf16[16,48,1152]{2,1,0:T(8,128)(2,1)}), bf16[16,48,1152]{2,1,0:T(8,128)(2,1)S(1)}, u32[]{:S(2)}, u32[]{:S(2)}) async-start(bf16[16,48,1152]{2,1,0:T(8,128)(2,1)} %bitcast.170), calls=%async_computation.1 | async-start | bytes 3538944 | tf_op jit(solution)/shard_map/all_to_all | solution.py:200
  76.9 14.7 %collective-permute-start.11 = (bf16[96,1152]{1,0:T(8,128)(2,1)S(1)}, bf16[96,1152]{1,0:T(8,128)(2,1)S(1)}, u32[]{:S(2)}, u32[]{:S(2)}) collective-permute-start(bf16[96,1152]{1,0:T(8,128)(2,1)S(1)} %get-tuple-element.28), channel_id=1, source_target_pairs={{0,80},{16,96},{32,112},{48,0},{64,16},{80,32},{96,48},{112,64},{1... | collective-permute-start | bytes 663560 | tf_op jit(solution)/shard_map/ppermute | solution.py:57
  80.9 13.7 %collective-permute-start.12 = (bf16[96,1152]{1,0:T(8,128)(2,1)S(1)}, bf16[96,1152]{1,0:T(8,128)(2,1)S(1)}, u32[]{:S(2)}, u32[]{:S(2)}) collective-permute-start(bf16[96,1152]{1,0:T(8,128)(2,1)S(1)} %get-tuple-element.30), channel_id=1, source_target_pairs={{0,96},{16,112},{32,0},{48,16},{64,32},{80,48},{96,64},{112,80},{1... | collective-permute-start | bytes 663560 | tf_op jit(solution)/shard_map/ppermute | solution.py:57
  80.9 16.6 %collective-permute-start.13 = (bf16[96,1152]{1,0:T(8,128)(2,1)S(1)}, bf16[96,1152]{1,0:T(8,128)(2,1)S(1)}, u32[]{:S(2)}, u32[]{:S(2)}) collective-permute-start(bf16[96,1152]{1,0:T(8,128)(2,1)S(1)} %get-tuple-element.29), channel_id=1, source_target_pairs={{0,112},{16,0},{32,16},{48,32},{64,48},{80,64},{96,80},{112,96},{1... | collective-permute-start | bytes 663560 | tf_op jit(solution)/shard_map/ppermute | solution.py:57
  83.2 20.1 %collective-permute-start.14 = (bf16[48,1152]{1,0:T(8,128)(2,1)}, bf16[48,1152]{1,0:T(8,128)(2,1)}, u32[]{:S(2)}, u32[]{:S(2)}) collective-permute-start(bf16[48,1152]{1,0:T(8,128)(2,1)} %add_convert_fusion.3), channel_id=1, source_target_pairs={{0,64},{16,80},{32,96},{48,112},{64,0},{80,16},{96,32},{112,48},{1... | collective-permute-start | bytes 331784 | tf_op jit(solution)/shard_map/ppermute | solution.py:57
  114.9 10.5 %collective-permute-start.16 = (bf16[2,40,1152]{2,1,0:T(8,128)(2,1)S(1)}, bf16[2,40,1152]{2,1,0:T(8,128)(2,1)S(1)}, u32[]{:S(2)}, u32[]{:S(2)}) collective-permute-start(bf16[2,40,1152]{2,1,0:T(8,128)(2,1)S(1)} %fusion.19), channel_id=1, source_target_pairs={{0,4},{4,8},{8,12},{12,0},{1,5},{5,9},{9,13},{13,1},{2,6},{6,10},{... | collective-permute-start | bytes 552968 | tf_op jit(solution)/shard_map/ppermute | solution.py:20
  115.0 6.6 %collective-permute-start.18 = (bf16[2,32,1152]{2,1,0:T(8,128)(2,1)S(1)}, bf16[2,32,1152]{2,1,0:T(8,128)(2,1)S(1)}, u32[]{:S(2)}, u32[]{:S(2)}) collective-permute-start(bf16[2,32,1152]{2,1,0:T(8,128)(2,1)S(1)} %pad_maximum_fusion.10), channel_id=1, source_target_pairs={{0,12},{4,0},{8,4},{12,8},{1,13},{5,1},{9,5},{13,9},{2,14},{6,2},{... | collective-permute-start | bytes 442376 | tf_op jit(solution)/shard_map/ppermute | solution.py:20
  121.6 10.2 %collective-permute-start.19 = (bf16[2,72,1152]{2,1,0:T(8,128)(2,1)S(1)}, bf16[2,72,1152]{2,1,0:T(8,128)(2,1)S(1)}, u32[]{:S(2)}, u32[]{:S(2)}) collective-permute-start(bf16[2,72,1152]{2,1,0:T(8,128)(2,1)S(1)} %pad_maximum_fusion.3), channel_id=1, source_target_pairs={{0,12},{4,0},{8,4},{12,8},{1,13},{5,1},{9,5},{13,9},{2,14},{6,2},{... | collective-permute-start | bytes 995336 | tf_op jit(solution)/shard_map/ppermute | solution.py:20
  125.5 9.9 %collective-permute-start.17 = (bf16[2,72,1152]{2,1,0:T(8,128)(2,1)S(1)}, bf16[2,72,1152]{2,1,0:T(8,128)(2,1)S(1)}, u32[]{:S(2)}, u32[]{:S(2)}) collective-permute-start(bf16[2,72,1152]{2,1,0:T(8,128)(2,1)S(1)} %pad_maximum_fusion.2), channel_id=1, source_target_pairs={{0,4},{4,8},{8,12},{12,0},{1,5},{5,9},{9,13},{13,1},{2,6},{6,10},{... | collective-permute-start | bytes 995336 | tf_op jit(solution)/shard_map/ppermute | solution.py:20
  137.1 10.9 %collective-permute-start.22 = (bf16[2,168,128]{2,1,0:T(8,128)(2,1)S(1)}, bf16[2,168,128]{2,1,0:T(8,128)(2,1)S(1)}, u32[]{:S(2)}, u32[]{:S(2)}) collective-permute-start(bf16[2,168,128]{2,1,0:T(8,128)(2,1)S(1)} %pad_maximum_fusion.13), channel_id=1, source_target_pairs={{0,16},{16,32},{32,48},{48,64},{64,80},{80,96},{96,112},{112,0},{1... | collective-permute-start | bytes 258056 | tf_op jit(solution)/shard_map/ppermute | solution.py:57
  139.7 8.4 %collective-permute-start.23 = (bf16[2,168,128]{2,1,0:T(8,128)(2,1)S(1)}, bf16[2,168,128]{2,1,0:T(8,128)(2,1)S(1)}, u32[]{:S(2)}, u32[]{:S(2)}) collective-permute-start(bf16[2,168,128]{2,1,0:T(8,128)(2,1)S(1)} %pad_maximum_fusion.14), channel_id=1, source_target_pairs={{0,32},{16,48},{32,64},{48,80},{64,96},{80,112},{96,0},{112,16},{1... | collective-permute-start | bytes 258056 | tf_op jit(solution)/shard_map/ppermute | solution.py:57
  142.2 8.7 %collective-permute-start.24 = (bf16[2,168,128]{2,1,0:T(8,128)(2,1)S(1)}, bf16[2,168,128]{2,1,0:T(8,128)(2,1)S(1)}, u32[]{:S(2)}, u32[]{:S(2)}) collective-permute-start(bf16[2,168,128]{2,1,0:T(8,128)(2,1)S(1)} %pad_maximum_fusion.15), channel_id=1, source_target_pairs={{0,48},{16,64},{32,80},{48,96},{64,112},{80,0},{96,16},{112,32},{1... | collective-permute-start | bytes 258056 | tf_op jit(solution)/shard_map/ppermute | solution.py:57
  143.2 8.3 %collective-permute-start.20 = (bf16[168,128]{1,0:T(8,128)(2,1)S(1)}, bf16[168,128]{1,0:T(8,128)(2,1)S(1)}, u32[]{:S(2)}, u32[]{:S(2)}) collective-permute-start(bf16[168,128]{1,0:T(8,128)(2,1)S(1)} %get-tuple-element.37), channel_id=1, source_target_pairs={{0,64},{16,80},{32,96},{48,112},{64,0},{80,16},{96,32},{112,48},{1... | collective-permute-start | bytes 129032 | tf_op jit(solution)/shard_map/ppermute | solution.py:57
  152.3 5.6 %collective-permute-start.26 = (bf16[168,128]{1,0:T(8,128)(2,1)S(1)}, bf16[168,128]{1,0:T(8,128)(2,1)S(1)}, u32[]{:S(2)}, u32[]{:S(2)}) collective-permute-start(bf16[168,128]{1,0:T(8,128)(2,1)S(1)} %fusion.27), channel_id=1, source_target_pairs={{0,128},{128,0},{1,129},{129,1},{2,130},{130,2},{3,131},{131,3},{4... | collective-permute-start | bytes 129032 | tf_op jit(solution)/shard_map/ppermute | solution.py:25
  157.9 4.2 %collective-permute-start.28 = (bf16[168,128]{1,0:T(8,128)(2,1)S(1)}, bf16[168,128]{1,0:T(8,128)(2,1)S(1)}, u32[]{:S(2)}, u32[]{:S(2)}) collective-permute-start(bf16[168,128]{1,0:T(8,128)(2,1)S(1)} %get-tuple-element.25), channel_id=1, source_target_pairs={{0,1},{1,0},{2,3},{3,2},{4,5},{5,4},{6,7},{7,6},{8,9},{9,8},{10,11... | collective-permute-start | bytes 129032 | tf_op jit(solution)/shard_map/ppermute | solution.py:25
  158.0 10.0 %collective-permute-start.27 = (bf16[168,128]{1,0:T(8,128)(2,1)S(1)}, bf16[168,128]{1,0:T(8,128)(2,1)S(1)}, u32[]{:S(2)}, u32[]{:S(2)}) collective-permute-start(bf16[168,128]{1,0:T(8,128)(2,1)S(1)} %get-tuple-element.25), channel_id=1, source_target_pairs={{0,64},{16,80},{32,96},{48,112},{64,0},{80,16},{96,32},{112,48},{1... | collective-permute-start | bytes 129032 | tf_op jit(solution)/shard_map/ppermute | solution.py:57
  162.1 5.9 %collective-permute-start.29 = (bf16[2,168,128]{2,1,0:T(8,128)(2,1)S(1)}, bf16[2,168,128]{2,1,0:T(8,128)(2,1)S(1)}, u32[]{:S(2)}, u32[]{:S(2)}) collective-permute-start(bf16[2,168,128]{2,1,0:T(8,128)(2,1)S(1)} %pad_maximum_fusion.16), channel_id=1, source_target_pairs={{0,16},{16,32},{32,48},{48,64},{64,80},{80,96},{96,112},{112,0},{1... | collective-permute-start | bytes 258056 | tf_op jit(solution)/shard_map/ppermute | solution.py:57
  163.3 7.8 %collective-permute-start.30 = (bf16[2,168,128]{2,1,0:T(8,128)(2,1)S(1)}, bf16[2,168,128]{2,1,0:T(8,128)(2,1)S(1)}, u32[]{:S(2)}, u32[]{:S(2)}) collective-permute-start(bf16[2,168,128]{2,1,0:T(8,128)(2,1)S(1)} %pad_maximum_fusion.16), channel_id=1, source_target_pairs={{0,32},{16,48},{32,64},{48,80},{64,96},{80,112},{96,0},{112,16},{1... | collective-permute-start | bytes 258056 | tf_op jit(solution)/shard_map/ppermute | solution.py:57
  166.2 8.7 %collective-permute-start.31 = (bf16[2,168,128]{2,1,0:T(8,128)(2,1)S(1)}, bf16[2,168,128]{2,1,0:T(8,128)(2,1)S(1)}, u32[]{:S(2)}, u32[]{:S(2)}) collective-permute-start(bf16[2,168,128]{2,1,0:T(8,128)(2,1)S(1)} %pad_maximum_fusion.16), channel_id=1, source_target_pairs={{0,48},{16,64},{32,80},{48,96},{64,112},{80,0},{96,16},{112,32},{1... | collective-permute-start | bytes 258056 | tf_op jit(solution)/shard_map/ppermute | solution.py:57
  176.9 11.9 %collective-permute-start.33 = (bf16[2,72,1152]{2,1,0:T(8,128)(2,1)S(1)}, bf16[2,72,1152]{2,1,0:T(8,128)(2,1)S(1)}, u32[]{:S(2)}, u32[]{:S(2)}) collective-permute-start(bf16[2,72,1152]{2,1,0:T(8,128)(2,1)S(1)} %bitcast.174), channel_id=1, source_target_pairs={{0,12},{4,0},{8,4},{12,8},{1,13},{5,1},{9,5},{13,9},{2,14},{6,2},{... | collective-permute-start | bytes 995336 | tf_op jit(solution)/shard_map/ppermute | solution.py:20
  177.1 11.2 %collective-permute-start.34 = (bf16[2,72,1152]{2,1,0:T(8,128)(2,1)S(1)}, bf16[2,72,1152]{2,1,0:T(8,128)(2,1)S(1)}, u32[]{:S(2)}, u32[]{:S(2)}) collective-permute-start(bf16[2,72,1152]{2,1,0:T(8,128)(2,1)S(1)} %bitcast.175), channel_id=1, source_target_pairs={{0,4},{4,8},{8,12},{12,0},{1,5},{5,9},{9,13},{13,1},{2,6},{6,10},{... | collective-permute-start | bytes 995336 | tf_op jit(solution)/shard_map/ppermute | solution.py:20
  188.3 7.3 %collective-permute-start.35 = (bf16[2,40,1152]{2,1,0:T(8,128)(2,1)S(1)}, bf16[2,40,1152]{2,1,0:T(8,128)(2,1)S(1)}, u32[]{:S(2)}, u32[]{:S(2)}) collective-permute-start(bf16[2,40,1152]{2,1,0:T(8,128)(2,1)S(1)} %slice.242), channel_id=1, source_target_pairs={{0,4},{4,8},{8,12},{12,0},{1,5},{5,9},{9,13},{13,1},{2,6},{6,10},{... | collective-permute-start | bytes 552968 | tf_op jit(solution)/shard_map/ppermute | solution.py:20
  188.8 5.5 %collective-permute-start.36 = (bf16[2,32,1152]{2,1,0:T(8,128)(2,1)S(1)}, bf16[2,32,1152]{2,1,0:T(8,128)(2,1)S(1)}, u32[]{:S(2)}, u32[]{:S(2)}) collective-permute-start(bf16[2,32,1152]{2,1,0:T(8,128)(2,1)S(1)} %slice.244), channel_id=1, source_target_pairs={{0,12},{4,0},{8,4},{12,8},{1,13},{5,1},{9,5},{13,9},{2,14},{6,2},{... | collective-permute-start | bytes 442376 | tf_op jit(solution)/shard_map/ppermute | solution.py:20
  (22 other events, 92.6 us)

commit v3 on v2

--- a/solution.py
+++ b/solution.py
@@ -61,8 +61,9 @@
     first = lax.axis_index("core") == 0
     other = flip(value, "core", 1)
     pair = jnp.concatenate([jnp.where(first, value, other), jnp.where(first, other, value)], axis=0)
-    far = column_shift(value, 4)
+    rows = value.shape[0]
     got = {k: column_shift(pair, k) for k in (3, 2, 1)}
+    far = column_shift(jnp.where(first, got[3][:rows], got[3][rows:]), 1)
     mine = lax.optimization_barrier(jnp.concatenate([got[1], got[2], got[3], far], axis=0))
     return jnp.concatenate([pair, mine, flip(mine, "core", 1)], axis=0)
 

time: 198 us -> 196 us (0.990)
  starting transfers between devices: 70.9 us -> 63.4 us
  waiting for transfers between devices: 79.2 us -> 84.4 us
    all_to_all x1, waiting for transfers between devices: 0.01 us -> 10.6 us  [per_device(): images = lax.all_to_all(spread, PLANE, 0, 0).reshape(-1, width)]
    ppermute x16, waiting for transfers between devices: 38 us -> 29.9 us  [column_shift(): return lax.ppermute(value, ('z', 'core'), pairs)]
    all_to_all x1, starting transfers between devices: 6.93 us -> 3.71 us  [per_device(): lax.all_to_all(image_part.reshape(plane, quarter, width), PLANE, 0, 0)]
    ppermute x16, starting transfers between devices: 37.2 us -> 33.9 us  [column_shift(): return lax.ppermute(value, ('z', 'core'), pairs)]
    ppermute x13, waiting for transfers between devices: 11.9 us -> 14 us  [flip(): return lax.ppermute(value, axis, [(i, i ^ bit) for i in range(n)])]
  transfers between devices with their start and end apart: 39 -> 39, of which waited for: 24 -> 27; matrix products, arithmetic and copies ran while one was open for 9% -> 10% of each run, Pallas kernels for 0% -> 0%
where the time goes in v3:
time: 196 us
  waiting for transfers between devices  84.4 us (43%)
  starting transfers between devices  63.4 us (32%)
  matrix products  14.9 us (8%)
  other arithmetic  14.5 us (7%)
  local copies, waits for them, and re-layouts  8.82 us (4%)
  blocking collectives  8.15 us (4%)
    ppermute x16, starting transfers between devices, column_shift(): return lax.ppermute(value, ('z', 'core'), pairs)  33.9 us
    ppermute x16, waiting for transfers between devices, column_shift(): return lax.ppermute(value, ('z', 'core'), pairs)  29.9 us
    ppermute x8, waiting for transfers between devices, shift(): return lax.ppermute(value, axis, [(i, (i + by) % n) for i in range(n)])  25.8 us
    ppermute x13, waiting for transfers between devices, flip(): return lax.ppermute(value, axis, [(i, i ^ bit) for i in range(n)])  14 us
    ppermute x8, starting transfers between devices, shift(): return lax.ppermute(value, axis, [(i, (i + by) % n) for i in range(n)])  12.7 us
    all_to_all x1, waiting for transfers between devices, per_device(): images = lax.all_to_all(spread, PLANE, 0, 0).reshape(-1, width)  10.6 us
    all_gather x1, blocking collectives, per_device(): lax.all_gather(jnp.concatenate([image_grad_raw, text_grad_raw], axis=1),...  8.15 us
    all_to_all x1, starting transfers between devices, per_device(): images = lax.all_to_all(spread, PLANE, 0, 0).reshape(-1, width)  7 us
  transfers between devices with their start and end apart: 39, of which 27 were waited for; matrix products, arithmetic and copies ran while one was open for 10% of the time, Pallas kernels for 0%

profile of v3, /device:TPU:32, one launch (start us, length us, event | category | flops | bytes accessed | tf_op | source)
XLA Modules:
  0.0 195.6 jit_solution(8802024856965890540)
XLA Ops:
  11.9 2.3 %collective-permute-done.1 = bf16[48,1152]{1,0:T(8,128)(2,1)S(1)} collective-permute-done((bf16[48,1152]{1,0:T(8,128)(2,1)S(1)}, bf16[48,1152]{1,0:T(8,128)(2,1)S(1)}, u32[]{:S(2)}, u32[]{:S(2)}) %collective-permute-start.1) | collective-permute-done | bytes 110624 | tf_op jit(solution)/shard_map/ppermute | solution.py:25
  18.6 5.8 %collective-permute-start.7 = (bf16[96,1152]{1,0:T(8,128)(2,1)}, bf16[96,1152]{1,0:T(8,128)(2,1)}, u32[]{:S(2)}, u32[]{:S(2)}) collective-permute-start(bf16[96,1152]{1,0:T(8,128)(2,1)} %pad_maximum_fusion.8), channel_id=1, source_target_pairs={{0,48},{16,64},{32,80},{48,96},{64,112},{80,0},{96,16},{112,32},{1... | collective-permute-start | bytes 663560 | tf_op jit(solution)/shard_map/ppermute | solution.py:57
  24.5 7.0 %all-to-all-start = ((bf16[16,48,1152]{2,1,0:T(8,128)(2,1)}), bf16[16,48,1152]{2,1,0:T(8,128)(2,1)S(1)}, u32[]{:S(2)}, u32[]{:S(2)}) async-start(bf16[16,48,1152]{2,1,0:T(8,128)(2,1)} %broadcast_in_dim.2), calls=%async_computation | async-start | bytes 3538944 | tf_op jit(solution)/shard_map/all_to_all | solution.py:183
  35.6 2.1 %collective-permute-done.5 = bf16[96,1152]{1,0:T(8,128)(2,1)S(1)} collective-permute-done((bf16[96,1152]{1,0:T(8,128)(2,1)}, bf16[96,1152]{1,0:T(8,128)(2,1)S(1)}, u32[]{:S(2)}, u32[]{:S(2)}) %collective-permute-start.5) | collective-permute-done | bytes 221216 | tf_op jit(solution)/shard_map/ppermute | solution.py:57
  37.7 5.6 %collective-permute-done.6 = bf16[96,1152]{1,0:T(8,128)(2,1)S(1)} collective-permute-done((bf16[96,1152]{1,0:T(8,128)(2,1)}, bf16[96,1152]{1,0:T(8,128)(2,1)S(1)}, u32[]{:S(2)}, u32[]{:S(2)}) %collective-permute-start.6) | collective-permute-done | bytes 221216 | tf_op jit(solution)/shard_map/ppermute | solution.py:57
  46.1 2.0 %collective-permute-done.9 = bf16[336,1152]{1,0:T(8,128)(2,1)} collective-permute-done((bf16[336,1152]{1,0:T(8,128)(2,1)}, bf16[336,1152]{1,0:T(8,128)(2,1)}, u32[]{:S(2)}, u32[]{:S(2)}) %collective-permute-start.9) | collective-permute-done | bytes 774176 | tf_op jit(solution)/shard_map/ppermute | solution.py:25
  48.1 10.6 %all-to-all-done = bf16[16,48,1152]{2,1,0:T(8,128)(2,1)S(1)} async-done(((bf16[16,48,1152]{2,1,0:T(8,128)(2,1)}), bf16[16,48,1152]{2,1,0:T(8,128)(2,1)S(1)}, u32[]{:S(2)}, u32[]{:S(2)}) %all-to-all-start) | async-done | bytes 1769504 | tf_op jit(solution)/shard_map/all_to_all | solution.py:183
  58.7 3.7 %multiply_convert_fusion = bf16[768,768]{1,0:T(8,128)(2,1)S(1)} fusion(bf16[768,1152]{1,0:T(8,128)(2,1)S(1)} %bitcast.168, s32[768]{0:T(1024)S(1)} %fusion.32, pred[768]{0:T(1024)(128)(4,1)S(1)} %fusion.30, pred[768]{0:T(1024)(128)(4,1)} %fusion.31, bf16[336,1152]{1,0:T(8,128)(2,1)} %collective-permute-done.9, bf16[336,1152]{1,0:T(8,128)(2,1)} %pad_maximum_fusion.1, ...), kind=kOutput, calls=%fused_computation.3 | convolution fusion | flops 1373110272 | bytes 4723200 | tf_op jit(solution)/shard_map/dot_general | solution.py:187
  65.8 4.7 %convolution_convert_fusion = bf16[768,1152]{1,0:T(8,128)(2,1)} fusion(bf16[768,768]{1,0:T(8,128)(2,1)} %copy-done.14, bf16[336,1152]{1,0:T(8,128)(2,1)} %collective-permute-done.9, bf16[336,1152]{1,0:T(8,128)(2,1)} %pad_maximum_fusion.1, bf16[48,1152]{1,0:T(8,128)(2,1)} %copy-done.13, bf16[48,1152]{1,0:T(8,128)(2,1)} %copy-done.12), kind=kOutput, calls=%fused_computation.1 | convolution fusion | flops 1366917120 | bytes 4718592 | tf_op jit(solution)/shard_map/dot_general | solution.py:199
  71.4 3.7 %all-to-all-start.1 = ((bf16[16,48,1152]{2,1,0:T(8,128)(2,1)}), bf16[16,48,1152]{2,1,0:T(8,128)(2,1)S(1)}, u32[]{:S(2)}, u32[]{:S(2)}) async-start(bf16[16,48,1152]{2,1,0:T(8,128)(2,1)} %bitcast.170), calls=%async_computation.1 | async-start | bytes 3538944 | tf_op jit(solution)/shard_map/all_to_all | solution.py:201
  80.2 5.6 %collective-permute-start.14 = (bf16[48,1152]{1,0:T(8,128)(2,1)}, bf16[48,1152]{1,0:T(8,128)(2,1)}, u32[]{:S(2)}, u32[]{:S(2)}) collective-permute-start(bf16[48,1152]{1,0:T(8,128)(2,1)} %add_convert_fusion.3), channel_id=1, source_target_pairs={{0,64},{16,80},{32,96},{48,112},{64,0},{80,16},{96,32},{112,48},{1... | collective-permute-start | bytes 331784 | tf_op jit(solution)/shard_map/ppermute | solution.py:57
  85.8 4.9 %collective-permute-done.11 = bf16[96,1152]{1,0:T(8,128)(2,1)S(1)} collective-permute-done((bf16[96,1152]{1,0:T(8,128)(2,1)S(1)}, bf16[96,1152]{1,0:T(8,128)(2,1)S(1)}, u32[]{:S(2)}, u32[]{:S(2)}) %collective-permute-start.11) | collective-permute-done | bytes 221216 | tf_op jit(solution)/shard_map/ppermute | solution.py:57
  90.7 2.5 %collective-permute-done.12 = bf16[96,1152]{1,0:T(8,128)(2,1)S(1)} collective-permute-done((bf16[96,1152]{1,0:T(8,128)(2,1)S(1)}, bf16[96,1152]{1,0:T(8,128)(2,1)S(1)}, u32[]{:S(2)}, u32[]{:S(2)}) %collective-permute-start.12) | collective-permute-done | bytes 221216 | tf_op jit(solution)/shard_map/ppermute | solution.py:57
  93.2 4.2 %collective-permute-done.13 = bf16[96,1152]{1,0:T(8,128)(2,1)S(1)} collective-permute-done((bf16[96,1152]{1,0:T(8,128)(2,1)S(1)}, bf16[96,1152]{1,0:T(8,128)(2,1)S(1)}, u32[]{:S(2)}, u32[]{:S(2)}) %collective-permute-start.13) | collective-permute-done | bytes 221216 | tf_op jit(solution)/shard_map/ppermute | solution.py:57
  99.2 4.1 %all-to-all-done.1 = bf16[16,48,1152]{2,1,0:T(8,128)(2,1)S(1)} async-done(((bf16[16,48,1152]{2,1,0:T(8,128)(2,1)}), bf16[16,48,1152]{2,1,0:T(8,128)(2,1)S(1)}, u32[]{:S(2)}, u32[]{:S(2)}) %all-to-all-start.1) | async-done | bytes 1769504 | tf_op jit(solution)/shard_map/all_to_all | solution.py:201
  105.7 8.1 %all_gather.3 = bf16[192,2304]{1,0:T(8,128)(2,1)S(1)} all-gather(bf16[48,2304]{1,0:T(8,128)(2,1)S(1)} %pad_maximum_fusion.9), channel_id=1, replica_groups=mesh['yhi'=2,'z'=8,'x'=4,'ylo'=2,'core'=2] {'ylo','core'}, dimensions={0}, use_global_device_ids=true | all-gather | bytes 1105920 | tf_op jit(solution)/shard_map/all_gather | solution.py:207
  115.1 3.2 %collective-permute-start.18 = (bf16[2,32,1152]{2,1,0:T(8,128)(2,1)S(1)}, bf16[2,32,1152]{2,1,0:T(8,128)(2,1)S(1)}, u32[]{:S(2)}, u32[]{:S(2)}) collective-permute-start(bf16[2,32,1152]{2,1,0:T(8,128)(2,1)S(1)} %pad_maximum_fusion.10), channel_id=1, source_target_pairs={{0,12},{4,0},{8,4},{12,8},{1,13},{5,1},{9,5},{13,9},{2,14},{6,2},{... | collective-permute-start | bytes 442376 | tf_op jit(solution)/shard_map/ppermute | solution.py:20
  118.4 3.3 %collective-permute-done.18 = bf16[2,32,1152]{2,1,0:T(8,128)(2,1)S(1)} collective-permute-done((bf16[2,32,1152]{2,1,0:T(8,128)(2,1)S(1)}, bf16[2,32,1152]{2,1,0:T(8,128)(2,1)S(1)}, u32[]{:S(2)}, u32[]{:S(2)}) %collective-permute-start.18) | collective-permute-done | bytes 147488 | tf_op jit(solution)/shard_map/ppermute | solution.py:20
  121.8 3.8 %collective-permute-start.19 = (bf16[2,72,1152]{2,1,0:T(8,128)(2,1)S(1)}, bf16[2,72,1152]{2,1,0:T(8,128)(2,1)S(1)}, u32[]{:S(2)}, u32[]{:S(2)}) collective-permute-start(bf16[2,72,1152]{2,1,0:T(8,128)(2,1)S(1)} %pad_maximum_fusion.3), channel_id=1, source_target_pairs={{0,12},{4,0},{8,4},{12,8},{1,13},{5,1},{9,5},{13,9},{2,14},{6,2},{... | collective-permute-start | bytes 995336 | tf_op jit(solution)/shard_map/ppermute | solution.py:20
  125.8 6.1 %collective-permute-done.19 = bf16[2,72,1152]{2,1,0:T(8,128)(2,1)S(1)} collective-permute-done((bf16[2,72,1152]{2,1,0:T(8,128)(2,1)S(1)}, bf16[2,72,1152]{2,1,0:T(8,128)(2,1)S(1)}, u32[]{:S(2)}, u32[]{:S(2)}) %collective-permute-start.19) | collective-permute-done | bytes 331808 | tf_op jit(solution)/shard_map/ppermute | solution.py:20
  132.0 3.6 %collective-permute-done.17 = bf16[2,72,1152]{2,1,0:T(8,128)(2,1)S(1)} collective-permute-done((bf16[2,72,1152]{2,1,0:T(8,128)(2,1)S(1)}, bf16[2,72,1152]{2,1,0:T(8,128)(2,1)S(1)}, u32[]{:S(2)}, u32[]{:S(2)}) %collective-permute-start.17) | collective-permute-done | bytes 331808 | tf_op jit(solution)/shard_map/ppermute | solution.py:20
  138.4 2.0 %collective-permute-start.23 = (bf16[2,168,128]{2,1,0:T(8,128)(2,1)S(1)}, bf16[2,168,128]{2,1,0:T(8,128)(2,1)S(1)}, u32[]{:S(2)}, u32[]{:S(2)}) collective-permute-start(bf16[2,168,128]{2,1,0:T(8,128)(2,1)S(1)} %pad_maximum_fusion.14), channel_id=1, source_target_pairs={{0,32},{16,48},{32,64},{48,80},{64,96},{80,112},{96,0},{112,16},{1... | collective-permute-start | bytes 258056 | tf_op jit(solution)/shard_map/ppermute | solution.py:57
  141.7 5.3 %collective-permute-start.20 = (bf16[168,128]{1,0:T(8,128)(2,1)S(1)}, bf16[168,128]{1,0:T(8,128)(2,1)S(1)}, u32[]{:S(2)}, u32[]{:S(2)}) collective-permute-start(bf16[168,128]{1,0:T(8,128)(2,1)S(1)} %get-tuple-element.37), channel_id=1, source_target_pairs={{0,64},{16,80},{32,96},{48,112},{64,0},{80,16},{96,32},{112,48},{1... | collective-permute-start | bytes 129032 | tf_op jit(solution)/shard_map/ppermute | solution.py:57
  147.0 3.8 %collective-permute-done.24 = bf16[2,168,128]{2,1,0:T(8,128)(2,1)S(1)} collective-permute-done((bf16[2,168,128]{2,1,0:T(8,128)(2,1)S(1)}, bf16[2,168,128]{2,1,0:T(8,128)(2,1)S(1)}, u32[]{:S(2)}, u32[]{:S(2)}) %collective-permute-start.24) | collective-permute-done | bytes 86048 | tf_op jit(solution)/shard_map/ppermute | solution.py:57
  152.2 2.7 %collective-permute-start.26 = (bf16[168,128]{1,0:T(8,128)(2,1)S(1)}, bf16[168,128]{1,0:T(8,128)(2,1)S(1)}, u32[]{:S(2)}, u32[]{:S(2)}) collective-permute-start(bf16[168,128]{1,0:T(8,128)(2,1)S(1)} %fusion.27), channel_id=1, source_target_pairs={{0,128},{128,0},{1,129},{129,1},{2,130},{130,2},{3,131},{131,3},{4... | collective-permute-start | bytes 129032 | tf_op jit(solution)/shard_map/ppermute | solution.py:25
  154.9 2.9 %collective-permute-done.26 = bf16[168,128]{1,0:T(8,128)(2,1)S(1)} collective-permute-done((bf16[168,128]{1,0:T(8,128)(2,1)S(1)}, bf16[168,128]{1,0:T(8,128)(2,1)S(1)}, u32[]{:S(2)}, u32[]{:S(2)}) %collective-permute-start.26) | collective-permute-done | bytes 43040 | tf_op jit(solution)/shard_map/ppermute | solution.py:25
  158.0 2.9 %collective-permute-start.27 = (bf16[168,128]{1,0:T(8,128)(2,1)S(1)}, bf16[168,128]{1,0:T(8,128)(2,1)S(1)}, u32[]{:S(2)}, u32[]{:S(2)}) collective-permute-start(bf16[168,128]{1,0:T(8,128)(2,1)S(1)} %get-tuple-element.25), channel_id=1, source_target_pairs={{0,64},{16,80},{32,96},{48,112},{64,0},{80,16},{96,32},{112,48},{1... | collective-permute-start | bytes 129032 | tf_op jit(solution)/shard_map/ppermute | solution.py:57
  167.3 2.7 %collective-permute-done.30 = bf16[2,168,128]{2,1,0:T(8,128)(2,1)S(1)} collective-permute-done((bf16[2,168,128]{2,1,0:T(8,128)(2,1)S(1)}, bf16[2,168,128]{2,1,0:T(8,128)(2,1)S(1)}, u32[]{:S(2)}, u32[]{:S(2)}) %collective-permute-start.30) | collective-permute-done | bytes 86048 | tf_op jit(solution)/shard_map/ppermute | solution.py:57
  169.9 3.4 %collective-permute-done.31 = bf16[2,168,128]{2,1,0:T(8,128)(2,1)S(1)} collective-permute-done((bf16[2,168,128]{2,1,0:T(8,128)(2,1)S(1)}, bf16[2,168,128]{2,1,0:T(8,128)(2,1)S(1)}, u32[]{:S(2)}, u32[]{:S(2)}) %collective-permute-start.31) | collective-permute-done | bytes 86048 | tf_op jit(solution)/shard_map/ppermute | solution.py:57
  177.6 9.0 %collective-permute-done.34 = bf16[2,72,1152]{2,1,0:T(8,128)(2,1)S(1)} collective-permute-done((bf16[2,72,1152]{2,1,0:T(8,128)(2,1)S(1)}, bf16[2,72,1152]{2,1,0:T(8,128)(2,1)S(1)}, u32[]{:S(2)}, u32[]{:S(2)}) %collective-permute-start.34) | collective-permute-done | bytes 331808 | tf_op jit(solution)/shard_map/ppermute | solution.py:20
  187.2 2.9 %collective-permute-start.36 = (bf16[2,32,1152]{2,1,0:T(8,128)(2,1)S(1)}, bf16[2,32,1152]{2,1,0:T(8,128)(2,1)S(1)}, u32[]{:S(2)}, u32[]{:S(2)}) collective-permute-start(bf16[2,32,1152]{2,1,0:T(8,128)(2,1)S(1)} %slice.254), channel_id=1, source_target_pairs={{0,12},{4,0},{8,4},{12,8},{1,13},{5,1},{9,5},{13,9},{2,14},{6,2},{... | collective-permute-start | bytes 442376 | tf_op jit(solution)/shard_map/ppermute | solution.py:20
  190.1 2.6 %collective-permute-done.36 = bf16[2,32,1152]{2,1,0:T(8,128)(2,1)S(1)} collective-permute-done((bf16[2,32,1152]{2,1,0:T(8,128)(2,1)S(1)}, bf16[2,32,1152]{2,1,0:T(8,128)(2,1)S(1)}, u32[]{:S(2)}, u32[]{:S(2)}) %collective-permute-start.36) | collective-permute-done | bytes 147488 | tf_op jit(solution)/shard_map/ppermute | solution.py:20
  (173 shorter events, 57.0 us)
Async XLA Ops:
  4.2 4.0 %collective-permute-start = (bf16[2,48,1152]{2,1,0:T(8,128)(2,1)S(1)}, bf16[2,48,1152]{2,1,0:T(8,128)(2,1)}, u32[]{:S(2)}, u32[]{:S(2)}) collective-permute-start(bf16[2,48,1152]{2,1,0:T(8,128)(2,1)S(1)} %fusion.17), channel_id=1, source_target_pairs={{0,1},{1,0},{2,3},{3,2},{4,5},{5,4},{6,7},{7,6},{8,9},{9,8},{10,11... | collective-permute-start | bytes 663560 | tf_op jit(solution)/shard_map/ppermute | solution.py:25
  6.6 5.2 %collective-permute-start.3 = (bf16[48,1152]{1,0:T(8,128)(2,1)S(1)}, bf16[48,1152]{1,0:T(8,128)(2,1)S(1)}, u32[]{:S(2)}, u32[]{:S(2)}) collective-permute-start(bf16[48,1152]{1,0:T(8,128)(2,1)S(1)} %fusion.25), channel_id=1, source_target_pairs={{0,2},{2,0},{1,3},{3,1},{4,6},{6,4},{5,7},{7,5},{8,10},{10,8},{9,1... | collective-permute-start | bytes 331784 | tf_op jit(solution)/shard_map/ppermute | solution.py:25
  9.3 4.9 %collective-permute-start.1 = (bf16[48,1152]{1,0:T(8,128)(2,1)S(1)}, bf16[48,1152]{1,0:T(8,128)(2,1)S(1)}, u32[]{:S(2)}, u32[]{:S(2)}) collective-permute-start(bf16[48,1152]{1,0:T(8,128)(2,1)S(1)} %fusion.24), channel_id=1, source_target_pairs={{0,2},{2,0},{1,3},{3,1},{4,6},{6,4},{5,7},{7,5},{8,10},{10,8},{9,1... | collective-permute-start | bytes 331784 | tf_op jit(solution)/shard_map/ppermute | solution.py:25
  18.6 15.4 %collective-permute-start.7 = (bf16[96,1152]{1,0:T(8,128)(2,1)}, bf16[96,1152]{1,0:T(8,128)(2,1)}, u32[]{:S(2)}, u32[]{:S(2)}) collective-permute-start(bf16[96,1152]{1,0:T(8,128)(2,1)} %pad_maximum_fusion.8), channel_id=1, source_target_pairs={{0,48},{16,64},{32,80},{48,96},{64,112},{80,0},{96,16},{112,32},{1... | collective-permute-start | bytes 663560 | tf_op jit(solution)/shard_map/ppermute | solution.py:57
  24.5 34.3 %all-to-all-start = ((bf16[16,48,1152]{2,1,0:T(8,128)(2,1)}), bf16[16,48,1152]{2,1,0:T(8,128)(2,1)S(1)}, u32[]{:S(2)}, u32[]{:S(2)}) async-start(bf16[16,48,1152]{2,1,0:T(8,128)(2,1)} %broadcast_in_dim.2), calls=%async_computation | async-start | bytes 3538944 | tf_op jit(solution)/shard_map/all_to_all | solution.py:183
  31.5 6.2 %collective-permute-start.5 = (bf16[96,1152]{1,0:T(8,128)(2,1)}, bf16[96,1152]{1,0:T(8,128)(2,1)S(1)}, u32[]{:S(2)}, u32[]{:S(2)}) collective-permute-start(bf16[96,1152]{1,0:T(8,128)(2,1)} %pad_maximum_fusion.8), channel_id=1, source_target_pairs={{0,16},{16,32},{32,48},{48,64},{64,80},{80,96},{96,112},{112,0},{1... | collective-permute-start | bytes 663560 | tf_op jit(solution)/shard_map/ppermute | solution.py:57
  32.6 10.7 %collective-permute-start.6 = (bf16[96,1152]{1,0:T(8,128)(2,1)}, bf16[96,1152]{1,0:T(8,128)(2,1)S(1)}, u32[]{:S(2)}, u32[]{:S(2)}) collective-permute-start(bf16[96,1152]{1,0:T(8,128)(2,1)} %pad_maximum_fusion.8), channel_id=1, source_target_pairs={{0,32},{16,48},{32,64},{48,80},{64,96},{80,112},{96,0},{112,16},{1... | collective-permute-start | bytes 663560 | tf_op jit(solution)/shard_map/ppermute | solution.py:57
  35.0 8.6 %collective-permute-start.8 = (bf16[48,1152]{1,0:T(8,128)(2,1)S(1)}, bf16[48,1152]{1,0:T(8,128)(2,1)S(1)}, u32[]{:S(2)}, u32[]{:S(2)}) collective-permute-start(bf16[48,1152]{1,0:T(8,128)(2,1)S(1)} %slice_select_fusion), channel_id=1, source_target_pairs={{0,16},{16,32},{32,48},{48,64},{64,80},{80,96},{96,112},{112,0},{1... | collective-permute-start | bytes 331784 | tf_op jit(solution)/shard_map/ppermute | solution.py:57
  65.4 5.0 %collective-permute-start.10 = (bf16[336,1152]{1,0:T(8,128)(2,1)S(1)}, bf16[336,1152]{1,0:T(8,128)(2,1)S(1)}, u32[]{:S(2)}, u32[]{:S(2)}) collective-permute-start(bf16[336,1152]{1,0:T(8,128)(2,1)S(1)} %slice.226), channel_id=1, source_target_pairs={{0,1},{1,0},{2,3},{3,2},{4,5},{5,4},{6,7},{7,6},{8,9},{9,8},{10,11... | collective-permute-start | bytes 2322440 | tf_op jit(solution)/shard_map/ppermute | solution.py:25
  71.4 31.9 %all-to-all-start.1 = ((bf16[16,48,1152]{2,1,0:T(8,128)(2,1)}), bf16[16,48,1152]{2,1,0:T(8,128)(2,1)S(1)}, u32[]{:S(2)}, u32[]{:S(2)}) async-start(bf16[16,48,1152]{2,1,0:T(8,128)(2,1)} %bitcast.170), calls=%async_computation.1 | async-start | bytes 3538944 | tf_op jit(solution)/shard_map/all_to_all | solution.py:201
  76.7 14.1 %collective-permute-start.11 = (bf16[96,1152]{1,0:T(8,128)(2,1)S(1)}, bf16[96,1152]{1,0:T(8,128)(2,1)S(1)}, u32[]{:S(2)}, u32[]{:S(2)}) collective-permute-start(bf16[96,1152]{1,0:T(8,128)(2,1)S(1)} %get-tuple-element.28), channel_id=1, source_target_pairs={{0,80},{16,96},{32,112},{48,0},{64,16},{80,32},{96,48},{112,64},{1... | collective-permute-start | bytes 663560 | tf_op jit(solution)/shard_map/ppermute | solution.py:57
  77.9 15.3 %collective-permute-start.12 = (bf16[96,1152]{1,0:T(8,128)(2,1)S(1)}, bf16[96,1152]{1,0:T(8,128)(2,1)S(1)}, u32[]{:S(2)}, u32[]{:S(2)}) collective-permute-start(bf16[96,1152]{1,0:T(8,128)(2,1)S(1)} %get-tuple-element.30), channel_id=1, source_target_pairs={{0,96},{16,112},{32,0},{48,16},{64,32},{80,48},{96,64},{112,80},{1... | collective-permute-start | bytes 663560 | tf_op jit(solution)/shard_map/ppermute | solution.py:57
  77.9 19.5 %collective-permute-start.13 = (bf16[96,1152]{1,0:T(8,128)(2,1)S(1)}, bf16[96,1152]{1,0:T(8,128)(2,1)S(1)}, u32[]{:S(2)}, u32[]{:S(2)}) collective-permute-start(bf16[96,1152]{1,0:T(8,128)(2,1)S(1)} %get-tuple-element.29), channel_id=1, source_target_pairs={{0,112},{16,0},{32,16},{48,32},{64,48},{80,64},{96,80},{112,96},{1... | collective-permute-start | bytes 663560 | tf_op jit(solution)/shard_map/ppermute | solution.py:57
  80.2 23.6 %collective-permute-start.14 = (bf16[48,1152]{1,0:T(8,128)(2,1)}, bf16[48,1152]{1,0:T(8,128)(2,1)}, u32[]{:S(2)}, u32[]{:S(2)}) collective-permute-start(bf16[48,1152]{1,0:T(8,128)(2,1)} %add_convert_fusion.3), channel_id=1, source_target_pairs={{0,64},{16,80},{32,96},{48,112},{64,0},{80,16},{96,32},{112,48},{1... | collective-permute-start | bytes 331784 | tf_op jit(solution)/shard_map/ppermute | solution.py:57
  99.2 4.5 %collective-permute-start.15 = (bf16[48,1152]{1,0:T(8,128)(2,1)}, bf16[48,1152]{1,0:T(8,128)(2,1)}, u32[]{:S(2)}, u32[]{:S(2)}) collective-permute-start(bf16[48,1152]{1,0:T(8,128)(2,1)} %select_convert_fusion), channel_id=1, source_target_pairs={{0,1},{1,0},{2,3},{3,2},{4,5},{5,4},{6,7},{7,6},{8,9},{9,8},{10,11... | collective-permute-start | bytes 331784 | tf_op jit(solution)/shard_map/ppermute | solution.py:25
  115.0 10.5 %collective-permute-start.16 = (bf16[2,40,1152]{2,1,0:T(8,128)(2,1)S(1)}, bf16[2,40,1152]{2,1,0:T(8,128)(2,1)S(1)}, u32[]{:S(2)}, u32[]{:S(2)}) collective-permute-start(bf16[2,40,1152]{2,1,0:T(8,128)(2,1)S(1)} %fusion.19), channel_id=1, source_target_pairs={{0,4},{4,8},{8,12},{12,0},{1,5},{5,9},{9,13},{13,1},{2,6},{6,10},{... | collective-permute-start | bytes 552968 | tf_op jit(solution)/shard_map/ppermute | solution.py:20
  115.1 6.6 %collective-permute-start.18 = (bf16[2,32,1152]{2,1,0:T(8,128)(2,1)S(1)}, bf16[2,32,1152]{2,1,0:T(8,128)(2,1)S(1)}, u32[]{:S(2)}, u32[]{:S(2)}) collective-permute-start(bf16[2,32,1152]{2,1,0:T(8,128)(2,1)S(1)} %pad_maximum_fusion.10), channel_id=1, source_target_pairs={{0,12},{4,0},{8,4},{12,8},{1,13},{5,1},{9,5},{13,9},{2,14},{6,2},{... | collective-permute-start | bytes 442376 | tf_op jit(solution)/shard_map/ppermute | solution.py:20
  121.8 10.2 %collective-permute-start.19 = (bf16[2,72,1152]{2,1,0:T(8,128)(2,1)S(1)}, bf16[2,72,1152]{2,1,0:T(8,128)(2,1)S(1)}, u32[]{:S(2)}, u32[]{:S(2)}) collective-permute-start(bf16[2,72,1152]{2,1,0:T(8,128)(2,1)S(1)} %pad_maximum_fusion.3), channel_id=1, source_target_pairs={{0,12},{4,0},{8,4},{12,8},{1,13},{5,1},{9,5},{13,9},{2,14},{6,2},{... | collective-permute-start | bytes 995336 | tf_op jit(solution)/shard_map/ppermute | solution.py:20
  125.6 9.9 %collective-permute-start.17 = (bf16[2,72,1152]{2,1,0:T(8,128)(2,1)S(1)}, bf16[2,72,1152]{2,1,0:T(8,128)(2,1)S(1)}, u32[]{:S(2)}, u32[]{:S(2)}) collective-permute-start(bf16[2,72,1152]{2,1,0:T(8,128)(2,1)S(1)} %pad_maximum_fusion.2), channel_id=1, source_target_pairs={{0,4},{4,8},{8,12},{12,0},{1,5},{5,9},{9,13},{13,1},{2,6},{6,10},{... | collective-permute-start | bytes 995336 | tf_op jit(solution)/shard_map/ppermute | solution.py:20
  137.3 9.7 %collective-permute-start.22 = (bf16[2,168,128]{2,1,0:T(8,128)(2,1)S(1)}, bf16[2,168,128]{2,1,0:T(8,128)(2,1)S(1)}, u32[]{:S(2)}, u32[]{:S(2)}) collective-permute-start(bf16[2,168,128]{2,1,0:T(8,128)(2,1)S(1)} %pad_maximum_fusion.13), channel_id=1, source_target_pairs={{0,16},{16,32},{32,48},{48,64},{64,80},{80,96},{96,112},{112,0},{1... | collective-permute-start | bytes 258056 | tf_op jit(solution)/shard_map/ppermute | solution.py:57
  138.4 8.6 %collective-permute-start.23 = (bf16[2,168,128]{2,1,0:T(8,128)(2,1)S(1)}, bf16[2,168,128]{2,1,0:T(8,128)(2,1)S(1)}, u32[]{:S(2)}, u32[]{:S(2)}) collective-permute-start(bf16[2,168,128]{2,1,0:T(8,128)(2,1)S(1)} %pad_maximum_fusion.14), channel_id=1, source_target_pairs={{0,32},{16,48},{32,64},{48,80},{64,96},{80,112},{96,0},{112,16},{1... | collective-permute-start | bytes 258056 | tf_op jit(solution)/shard_map/ppermute | solution.py:57
  140.5 10.4 %collective-permute-start.24 = (bf16[2,168,128]{2,1,0:T(8,128)(2,1)S(1)}, bf16[2,168,128]{2,1,0:T(8,128)(2,1)S(1)}, u32[]{:S(2)}, u32[]{:S(2)}) collective-permute-start(bf16[2,168,128]{2,1,0:T(8,128)(2,1)S(1)} %pad_maximum_fusion.15), channel_id=1, source_target_pairs={{0,48},{16,64},{32,80},{48,96},{64,112},{80,0},{96,16},{112,32},{1... | collective-permute-start | bytes 258056 | tf_op jit(solution)/shard_map/ppermute | solution.py:57
  141.7 9.3 %collective-permute-start.20 = (bf16[168,128]{1,0:T(8,128)(2,1)S(1)}, bf16[168,128]{1,0:T(8,128)(2,1)S(1)}, u32[]{:S(2)}, u32[]{:S(2)}) collective-permute-start(bf16[168,128]{1,0:T(8,128)(2,1)S(1)} %get-tuple-element.37), channel_id=1, source_target_pairs={{0,64},{16,80},{32,96},{48,112},{64,0},{80,16},{96,32},{112,48},{1... | collective-permute-start | bytes 129032 | tf_op jit(solution)/shard_map/ppermute | solution.py:57
  152.2 5.6 %collective-permute-start.26 = (bf16[168,128]{1,0:T(8,128)(2,1)S(1)}, bf16[168,128]{1,0:T(8,128)(2,1)S(1)}, u32[]{:S(2)}, u32[]{:S(2)}) collective-permute-start(bf16[168,128]{1,0:T(8,128)(2,1)S(1)} %fusion.27), channel_id=1, source_target_pairs={{0,128},{128,0},{1,129},{129,1},{2,130},{130,2},{3,131},{131,3},{4... | collective-permute-start | bytes 129032 | tf_op jit(solution)/shard_map/ppermute | solution.py:25
  158.0 9.3 %collective-permute-start.27 = (bf16[168,128]{1,0:T(8,128)(2,1)S(1)}, bf16[168,128]{1,0:T(8,128)(2,1)S(1)}, u32[]{:S(2)}, u32[]{:S(2)}) collective-permute-start(bf16[168,128]{1,0:T(8,128)(2,1)S(1)} %get-tuple-element.25), channel_id=1, source_target_pairs={{0,64},{16,80},{32,96},{48,112},{64,0},{80,16},{96,32},{112,48},{1... | collective-permute-start | bytes 129032 | tf_op jit(solution)/shard_map/ppermute | solution.py:57
  160.9 6.4 %collective-permute-start.29 = (bf16[2,168,128]{2,1,0:T(8,128)(2,1)S(1)}, bf16[2,168,128]{2,1,0:T(8,128)(2,1)S(1)}, u32[]{:S(2)}, u32[]{:S(2)}) collective-permute-start(bf16[2,168,128]{2,1,0:T(8,128)(2,1)S(1)} %pad_maximum_fusion.16), channel_id=1, source_target_pairs={{0,16},{16,32},{32,48},{48,64},{64,80},{80,96},{96,112},{112,0},{1... | collective-permute-start | bytes 258056 | tf_op jit(solution)/shard_map/ppermute | solution.py:57
  162.3 7.6 %collective-permute-start.30 = (bf16[2,168,128]{2,1,0:T(8,128)(2,1)S(1)}, bf16[2,168,128]{2,1,0:T(8,128)(2,1)S(1)}, u32[]{:S(2)}, u32[]{:S(2)}) collective-permute-start(bf16[2,168,128]{2,1,0:T(8,128)(2,1)S(1)} %pad_maximum_fusion.16), channel_id=1, source_target_pairs={{0,32},{16,48},{32,64},{48,80},{64,96},{80,112},{96,0},{112,16},{1... | collective-permute-start | bytes 258056 | tf_op jit(solution)/shard_map/ppermute | solution.py:57
  163.9 9.4 %collective-permute-start.31 = (bf16[2,168,128]{2,1,0:T(8,128)(2,1)S(1)}, bf16[2,168,128]{2,1,0:T(8,128)(2,1)S(1)}, u32[]{:S(2)}, u32[]{:S(2)}) collective-permute-start(bf16[2,168,128]{2,1,0:T(8,128)(2,1)S(1)} %pad_maximum_fusion.16), channel_id=1, source_target_pairs={{0,48},{16,64},{32,80},{48,96},{64,112},{80,0},{96,16},{112,32},{1... | collective-permute-start | bytes 258056 | tf_op jit(solution)/shard_map/ppermute | solution.py:57
  175.3 11.9 %collective-permute-start.33 = (bf16[2,72,1152]{2,1,0:T(8,128)(2,1)S(1)}, bf16[2,72,1152]{2,1,0:T(8,128)(2,1)S(1)}, u32[]{:S(2)}, u32[]{:S(2)}) collective-permute-start(bf16[2,72,1152]{2,1,0:T(8,128)(2,1)S(1)} %bitcast.174), channel_id=1, source_target_pairs={{0,12},{4,0},{8,4},{12,8},{1,13},{5,1},{9,5},{13,9},{2,14},{6,2},{... | collective-permute-start | bytes 995336 | tf_op jit(solution)/shard_map/ppermute | solution.py:20
  175.4 11.2 %collective-permute-start.34 = (bf16[2,72,1152]{2,1,0:T(8,128)(2,1)S(1)}, bf16[2,72,1152]{2,1,0:T(8,128)(2,1)S(1)}, u32[]{:S(2)}, u32[]{:S(2)}) collective-permute-start(bf16[2,72,1152]{2,1,0:T(8,128)(2,1)S(1)} %bitcast.175), channel_id=1, source_target_pairs={{0,4},{4,8},{8,12},{12,0},{1,5},{5,9},{9,13},{13,1},{2,6},{6,10},{... | collective-permute-start | bytes 995336 | tf_op jit(solution)/shard_map/ppermute | solution.py:20
  186.6 7.3 %collective-permute-start.35 = (bf16[2,40,1152]{2,1,0:T(8,128)(2,1)S(1)}, bf16[2,40,1152]{2,1,0:T(8,128)(2,1)S(1)}, u32[]{:S(2)}, u32[]{:S(2)}) collective-permute-start(bf16[2,40,1152]{2,1,0:T(8,128)(2,1)S(1)} %slice.252), channel_id=1, source_target_pairs={{0,4},{4,8},{8,12},{12,0},{1,5},{5,9},{9,13},{13,1},{2,6},{6,10},{... | collective-permute-start | bytes 552968 | tf_op jit(solution)/shard_map/ppermute | solution.py:20
  187.2 5.5 %collective-permute-start.36 = (bf16[2,32,1152]{2,1,0:T(8,128)(2,1)S(1)}, bf16[2,32,1152]{2,1,0:T(8,128)(2,1)S(1)}, u32[]{:S(2)}, u32[]{:S(2)}) collective-permute-start(bf16[2,32,1152]{2,1,0:T(8,128)(2,1)S(1)} %slice.254), channel_id=1, source_target_pairs={{0,12},{4,0},{8,4},{12,8},{1,13},{5,1},{9,5},{13,9},{2,14},{6,2},{... | collective-permute-start | bytes 442376 | tf_op jit(solution)/shard_map/ppermute | solution.py:20
  (22 other events, 86.8 us)

commit v4 on v3

--- a/solution.py
+++ b/solution.py
@@ -57,7 +57,7 @@
     return lax.ppermute(value, ("z", "core"), pairs)
 
 
-def column_gather(value):
+def column_gather(value, images):
     first = lax.axis_index("core") == 0
     other = flip(value, "core", 1)
     pair = jnp.concatenate([jnp.where(first, value, other), jnp.where(first, other, value)], axis=0)
@@ -65,7 +65,8 @@
     got = {k: column_shift(pair, k) for k in (3, 2, 1)}
     far = column_shift(jnp.where(first, got[3][:rows], got[3][rows:]), 1)
     mine = lax.optimization_barrier(jnp.concatenate([got[1], got[2], got[3], far], axis=0))
-    return jnp.concatenate([pair, mine, flip(mine, "core", 1)], axis=0)
+    mine, images = lax.optimization_barrier((mine, images))
+    return jnp.concatenate([pair, mine, flip(mine, "core", 1)], axis=0), images
 
 
 def column_sum(parts, swapped, rows):
@@ -181,7 +182,7 @@
     spread = jnp.broadcast_to(image_unit.astype(BF16)[None], (plane, quarter, width))
     spread, text_emb = lax.optimization_barrier((spread, text_unit.astype(BF16)))
     images = lax.all_to_all(spread, PLANE, 0, 0).reshape(-1, width)
-    texts = column_gather(text_emb)
+    texts, images = column_gather(text_emb, images)
     own_image = lax.axis_index(PLANE) * quarter
     own_text = lax.axis_index("core") * quarter
     scores = lax.dot_general(images, texts, (((1,), (1,)), ((), ())), preferred_element_type=F32)

time: 196 us -> 196 us (level)
  starting transfers between devices: 63.4 us -> 70.5 us
  waiting for transfers between devices: 84.4 us -> 78.4 us
    ppermute x16, starting transfers between devices: 33.9 us -> 40.4 us  [column_shift(): return lax.ppermute(value, ('z', 'core'), pairs)]
    all_to_all x1, waiting for transfers between devices: 10.6 us -> 4.19 us  [per_device(): images = lax.all_to_all(spread, PLANE, 0, 0).reshape(-1, width)]
    ppermute x16, waiting for transfers between devices: 29.9 us -> 34.3 us  [column_shift(): return lax.ppermute(value, ('z', 'core'), pairs)]
    ppermute x13, waiting for transfers between devices: 14 us -> 11.7 us  [flip(): return lax.ppermute(value, axis, [(i, i ^ bit) for i in range(n)])]
    unnamed x33 -> x35, local copies, waits for them, and re-layouts: 5.89 us -> 5.29 us
  transfers between devices with their start and end apart: 39 -> 39, of which waited for: 27 -> 27; matrix products, arithmetic and copies ran while one was open for 10% -> 9% of each run, Pallas kernels for 0% -> 0%
where the time goes in v4:
time: 196 us; the launch traced here: 195 us
  waiting for transfers between devices  78.4 us (40%)
  starting transfers between devices  70.5 us (36%)
  matrix products  14.9 us (8%)
  other arithmetic  13.6 us (7%)
  blocking collectives  8.29 us (4%)
  local copies, waits for them, and re-layouts  8.2 us (4%)
    ppermute x16, starting transfers between devices, column_shift(): return lax.ppermute(value, ('z', 'core'), pairs)  40.4 us
    ppermute x16, waiting for transfers between devices, column_shift(): return lax.ppermute(value, ('z', 'core'), pairs)  34.3 us
    ppermute x8, waiting for transfers between devices, shift(): return lax.ppermute(value, axis, [(i, (i + by) % n) for i in range(n)])  26.1 us
    ppermute x8, starting transfers between devices, shift(): return lax.ppermute(value, axis, [(i, (i + by) % n) for i in range(n)])  12.3 us
    ppermute x13, waiting for transfers between devices, flip(): return lax.ppermute(value, axis, [(i, i ^ bit) for i in range(n)])  11.7 us
    all_gather x1, blocking collectives, per_device(): lax.all_gather(jnp.concatenate([image_grad_raw, text_grad_raw], axis=1),...  8.29 us
    ppermute x13, starting transfers between devices, flip(): return lax.ppermute(value, axis, [(i, i ^ bit) for i in range(n)])  7.02 us
    all_to_all x1, starting transfers between devices, per_device(): images = lax.all_to_all(spread, PLANE, 0, 0).reshape(-1, width)  7 us
  transfers between devices with their start and end apart: 39, of which 27 were waited for; matrix products, arithmetic and copies ran while one was open for 9% of the time, Pallas kernels for 0%

profile of v4, /device:TPU:32, one launch (start us, length us, event | category | flops | bytes accessed | tf_op | source)
XLA Modules:
  0.0 195.2 jit_solution(10462310095302862389)
XLA Ops:
  11.9 2.3 %collective-permute-done.1 = bf16[48,1152]{1,0:T(8,128)(2,1)S(1)} collective-permute-done((bf16[48,1152]{1,0:T(8,128)(2,1)S(1)}, bf16[48,1152]{1,0:T(8,128)(2,1)S(1)}, u32[]{:S(2)}, u32[]{:S(2)}) %collective-permute-start.1) | collective-permute-done | bytes 110624 | tf_op jit(solution)/shard_map/ppermute | solution.py:25
  16.5 7.0 %all-to-all-start = ((bf16[16,48,1152]{2,1,0:T(8,128)(2,1)}), bf16[16,48,1152]{2,1,0:T(8,128)(2,1)S(1)}, u32[]{:S(2)}, u32[]{:S(2)}) async-start(bf16[16,48,1152]{2,1,0:T(8,128)(2,1)} %broadcast_in_dim.2), calls=%async_computation | async-start | bytes 3538944 | tf_op jit(solution)/shard_map/all_to_all | solution.py:184
  24.6 5.9 %collective-permute-start.7 = (bf16[96,1152]{1,0:T(8,128)(2,1)S(1)}, bf16[96,1152]{1,0:T(8,128)(2,1)S(1)}, u32[]{:S(2)}, u32[]{:S(2)}) collective-permute-start(bf16[96,1152]{1,0:T(8,128)(2,1)S(1)} %pad_maximum_fusion.8), channel_id=1, source_target_pairs={{0,48},{16,64},{32,80},{48,96},{64,112},{80,0},{96,16},{112,32},{1... | collective-permute-start | bytes 663560 | tf_op jit(solution)/shard_map/ppermute | solution.py:57
  33.0 5.8 %collective-permute-done.7 = bf16[96,1152]{1,0:T(8,128)(2,1)S(1)} collective-permute-done((bf16[96,1152]{1,0:T(8,128)(2,1)S(1)}, bf16[96,1152]{1,0:T(8,128)(2,1)S(1)}, u32[]{:S(2)}, u32[]{:S(2)}) %collective-permute-start.7) | collective-permute-done | bytes 221216 | tf_op jit(solution)/shard_map/ppermute | solution.py:57
  40.7 3.9 %collective-permute-done.6 = bf16[96,1152]{1,0:T(8,128)(2,1)S(1)} collective-permute-done((bf16[96,1152]{1,0:T(8,128)(2,1)S(1)}, bf16[96,1152]{1,0:T(8,128)(2,1)S(1)}, u32[]{:S(2)}, u32[]{:S(2)}) %collective-permute-start.6) | collective-permute-done | bytes 221216 | tf_op jit(solution)/shard_map/ppermute | solution.py:57
  47.3 4.2 %all-to-all-done = bf16[16,48,1152]{2,1,0:T(8,128)(2,1)S(1)} async-done(((bf16[16,48,1152]{2,1,0:T(8,128)(2,1)}), bf16[16,48,1152]{2,1,0:T(8,128)(2,1)S(1)}, u32[]{:S(2)}, u32[]{:S(2)}) %all-to-all-start) | async-done | bytes 1769504 | tf_op jit(solution)/shard_map/all_to_all | solution.py:184
  51.6 2.6 %collective-permute-done.9 = bf16[336,1152]{1,0:T(8,128)(2,1)} collective-permute-done((bf16[336,1152]{1,0:T(8,128)(2,1)}, bf16[336,1152]{1,0:T(8,128)(2,1)}, u32[]{:S(2)}, u32[]{:S(2)}) %collective-permute-start.9) | collective-permute-done | bytes 774176 | tf_op jit(solution)/shard_map/ppermute | solution.py:25
  54.1 3.7 %multiply_convert_fusion = bf16[768,768]{1,0:T(8,128)(2,1)S(1)} fusion(bf16[768,1152]{1,0:T(8,128)(2,1)S(1)} %bitcast.168, s32[768]{0:T(1024)S(1)} %fusion.32, pred[768]{0:T(1024)(128)(4,1)S(1)} %fusion.30, pred[768]{0:T(1024)(128)(4,1)S(1)} %fusion.31, bf16[336,1152]{1,0:T(8,128)(2,1)} %collective-permute-done.9, bf16[336,1152]{1,0:T(8,128)(2,1)} %pad_maximum_fusion.1, ...), kind=kOutput, calls=%fused_computation.3 | convolution fusion | flops 1373110272 | bytes 4723200 | tf_op jit(solution)/shard_map/dot_general | solution.py:188
  61.3 4.7 %convolution_convert_fusion = bf16[768,1152]{1,0:T(8,128)(2,1)} fusion(bf16[768,768]{1,0:T(8,128)(2,1)} %copy-done.15, bf16[336,1152]{1,0:T(8,128)(2,1)} %collective-permute-done.9, bf16[336,1152]{1,0:T(8,128)(2,1)} %pad_maximum_fusion.1, bf16[48,1152]{1,0:T(8,128)(2,1)} %copy-done.13, bf16[48,1152]{1,0:T(8,128)(2,1)} %copy-done.12), kind=kOutput, calls=%fused_computation.1 | convolution fusion | flops 1366917120 | bytes 4718592 | tf_op jit(solution)/shard_map/dot_general | solution.py:200
  66.9 3.7 %all-to-all-start.1 = ((bf16[16,48,1152]{2,1,0:T(8,128)(2,1)}), bf16[16,48,1152]{2,1,0:T(8,128)(2,1)S(1)}, u32[]{:S(2)}, u32[]{:S(2)}) async-start(bf16[16,48,1152]{2,1,0:T(8,128)(2,1)} %bitcast.170), calls=%async_computation.1 | async-start | bytes 3538944 | tf_op jit(solution)/shard_map/all_to_all | solution.py:202
  72.2 5.9 %collective-permute-start.11 = (bf16[96,1152]{1,0:T(8,128)(2,1)S(1)}, bf16[96,1152]{1,0:T(8,128)(2,1)S(1)}, u32[]{:S(2)}, u32[]{:S(2)}) collective-permute-start(bf16[96,1152]{1,0:T(8,128)(2,1)S(1)} %get-tuple-element.32), channel_id=1, source_target_pairs={{0,80},{16,96},{32,112},{48,0},{64,16},{80,32},{96,48},{112,64},{1... | collective-permute-start | bytes 663560 | tf_op jit(solution)/shard_map/ppermute | solution.py:57
  81.3 4.5 %collective-permute-start.14 = (bf16[48,1152]{1,0:T(8,128)(2,1)}, bf16[48,1152]{1,0:T(8,128)(2,1)}, u32[]{:S(2)}, u32[]{:S(2)}) collective-permute-start(bf16[48,1152]{1,0:T(8,128)(2,1)} %add_convert_fusion.3), channel_id=1, source_target_pairs={{0,64},{16,80},{32,96},{48,112},{64,0},{80,16},{96,32},{112,48},{1... | collective-permute-start | bytes 331784 | tf_op jit(solution)/shard_map/ppermute | solution.py:57
  86.2 4.7 %collective-permute-done.12 = bf16[96,1152]{1,0:T(8,128)(2,1)S(1)} collective-permute-done((bf16[96,1152]{1,0:T(8,128)(2,1)S(1)}, bf16[96,1152]{1,0:T(8,128)(2,1)S(1)}, u32[]{:S(2)}, u32[]{:S(2)}) %collective-permute-start.12) | collective-permute-done | bytes 221216 | tf_op jit(solution)/shard_map/ppermute | solution.py:57
  90.9 3.4 %collective-permute-done.13 = bf16[96,1152]{1,0:T(8,128)(2,1)S(1)} collective-permute-done((bf16[96,1152]{1,0:T(8,128)(2,1)S(1)}, bf16[96,1152]{1,0:T(8,128)(2,1)S(1)}, u32[]{:S(2)}, u32[]{:S(2)}) %collective-permute-start.13) | collective-permute-done | bytes 221216 | tf_op jit(solution)/shard_map/ppermute | solution.py:57
  96.7 2.1 %all-to-all-done.1 = bf16[16,48,1152]{2,1,0:T(8,128)(2,1)S(1)} async-done(((bf16[16,48,1152]{2,1,0:T(8,128)(2,1)}), bf16[16,48,1152]{2,1,0:T(8,128)(2,1)S(1)}, u32[]{:S(2)}, u32[]{:S(2)}) %all-to-all-start.1) | async-done | bytes 1769504 | tf_op jit(solution)/shard_map/all_to_all | solution.py:202
  101.2 8.3 %all_gather.3 = bf16[192,2304]{1,0:T(8,128)(2,1)S(1)} all-gather(bf16[48,2304]{1,0:T(8,128)(2,1)S(1)} %pad_maximum_fusion.9), channel_id=1, replica_groups=mesh['yhi'=2,'z'=8,'x'=4,'ylo'=2,'core'=2] {'ylo','core'}, dimensions={0}, use_global_device_ids=true | all-gather | bytes 1105920 | tf_op jit(solution)/shard_map/all_gather | solution.py:208
  111.8 2.2 %collective-permute-start.18 = (bf16[2,32,1152]{2,1,0:T(8,128)(2,1)S(1)}, bf16[2,32,1152]{2,1,0:T(8,128)(2,1)S(1)}, u32[]{:S(2)}, u32[]{:S(2)}) collective-permute-start(bf16[2,32,1152]{2,1,0:T(8,128)(2,1)S(1)} %pad_maximum_fusion.10), channel_id=1, source_target_pairs={{0,12},{4,0},{8,4},{12,8},{1,13},{5,1},{9,5},{13,9},{2,14},{6,2},{... | collective-permute-start | bytes 442376 | tf_op jit(solution)/shard_map/ppermute | solution.py:20
  114.0 3.6 %collective-permute-done.18 = bf16[2,32,1152]{2,1,0:T(8,128)(2,1)S(1)} collective-permute-done((bf16[2,32,1152]{2,1,0:T(8,128)(2,1)S(1)}, bf16[2,32,1152]{2,1,0:T(8,128)(2,1)S(1)}, u32[]{:S(2)}, u32[]{:S(2)}) %collective-permute-start.18) | collective-permute-done | bytes 147488 | tf_op jit(solution)/shard_map/ppermute | solution.py:20
  117.7 3.4 %collective-permute-start.19 = (bf16[2,72,1152]{2,1,0:T(8,128)(2,1)S(1)}, bf16[2,72,1152]{2,1,0:T(8,128)(2,1)S(1)}, u32[]{:S(2)}, u32[]{:S(2)}) collective-permute-start(bf16[2,72,1152]{2,1,0:T(8,128)(2,1)S(1)} %pad_maximum_fusion.3), channel_id=1, source_target_pairs={{0,12},{4,0},{8,4},{12,8},{1,13},{5,1},{9,5},{13,9},{2,14},{6,2},{... | collective-permute-start | bytes 995336 | tf_op jit(solution)/shard_map/ppermute | solution.py:20
  121.4 6.2 %collective-permute-done.19 = bf16[2,72,1152]{2,1,0:T(8,128)(2,1)S(1)} collective-permute-done((bf16[2,72,1152]{2,1,0:T(8,128)(2,1)S(1)}, bf16[2,72,1152]{2,1,0:T(8,128)(2,1)S(1)}, u32[]{:S(2)}, u32[]{:S(2)}) %collective-permute-start.19) | collective-permute-done | bytes 331808 | tf_op jit(solution)/shard_map/ppermute | solution.py:20
  127.6 3.6 %collective-permute-done.17 = bf16[2,72,1152]{2,1,0:T(8,128)(2,1)S(1)} collective-permute-done((bf16[2,72,1152]{2,1,0:T(8,128)(2,1)S(1)}, bf16[2,72,1152]{2,1,0:T(8,128)(2,1)S(1)}, u32[]{:S(2)}, u32[]{:S(2)}) %collective-permute-start.17) | collective-permute-done | bytes 331808 | tf_op jit(solution)/shard_map/ppermute | solution.py:20
  134.8 5.8 %collective-permute-start.23 = (bf16[2,168,128]{2,1,0:T(8,128)(2,1)S(1)}, bf16[2,168,128]{2,1,0:T(8,128)(2,1)S(1)}, u32[]{:S(2)}, u32[]{:S(2)}) collective-permute-start(bf16[2,168,128]{2,1,0:T(8,128)(2,1)S(1)} %pad_maximum_fusion.14), channel_id=1, source_target_pairs={{0,32},{16,48},{32,64},{48,80},{64,96},{80,112},{96,0},{112,16},{1... | collective-permute-start | bytes 258056 | tf_op jit(solution)/shard_map/ppermute | solution.py:57
  140.6 3.0 %collective-permute-start.24 = (bf16[2,168,128]{2,1,0:T(8,128)(2,1)S(1)}, bf16[2,168,128]{2,1,0:T(8,128)(2,1)S(1)}, u32[]{:S(2)}, u32[]{:S(2)}) collective-permute-start(bf16[2,168,128]{2,1,0:T(8,128)(2,1)S(1)} %pad_maximum_fusion.15), channel_id=1, source_target_pairs={{0,48},{16,64},{32,80},{48,96},{64,112},{80,0},{96,16},{112,32},{1... | collective-permute-start | bytes 258056 | tf_op jit(solution)/shard_map/ppermute | solution.py:57
  144.1 6.1 %collective-permute-done.24 = bf16[2,168,128]{2,1,0:T(8,128)(2,1)S(1)} collective-permute-done((bf16[2,168,128]{2,1,0:T(8,128)(2,1)S(1)}, bf16[2,168,128]{2,1,0:T(8,128)(2,1)S(1)}, u32[]{:S(2)}, u32[]{:S(2)}) %collective-permute-start.24) | collective-permute-done | bytes 86048 | tf_op jit(solution)/shard_map/ppermute | solution.py:57
  151.6 3.0 %collective-permute-start.26 = (bf16[168,128]{1,0:T(8,128)(2,1)S(1)}, bf16[168,128]{1,0:T(8,128)(2,1)S(1)}, u32[]{:S(2)}, u32[]{:S(2)}) collective-permute-start(bf16[168,128]{1,0:T(8,128)(2,1)S(1)} %fusion.27), channel_id=1, source_target_pairs={{0,128},{128,0},{1,129},{129,1},{2,130},{130,2},{3,131},{131,3},{4... | collective-permute-start | bytes 129032 | tf_op jit(solution)/shard_map/ppermute | solution.py:25
  154.6 2.6 %collective-permute-done.26 = bf16[168,128]{1,0:T(8,128)(2,1)S(1)} collective-permute-done((bf16[168,128]{1,0:T(8,128)(2,1)S(1)}, bf16[168,128]{1,0:T(8,128)(2,1)S(1)}, u32[]{:S(2)}, u32[]{:S(2)}) %collective-permute-start.26) | collective-permute-done | bytes 43040 | tf_op jit(solution)/shard_map/ppermute | solution.py:25
  157.8 2.6 %collective-permute-start.27 = (bf16[168,128]{1,0:T(8,128)(2,1)S(1)}, bf16[168,128]{1,0:T(8,128)(2,1)S(1)}, u32[]{:S(2)}, u32[]{:S(2)}) collective-permute-start(bf16[168,128]{1,0:T(8,128)(2,1)S(1)} %get-tuple-element.29), channel_id=1, source_target_pairs={{0,64},{16,80},{32,96},{48,112},{64,0},{80,16},{96,32},{112,48},{1... | collective-permute-start | bytes 129032 | tf_op jit(solution)/shard_map/ppermute | solution.py:57
  166.3 2.9 %collective-permute-done.30 = bf16[2,168,128]{2,1,0:T(8,128)(2,1)S(1)} collective-permute-done((bf16[2,168,128]{2,1,0:T(8,128)(2,1)S(1)}, bf16[2,168,128]{2,1,0:T(8,128)(2,1)S(1)}, u32[]{:S(2)}, u32[]{:S(2)}) %collective-permute-start.30) | collective-permute-done | bytes 86048 | tf_op jit(solution)/shard_map/ppermute | solution.py:57
  169.3 3.7 %collective-permute-done.31 = bf16[2,168,128]{2,1,0:T(8,128)(2,1)S(1)} collective-permute-done((bf16[2,168,128]{2,1,0:T(8,128)(2,1)S(1)}, bf16[2,168,128]{2,1,0:T(8,128)(2,1)S(1)}, u32[]{:S(2)}, u32[]{:S(2)}) %collective-permute-start.31) | collective-permute-done | bytes 86048 | tf_op jit(solution)/shard_map/ppermute | solution.py:57
  177.3 9.0 %collective-permute-done.34 = bf16[2,72,1152]{2,1,0:T(8,128)(2,1)S(1)} collective-permute-done((bf16[2,72,1152]{2,1,0:T(8,128)(2,1)S(1)}, bf16[2,72,1152]{2,1,0:T(8,128)(2,1)S(1)}, u32[]{:S(2)}, u32[]{:S(2)}) %collective-permute-start.34) | collective-permute-done | bytes 331808 | tf_op jit(solution)/shard_map/ppermute | solution.py:20
  186.8 2.9 %collective-permute-start.36 = (bf16[2,32,1152]{2,1,0:T(8,128)(2,1)S(1)}, bf16[2,32,1152]{2,1,0:T(8,128)(2,1)S(1)}, u32[]{:S(2)}, u32[]{:S(2)}) collective-permute-start(bf16[2,32,1152]{2,1,0:T(8,128)(2,1)S(1)} %slice.254), channel_id=1, source_target_pairs={{0,12},{4,0},{8,4},{12,8},{1,13},{5,1},{9,5},{13,9},{2,14},{6,2},{... | collective-permute-start | bytes 442376 | tf_op jit(solution)/shard_map/ppermute | solution.py:20
  189.8 2.6 %collective-permute-done.36 = bf16[2,32,1152]{2,1,0:T(8,128)(2,1)S(1)} collective-permute-done((bf16[2,32,1152]{2,1,0:T(8,128)(2,1)S(1)}, bf16[2,32,1152]{2,1,0:T(8,128)(2,1)S(1)}, u32[]{:S(2)}, u32[]{:S(2)}) %collective-permute-start.36) | collective-permute-done | bytes 147488 | tf_op jit(solution)/shard_map/ppermute | solution.py:20
  (175 shorter events, 58.0 us)
Async XLA Ops:
  4.2 4.0 %collective-permute-start = (bf16[2,48,1152]{2,1,0:T(8,128)(2,1)S(1)}, bf16[2,48,1152]{2,1,0:T(8,128)(2,1)}, u32[]{:S(2)}, u32[]{:S(2)}) collective-permute-start(bf16[2,48,1152]{2,1,0:T(8,128)(2,1)S(1)} %fusion.17), channel_id=1, source_target_pairs={{0,1},{1,0},{2,3},{3,2},{4,5},{5,4},{6,7},{7,6},{8,9},{9,8},{10,11... | collective-permute-start | bytes 663560 | tf_op jit(solution)/shard_map/ppermute | solution.py:25
  6.6 5.2 %collective-permute-start.3 = (bf16[48,1152]{1,0:T(8,128)(2,1)S(1)}, bf16[48,1152]{1,0:T(8,128)(2,1)S(1)}, u32[]{:S(2)}, u32[]{:S(2)}) collective-permute-start(bf16[48,1152]{1,0:T(8,128)(2,1)S(1)} %fusion.25), channel_id=1, source_target_pairs={{0,2},{2,0},{1,3},{3,1},{4,6},{6,4},{5,7},{7,5},{8,10},{10,8},{9,1... | collective-permute-start | bytes 331784 | tf_op jit(solution)/shard_map/ppermute | solution.py:25
  9.3 4.9 %collective-permute-start.1 = (bf16[48,1152]{1,0:T(8,128)(2,1)S(1)}, bf16[48,1152]{1,0:T(8,128)(2,1)S(1)}, u32[]{:S(2)}, u32[]{:S(2)}) collective-permute-start(bf16[48,1152]{1,0:T(8,128)(2,1)S(1)} %fusion.24), channel_id=1, source_target_pairs={{0,2},{2,0},{1,3},{3,1},{4,6},{6,4},{5,7},{7,5},{8,10},{10,8},{9,1... | collective-permute-start | bytes 331784 | tf_op jit(solution)/shard_map/ppermute | solution.py:25
  16.5 7.0 %collective-permute-start.4 = (bf16[48,1152]{1,0:T(8,128)(2,1)}, bf16[48,1152]{1,0:T(8,128)(2,1)}, u32[]{:S(2)}, u32[]{:S(2)}) collective-permute-start(bf16[48,1152]{1,0:T(8,128)(2,1)} %fusion.35), channel_id=1, source_target_pairs={{0,1},{1,0},{2,3},{3,2},{4,5},{5,4},{6,7},{7,6},{8,9},{9,8},{10,11... | collective-permute-start | bytes 331784 | tf_op jit(solution)/shard_map/ppermute | solution.py:25
  16.5 35.0 %all-to-all-start = ((bf16[16,48,1152]{2,1,0:T(8,128)(2,1)}), bf16[16,48,1152]{2,1,0:T(8,128)(2,1)S(1)}, u32[]{:S(2)}, u32[]{:S(2)}) async-start(bf16[16,48,1152]{2,1,0:T(8,128)(2,1)} %broadcast_in_dim.2), calls=%async_computation | async-start | bytes 3538944 | tf_op jit(solution)/shard_map/all_to_all | solution.py:184
  24.6 14.2 %collective-permute-start.7 = (bf16[96,1152]{1,0:T(8,128)(2,1)S(1)}, bf16[96,1152]{1,0:T(8,128)(2,1)S(1)}, u32[]{:S(2)}, u32[]{:S(2)}) collective-permute-start(bf16[96,1152]{1,0:T(8,128)(2,1)S(1)} %pad_maximum_fusion.8), channel_id=1, source_target_pairs={{0,48},{16,64},{32,80},{48,96},{64,112},{80,0},{96,16},{112,32},{1... | collective-permute-start | bytes 663560 | tf_op jit(solution)/shard_map/ppermute | solution.py:57
  30.5 10.2 %collective-permute-start.5 = (bf16[96,1152]{1,0:T(8,128)(2,1)S(1)}, bf16[96,1152]{1,0:T(8,128)(2,1)S(1)}, u32[]{:S(2)}, u32[]{:S(2)}) collective-permute-start(bf16[96,1152]{1,0:T(8,128)(2,1)S(1)} %pad_maximum_fusion.8), channel_id=1, source_target_pairs={{0,16},{16,32},{32,48},{48,64},{64,80},{80,96},{96,112},{112,0},{1... | collective-permute-start | bytes 663560 | tf_op jit(solution)/shard_map/ppermute | solution.py:57
  31.5 13.0 %collective-permute-start.6 = (bf16[96,1152]{1,0:T(8,128)(2,1)S(1)}, bf16[96,1152]{1,0:T(8,128)(2,1)S(1)}, u32[]{:S(2)}, u32[]{:S(2)}) collective-permute-start(bf16[96,1152]{1,0:T(8,128)(2,1)S(1)} %pad_maximum_fusion.8), channel_id=1, source_target_pairs={{0,32},{16,48},{32,64},{48,80},{64,96},{80,112},{96,0},{112,16},{1... | collective-permute-start | bytes 663560 | tf_op jit(solution)/shard_map/ppermute | solution.py:57
  38.9 7.5 %collective-permute-start.8 = (bf16[48,1152]{1,0:T(8,128)(2,1)S(1)}, bf16[48,1152]{1,0:T(8,128)(2,1)S(1)}, u32[]{:S(2)}, u32[]{:S(2)}) collective-permute-start(bf16[48,1152]{1,0:T(8,128)(2,1)S(1)} %slice_select_fusion), channel_id=1, source_target_pairs={{0,16},{16,32},{32,48},{48,64},{64,80},{80,96},{96,112},{112,0},{1... | collective-permute-start | bytes 331784 | tf_op jit(solution)/shard_map/ppermute | solution.py:57
  60.9 5.1 %collective-permute-start.10 = (bf16[336,1152]{1,0:T(8,128)(2,1)S(1)}, bf16[336,1152]{1,0:T(8,128)(2,1)S(1)}, u32[]{:S(2)}, u32[]{:S(2)}) collective-permute-start(bf16[336,1152]{1,0:T(8,128)(2,1)S(1)} %slice.226), channel_id=1, source_target_pairs={{0,1},{1,0},{2,3},{3,2},{4,5},{5,4},{6,7},{7,6},{8,9},{9,8},{10,11... | collective-permute-start | bytes 2322440 | tf_op jit(solution)/shard_map/ppermute | solution.py:25
  66.9 31.9 %all-to-all-start.1 = ((bf16[16,48,1152]{2,1,0:T(8,128)(2,1)}), bf16[16,48,1152]{2,1,0:T(8,128)(2,1)S(1)}, u32[]{:S(2)}, u32[]{:S(2)}) async-start(bf16[16,48,1152]{2,1,0:T(8,128)(2,1)} %bitcast.170), calls=%async_computation.1 | async-start | bytes 3538944 | tf_op jit(solution)/shard_map/all_to_all | solution.py:202
  72.2 14.0 %collective-permute-start.11 = (bf16[96,1152]{1,0:T(8,128)(2,1)S(1)}, bf16[96,1152]{1,0:T(8,128)(2,1)S(1)}, u32[]{:S(2)}, u32[]{:S(2)}) collective-permute-start(bf16[96,1152]{1,0:T(8,128)(2,1)S(1)} %get-tuple-element.32), channel_id=1, source_target_pairs={{0,80},{16,96},{32,112},{48,0},{64,16},{80,32},{96,48},{112,64},{1... | collective-permute-start | bytes 663560 | tf_op jit(solution)/shard_map/ppermute | solution.py:57
  78.1 12.8 %collective-permute-start.12 = (bf16[96,1152]{1,0:T(8,128)(2,1)S(1)}, bf16[96,1152]{1,0:T(8,128)(2,1)S(1)}, u32[]{:S(2)}, u32[]{:S(2)}) collective-permute-start(bf16[96,1152]{1,0:T(8,128)(2,1)S(1)} %get-tuple-element.34), channel_id=1, source_target_pairs={{0,96},{16,112},{32,0},{48,16},{64,32},{80,48},{96,64},{112,80},{1... | collective-permute-start | bytes 663560 | tf_op jit(solution)/shard_map/ppermute | solution.py:57
  79.5 14.8 %collective-permute-start.13 = (bf16[96,1152]{1,0:T(8,128)(2,1)S(1)}, bf16[96,1152]{1,0:T(8,128)(2,1)S(1)}, u32[]{:S(2)}, u32[]{:S(2)}) collective-permute-start(bf16[96,1152]{1,0:T(8,128)(2,1)S(1)} %get-tuple-element.33), channel_id=1, source_target_pairs={{0,112},{16,0},{32,16},{48,32},{64,48},{80,64},{96,80},{112,96},{1... | collective-permute-start | bytes 663560 | tf_op jit(solution)/shard_map/ppermute | solution.py:57
  81.3 18.0 %collective-permute-start.14 = (bf16[48,1152]{1,0:T(8,128)(2,1)}, bf16[48,1152]{1,0:T(8,128)(2,1)}, u32[]{:S(2)}, u32[]{:S(2)}) collective-permute-start(bf16[48,1152]{1,0:T(8,128)(2,1)} %add_convert_fusion.3), channel_id=1, source_target_pairs={{0,64},{16,80},{32,96},{48,112},{64,0},{80,16},{96,32},{112,48},{1... | collective-permute-start | bytes 331784 | tf_op jit(solution)/shard_map/ppermute | solution.py:57
  110.6 10.5 %collective-permute-start.16 = (bf16[2,40,1152]{2,1,0:T(8,128)(2,1)S(1)}, bf16[2,40,1152]{2,1,0:T(8,128)(2,1)S(1)}, u32[]{:S(2)}, u32[]{:S(2)}) collective-permute-start(bf16[2,40,1152]{2,1,0:T(8,128)(2,1)S(1)} %fusion.19), channel_id=1, source_target_pairs={{0,4},{4,8},{8,12},{12,0},{1,5},{5,9},{9,13},{13,1},{2,6},{6,10},{... | collective-permute-start | bytes 552968 | tf_op jit(solution)/shard_map/ppermute | solution.py:20
  111.8 5.8 %collective-permute-start.18 = (bf16[2,32,1152]{2,1,0:T(8,128)(2,1)S(1)}, bf16[2,32,1152]{2,1,0:T(8,128)(2,1)S(1)}, u32[]{:S(2)}, u32[]{:S(2)}) collective-permute-start(bf16[2,32,1152]{2,1,0:T(8,128)(2,1)S(1)} %pad_maximum_fusion.10), channel_id=1, source_target_pairs={{0,12},{4,0},{8,4},{12,8},{1,13},{5,1},{9,5},{13,9},{2,14},{6,2},{... | collective-permute-start | bytes 442376 | tf_op jit(solution)/shard_map/ppermute | solution.py:20
  117.7 9.9 %collective-permute-start.19 = (bf16[2,72,1152]{2,1,0:T(8,128)(2,1)S(1)}, bf16[2,72,1152]{2,1,0:T(8,128)(2,1)S(1)}, u32[]{:S(2)}, u32[]{:S(2)}) collective-permute-start(bf16[2,72,1152]{2,1,0:T(8,128)(2,1)S(1)} %pad_maximum_fusion.3), channel_id=1, source_target_pairs={{0,12},{4,0},{8,4},{12,8},{1,13},{5,1},{9,5},{13,9},{2,14},{6,2},{... | collective-permute-start | bytes 995336 | tf_op jit(solution)/shard_map/ppermute | solution.py:20
  121.2 9.9 %collective-permute-start.17 = (bf16[2,72,1152]{2,1,0:T(8,128)(2,1)S(1)}, bf16[2,72,1152]{2,1,0:T(8,128)(2,1)S(1)}, u32[]{:S(2)}, u32[]{:S(2)}) collective-permute-start(bf16[2,72,1152]{2,1,0:T(8,128)(2,1)S(1)} %pad_maximum_fusion.2), channel_id=1, source_target_pairs={{0,4},{4,8},{8,12},{12,0},{1,5},{5,9},{9,13},{13,1},{2,6},{6,10},{... | collective-permute-start | bytes 995336 | tf_op jit(solution)/shard_map/ppermute | solution.py:20
  132.9 11.2 %collective-permute-start.22 = (bf16[2,168,128]{2,1,0:T(8,128)(2,1)S(1)}, bf16[2,168,128]{2,1,0:T(8,128)(2,1)S(1)}, u32[]{:S(2)}, u32[]{:S(2)}) collective-permute-start(bf16[2,168,128]{2,1,0:T(8,128)(2,1)S(1)} %pad_maximum_fusion.13), channel_id=1, source_target_pairs={{0,16},{16,32},{32,48},{48,64},{64,80},{80,96},{96,112},{112,0},{1... | collective-permute-start | bytes 258056 | tf_op jit(solution)/shard_map/ppermute | solution.py:57
  134.8 9.3 %collective-permute-start.23 = (bf16[2,168,128]{2,1,0:T(8,128)(2,1)S(1)}, bf16[2,168,128]{2,1,0:T(8,128)(2,1)S(1)}, u32[]{:S(2)}, u32[]{:S(2)}) collective-permute-start(bf16[2,168,128]{2,1,0:T(8,128)(2,1)S(1)} %pad_maximum_fusion.14), channel_id=1, source_target_pairs={{0,32},{16,48},{32,64},{48,80},{64,96},{80,112},{96,0},{112,16},{1... | collective-permute-start | bytes 258056 | tf_op jit(solution)/shard_map/ppermute | solution.py:57
  140.6 9.6 %collective-permute-start.24 = (bf16[2,168,128]{2,1,0:T(8,128)(2,1)S(1)}, bf16[2,168,128]{2,1,0:T(8,128)(2,1)S(1)}, u32[]{:S(2)}, u32[]{:S(2)}) collective-permute-start(bf16[2,168,128]{2,1,0:T(8,128)(2,1)S(1)} %pad_maximum_fusion.15), channel_id=1, source_target_pairs={{0,48},{16,64},{32,80},{48,96},{64,112},{80,0},{96,16},{112,32},{1... | collective-permute-start | bytes 258056 | tf_op jit(solution)/shard_map/ppermute | solution.py:57
  143.6 7.9 %collective-permute-start.20 = (bf16[168,128]{1,0:T(8,128)(2,1)S(1)}, bf16[168,128]{1,0:T(8,128)(2,1)S(1)}, u32[]{:S(2)}, u32[]{:S(2)}) collective-permute-start(bf16[168,128]{1,0:T(8,128)(2,1)S(1)} %get-tuple-element.41), channel_id=1, source_target_pairs={{0,64},{16,80},{32,96},{48,112},{64,0},{80,16},{96,32},{112,48},{1... | collective-permute-start | bytes 129032 | tf_op jit(solution)/shard_map/ppermute | solution.py:57
  151.6 5.6 %collective-permute-start.26 = (bf16[168,128]{1,0:T(8,128)(2,1)S(1)}, bf16[168,128]{1,0:T(8,128)(2,1)S(1)}, u32[]{:S(2)}, u32[]{:S(2)}) collective-permute-start(bf16[168,128]{1,0:T(8,128)(2,1)S(1)} %fusion.27), channel_id=1, source_target_pairs={{0,128},{128,0},{1,129},{129,1},{2,130},{130,2},{3,131},{131,3},{4... | collective-permute-start | bytes 129032 | tf_op jit(solution)/shard_map/ppermute | solution.py:25
  157.8 8.5 %collective-permute-start.27 = (bf16[168,128]{1,0:T(8,128)(2,1)S(1)}, bf16[168,128]{1,0:T(8,128)(2,1)S(1)}, u32[]{:S(2)}, u32[]{:S(2)}) collective-permute-start(bf16[168,128]{1,0:T(8,128)(2,1)S(1)} %get-tuple-element.29), channel_id=1, source_target_pairs={{0,64},{16,80},{32,96},{48,112},{64,0},{80,16},{96,32},{112,48},{1... | collective-permute-start | bytes 129032 | tf_op jit(solution)/shard_map/ppermute | solution.py:57
  160.5 5.9 %collective-permute-start.29 = (bf16[2,168,128]{2,1,0:T(8,128)(2,1)S(1)}, bf16[2,168,128]{2,1,0:T(8,128)(2,1)S(1)}, u32[]{:S(2)}, u32[]{:S(2)}) collective-permute-start(bf16[2,168,128]{2,1,0:T(8,128)(2,1)S(1)} %pad_maximum_fusion.16), channel_id=1, source_target_pairs={{0,16},{16,32},{32,48},{48,64},{64,80},{80,96},{96,112},{112,0},{1... | collective-permute-start | bytes 258056 | tf_op jit(solution)/shard_map/ppermute | solution.py:57
  161.7 7.5 %collective-permute-start.30 = (bf16[2,168,128]{2,1,0:T(8,128)(2,1)S(1)}, bf16[2,168,128]{2,1,0:T(8,128)(2,1)S(1)}, u32[]{:S(2)}, u32[]{:S(2)}) collective-permute-start(bf16[2,168,128]{2,1,0:T(8,128)(2,1)S(1)} %pad_maximum_fusion.16), channel_id=1, source_target_pairs={{0,32},{16,48},{32,64},{48,80},{64,96},{80,112},{96,0},{112,16},{1... | collective-permute-start | bytes 258056 | tf_op jit(solution)/shard_map/ppermute | solution.py:57
  163.1 9.8 %collective-permute-start.31 = (bf16[2,168,128]{2,1,0:T(8,128)(2,1)S(1)}, bf16[2,168,128]{2,1,0:T(8,128)(2,1)S(1)}, u32[]{:S(2)}, u32[]{:S(2)}) collective-permute-start(bf16[2,168,128]{2,1,0:T(8,128)(2,1)S(1)} %pad_maximum_fusion.16), channel_id=1, source_target_pairs={{0,48},{16,64},{32,80},{48,96},{64,112},{80,0},{96,16},{112,32},{1... | collective-permute-start | bytes 258056 | tf_op jit(solution)/shard_map/ppermute | solution.py:57
  174.9 11.9 %collective-permute-start.33 = (bf16[2,72,1152]{2,1,0:T(8,128)(2,1)S(1)}, bf16[2,72,1152]{2,1,0:T(8,128)(2,1)S(1)}, u32[]{:S(2)}, u32[]{:S(2)}) collective-permute-start(bf16[2,72,1152]{2,1,0:T(8,128)(2,1)S(1)} %bitcast.174), channel_id=1, source_target_pairs={{0,12},{4,0},{8,4},{12,8},{1,13},{5,1},{9,5},{13,9},{2,14},{6,2},{... | collective-permute-start | bytes 995336 | tf_op jit(solution)/shard_map/ppermute | solution.py:20
  175.1 11.2 %collective-permute-start.34 = (bf16[2,72,1152]{2,1,0:T(8,128)(2,1)S(1)}, bf16[2,72,1152]{2,1,0:T(8,128)(2,1)S(1)}, u32[]{:S(2)}, u32[]{:S(2)}) collective-permute-start(bf16[2,72,1152]{2,1,0:T(8,128)(2,1)S(1)} %bitcast.175), channel_id=1, source_target_pairs={{0,4},{4,8},{8,12},{12,0},{1,5},{5,9},{9,13},{13,1},{2,6},{6,10},{... | collective-permute-start | bytes 995336 | tf_op jit(solution)/shard_map/ppermute | solution.py:20
  186.3 7.3 %collective-permute-start.35 = (bf16[2,40,1152]{2,1,0:T(8,128)(2,1)S(1)}, bf16[2,40,1152]{2,1,0:T(8,128)(2,1)S(1)}, u32[]{:S(2)}, u32[]{:S(2)}) collective-permute-start(bf16[2,40,1152]{2,1,0:T(8,128)(2,1)S(1)} %slice.252), channel_id=1, source_target_pairs={{0,4},{4,8},{8,12},{12,0},{1,5},{5,9},{9,13},{13,1},{2,6},{6,10},{... | collective-permute-start | bytes 552968 | tf_op jit(solution)/shard_map/ppermute | solution.py:20
  186.8 5.5 %collective-permute-start.36 = (bf16[2,32,1152]{2,1,0:T(8,128)(2,1)S(1)}, bf16[2,32,1152]{2,1,0:T(8,128)(2,1)S(1)}, u32[]{:S(2)}, u32[]{:S(2)}) collective-permute-start(bf16[2,32,1152]{2,1,0:T(8,128)(2,1)S(1)} %slice.254), channel_id=1, source_target_pairs={{0,12},{4,0},{8,4},{12,8},{1,13},{5,1},{9,5},{13,9},{2,14},{6,2},{... | collective-permute-start | bytes 442376 | tf_op jit(solution)/shard_map/ppermute | solution.py:20
  (23 other events, 133.1 us)

commit v5 on v4

--- a/solution.py
+++ b/solution.py
@@ -69,7 +69,7 @@
     return jnp.concatenate([pair, mine, flip(mine, "core", 1)], axis=0), images
 
 
-def column_sum(parts, swapped, rows):
+def column_sum(parts, swapped, rows, image_sent):
     first = lax.axis_index("core") == 0
     own = parts[: 2 * rows].astype(F32)
 
@@ -77,11 +77,17 @@
         mine = parts[2 * rows + start : 2 * rows + stop].astype(F32)
         return (mine + swapped[start:stop].astype(F32)).astype(BF16)
 
-    half = column_shift(sent(6 * rows, 7 * rows), -4).astype(F32)
-    for k in (3, 2, 1):
+    relay = column_shift(sent(6 * rows, 7 * rows), -1)
+    none = jnp.zeros_like(relay)
+    relay = jnp.concatenate([jnp.where(first, relay, none), jnp.where(first, none, relay)], axis=0)
+    last = parts[6 * rows : 8 * rows].astype(F32) + swapped[4 * rows : 6 * rows].astype(F32)
+    last = (last + relay.astype(F32)).astype(BF16)
+    own = own + column_shift(last, -3).astype(F32)
+    for k in (2, 1):
         own = own + column_shift(sent(2 * rows * (k - 1), 2 * rows * k), -k).astype(F32)
+    own, image_sent = lax.optimization_barrier((own, image_sent))
     send = jnp.where(first, own[rows:], own[:rows]).astype(BF16)
-    return jnp.where(first, own[:rows], own[rows:]) + half + flip(send, "core", 1).astype(F32)
+    return jnp.where(first, own[:rows], own[rows:]) + flip(send, "core", 1).astype(F32), image_sent
 
 
 def to_tiles(grad, pieces):
@@ -200,7 +206,7 @@
     image_part = jnp.dot(weights, texts, preferred_element_type=F32).astype(BF16)
     image_part, swapped = lax.optimization_barrier((image_part, swapped))
     image_sent = lax.all_to_all(image_part.reshape(plane, quarter, width), PLANE, 0, 0)
-    grad_text_emb = column_sum(text_part, swapped, quarter)
+    grad_text_emb, image_sent = column_sum(text_part, swapped, quarter, image_sent)
     text_grad_raw = backnorm(text_unit, text_radius, grad_text_emb)
     grad_image_emb = jnp.sum(image_sent.astype(F32), axis=0)
     image_grad_raw = backnorm(image_unit, image_radius, grad_image_emb)

time: 196 us -> 193 us (0.985)
  waiting for transfers between devices: 78.4 us -> 84.7 us
  other arithmetic: 13.6 us -> 8.87 us
  starting transfers between devices: 70.5 us -> 67.5 us
  local copies, waits for them, and re-layouts: 8.2 us -> 6.16 us
    ppermute x16, waiting for transfers between devices: 34.3 us -> 39.4 us  [column_shift(): return lax.ppermute(value, ('z', 'core'), pairs)]
    convert_element_type x2 -> x1, other arithmetic: 3.18 us -> 0.04 us  [sent(): return (mine + swapped[start:stop].astype(F32)).astype(BF16)]
    ppermute x13, waiting for transfers between devices: 11.7 us -> 14.4 us  [flip(): return lax.ppermute(value, axis, [(i, i ^ bit) for i in range(n)])]
    ppermute x16, starting transfers between devices: 40.4 us -> 38.1 us  [column_shift(): return lax.ppermute(value, ('z', 'core'), pairs)]
    convert_element_type x0 -> x1, other arithmetic: none -> 2.3 us  [column_sum(): last = (last + relay.astype(F32)).astype(BF16)]
    all_to_all x1, waiting for transfers between devices: 2.13 us -> 0.01 us  [per_device(): lax.all_to_all(image_part.reshape(plane, quarter, width), PLANE, 0, 0)]
    unnamed x35 -> x31, local copies, waits for them, and re-layouts: 5.29 us -> 3.92 us
  transfers between devices with their start and end apart: 39 -> 39, of which waited for: 27 -> 28; matrix products, arithmetic and copies ran while one was open for 9% -> 7% of each run, Pallas kernels for 0% -> 0%
where the time goes in v5:
time: 193 us; the launch traced here: 192 us
  waiting for transfers between devices  84.7 us (44%)
  starting transfers between devices  67.5 us (35%)
  matrix products  14.5 us (8%)
  blocking collectives  9.22 us (5%)
  other arithmetic  8.87 us (5%)
  local copies, waits for them, and re-layouts  6.16 us (3%)
    ppermute x16, waiting for transfers between devices, column_shift(): return lax.ppermute(value, ('z', 'core'), pairs)  39.4 us
    ppermute x16, starting transfers between devices, column_shift(): return lax.ppermute(value, ('z', 'core'), pairs)  38.1 us
    ppermute x8, waiting for transfers between devices, shift(): return lax.ppermute(value, axis, [(i, (i + by) % n) for i in range(n)])  25.8 us
    ppermute x13, waiting for transfers between devices, flip(): return lax.ppermute(value, axis, [(i, i ^ bit) for i in range(n)])  14.4 us
    ppermute x8, starting transfers between devices, shift(): return lax.ppermute(value, axis, [(i, (i + by) % n) for i in range(n)])  12.7 us
    all_gather x1, blocking collectives, per_device(): lax.all_gather(jnp.concatenate([image_grad_raw, text_grad_raw], axis=1),...  9.22 us
    all_to_all x1, starting transfers between devices, per_device(): images = lax.all_to_all(spread, PLANE, 0, 0).reshape(-1, width)  7.04 us
    ppermute x13, starting transfers between devices, flip(): return lax.ppermute(value, axis, [(i, i ^ bit) for i in range(n)])  5.97 us
  transfers between devices with their start and end apart: 39, of which 28 were waited for; matrix products, arithmetic and copies ran while one was open for 7% of the time, Pallas kernels for 0%

profile of v5, /device:TPU:32, one launch (start us, length us, event | category | flops | bytes accessed | tf_op | source)
XLA Modules:
  0.0 192.3 jit_solution(4563411851954626288)
XLA Ops:
  8.2 3.7 %collective-permute-done.3 = bf16[48,1152]{1,0:T(8,128)(2,1)S(1)} collective-permute-done((bf16[48,1152]{1,0:T(8,128)(2,1)S(1)}, bf16[48,1152]{1,0:T(8,128)(2,1)S(1)}, u32[]{:S(2)}, u32[]{:S(2)}) %collective-permute-start.3) | collective-permute-done | bytes 110624 | tf_op jit(solution)/shard_map/ppermute | solution.py:25
  15.2 7.0 %all-to-all-start = ((bf16[16,48,1152]{2,1,0:T(8,128)(2,1)}), bf16[16,48,1152]{2,1,0:T(8,128)(2,1)S(1)}, u32[]{:S(2)}, u32[]{:S(2)}) async-start(bf16[16,48,1152]{2,1,0:T(8,128)(2,1)} %broadcast_in_dim.4), calls=%async_computation | async-start | bytes 3538944 | tf_op jit(solution)/shard_map/all_to_all | solution.py:190
  22.3 5.9 %collective-permute-start.7 = (bf16[96,1152]{1,0:T(8,128)(2,1)S(1)}, bf16[96,1152]{1,0:T(8,128)(2,1)S(1)}, u32[]{:S(2)}, u32[]{:S(2)}) collective-permute-start(bf16[96,1152]{1,0:T(8,128)(2,1)S(1)} %pad_maximum_fusion.8), channel_id=1, source_target_pairs={{0,48},{16,64},{32,80},{48,96},{64,112},{80,0},{96,16},{112,32},{1... | collective-permute-start | bytes 663560 | tf_op jit(solution)/shard_map/ppermute | solution.py:57
  30.7 5.9 %collective-permute-done.7 = bf16[96,1152]{1,0:T(8,128)(2,1)S(1)} collective-permute-done((bf16[96,1152]{1,0:T(8,128)(2,1)S(1)}, bf16[96,1152]{1,0:T(8,128)(2,1)S(1)}, u32[]{:S(2)}, u32[]{:S(2)}) %collective-permute-start.7) | collective-permute-done | bytes 221216 | tf_op jit(solution)/shard_map/ppermute | solution.py:57
  38.4 3.9 %collective-permute-done.6 = bf16[96,1152]{1,0:T(8,128)(2,1)S(1)} collective-permute-done((bf16[96,1152]{1,0:T(8,128)(2,1)S(1)}, bf16[96,1152]{1,0:T(8,128)(2,1)S(1)}, u32[]{:S(2)}, u32[]{:S(2)}) %collective-permute-start.6) | collective-permute-done | bytes 221216 | tf_op jit(solution)/shard_map/ppermute | solution.py:57
  45.0 5.2 %all-to-all-done = bf16[16,48,1152]{2,1,0:T(8,128)(2,1)S(1)} async-done(((bf16[16,48,1152]{2,1,0:T(8,128)(2,1)}), bf16[16,48,1152]{2,1,0:T(8,128)(2,1)S(1)}, u32[]{:S(2)}, u32[]{:S(2)}) %all-to-all-start) | async-done | bytes 1769504 | tf_op jit(solution)/shard_map/all_to_all | solution.py:190
  50.2 2.6 %collective-permute-done.9 = bf16[336,1152]{1,0:T(8,128)(2,1)} collective-permute-done((bf16[336,1152]{1,0:T(8,128)(2,1)}, bf16[336,1152]{1,0:T(8,128)(2,1)}, u32[]{:S(2)}, u32[]{:S(2)}) %collective-permute-start.9) | collective-permute-done | bytes 774176 | tf_op jit(solution)/shard_map/ppermute | solution.py:25
  52.8 3.7 %multiply_convert_fusion = bf16[768,768]{1,0:T(8,128)(2,1)S(1)} fusion(bf16[768,1152]{1,0:T(8,128)(2,1)S(1)} %bitcast.169, s32[768]{0:T(1024)S(1)} %fusion.32, pred[768]{0:T(1024)(128)(4,1)S(1)} %get-tuple-element.65, pred[768]{0:T(1024)(128)(4,1)S(1)} %get-tuple-element.66, bf16[336,1152]{1,0:T(8,128)(2,1)} %collective-permute-done.9, ...), kind=kOutput, calls=%fused_computation.3 | convolution fusion | flops 1373110272 | bytes 4723200 | tf_op jit(solution)/shard_map/dot_general | solution.py:194
  58.7 4.2 %convolution_convert_fusion = bf16[768,1152]{1,0:T(8,128)(2,1)} fusion(bf16[768,768]{1,0:T(8,128)(2,1)S(1)} %multiply_convert_fusion, bf16[336,1152]{1,0:T(8,128)(2,1)} %collective-permute-done.9, bf16[336,1152]{1,0:T(8,128)(2,1)S(1)} %copy-done.6, bf16[48,1152]{1,0:T(8,128)(2,1)S(1)} %get-tuple-element.55, bf16[48,1152]{1,0:T(8,128)(2,1)S(1)} %get-tuple-element.54), kind=kOutput, calls=%fused_computation.1 | convolution fusion | flops 1366917120 | bytes 4718592 | tf_op jit(solution)/shard_map/dot_general | solution.py:206
  63.9 3.7 %all-to-all-start.1 = ((bf16[16,48,1152]{2,1,0:T(8,128)(2,1)}), bf16[16,48,1152]{2,1,0:T(8,128)(2,1)S(1)}, u32[]{:S(2)}, u32[]{:S(2)}) async-start(bf16[16,48,1152]{2,1,0:T(8,128)(2,1)} %bitcast.168), calls=%async_computation.1 | async-start | bytes 3538944 | tf_op jit(solution)/shard_map/all_to_all | solution.py:208
  68.6 2.3 %add_convert_fusion.2 = (bf16[96,1152]{1,0:T(8,128)(2,1)}, bf16[96,1152]{1,0:T(8,128)(2,1)S(1)}, bf16[96,1152]{1,0:T(8,128)(2,1)S(1)}) fusion(bf16[48,1152]{1,0:T(8,128)(2,1)S(1)} %get-tuple-element.64, bf16[48,1152]{1,0:T(8,128)(2,1)S(1)} %get-tuple-element.63, bf16[336,1152]{1,0:T(8,128)(2,1)} %copy-done.7, bf16[768,1152]{1,0:T(8,128)(2,1)} %copy-done.3), kind=kLoop, calls=%fused_computation.24 | loop fusion | flops 1880064 | bytes 2211840 | tf_op jit(solution)/shard_map/convert_element_type | solution.py:84
  70.9 5.8 %collective-permute-start.12 = (bf16[96,1152]{1,0:T(8,128)(2,1)}, bf16[96,1152]{1,0:T(8,128)(2,1)}, u32[]{:S(2)}, u32[]{:S(2)}) collective-permute-start(bf16[96,1152]{1,0:T(8,128)(2,1)} %get-tuple-element.34), channel_id=1, source_target_pairs={{0,80},{16,96},{32,112},{48,0},{64,16},{80,32},{96,48},{112,64},{1... | collective-permute-start | bytes 663560 | tf_op jit(solution)/shard_map/ppermute | solution.py:57
  79.5 4.1 %collective-permute-done.12 = bf16[96,1152]{1,0:T(8,128)(2,1)} collective-permute-done((bf16[96,1152]{1,0:T(8,128)(2,1)}, bf16[96,1152]{1,0:T(8,128)(2,1)}, u32[]{:S(2)}, u32[]{:S(2)}) %collective-permute-start.12) | collective-permute-done | bytes 221216 | tf_op jit(solution)/shard_map/ppermute | solution.py:57
  83.6 5.3 %collective-permute-done.13 = bf16[96,1152]{1,0:T(8,128)(2,1)} collective-permute-done((bf16[96,1152]{1,0:T(8,128)(2,1)S(1)}, bf16[96,1152]{1,0:T(8,128)(2,1)}, u32[]{:S(2)}, u32[]{:S(2)}) %collective-permute-start.13) | collective-permute-done | bytes 221216 | tf_op jit(solution)/shard_map/ppermute | solution.py:57
  89.0 5.5 %collective-permute-done.14 = bf16[96,1152]{1,0:T(8,128)(2,1)} collective-permute-done((bf16[96,1152]{1,0:T(8,128)(2,1)S(1)}, bf16[96,1152]{1,0:T(8,128)(2,1)}, u32[]{:S(2)}, u32[]{:S(2)}) %collective-permute-start.14) | collective-permute-done | bytes 221216 | tf_op jit(solution)/shard_map/ppermute | solution.py:57
  97.9 9.2 %all_gather.3 = bf16[192,2304]{1,0:T(8,128)(2,1)S(1)} all-gather(bf16[48,2304]{1,0:T(8,128)(2,1)S(1)} %pad_maximum_fusion.9), channel_id=1, replica_groups=mesh['yhi'=2,'z'=8,'x'=4,'ylo'=2,'core'=2] {'ylo','core'}, dimensions={0}, use_global_device_ids=true | all-gather | bytes 1105920 | tf_op jit(solution)/shard_map/all_gather | solution.py:214
  108.3 3.2 %collective-permute-start.18 = (bf16[2,32,1152]{2,1,0:T(8,128)(2,1)S(1)}, bf16[2,32,1152]{2,1,0:T(8,128)(2,1)S(1)}, u32[]{:S(2)}, u32[]{:S(2)}) collective-permute-start(bf16[2,32,1152]{2,1,0:T(8,128)(2,1)S(1)} %pad_maximum_fusion.10), channel_id=1, source_target_pairs={{0,12},{4,0},{8,4},{12,8},{1,13},{5,1},{9,5},{13,9},{2,14},{6,2},{... | collective-permute-start | bytes 442376 | tf_op jit(solution)/shard_map/ppermute | solution.py:20
  111.6 3.3 %collective-permute-done.18 = bf16[2,32,1152]{2,1,0:T(8,128)(2,1)S(1)} collective-permute-done((bf16[2,32,1152]{2,1,0:T(8,128)(2,1)S(1)}, bf16[2,32,1152]{2,1,0:T(8,128)(2,1)S(1)}, u32[]{:S(2)}, u32[]{:S(2)}) %collective-permute-start.18) | collective-permute-done | bytes 147488 | tf_op jit(solution)/shard_map/ppermute | solution.py:20
  115.0 3.8 %collective-permute-start.19 = (bf16[2,72,1152]{2,1,0:T(8,128)(2,1)S(1)}, bf16[2,72,1152]{2,1,0:T(8,128)(2,1)S(1)}, u32[]{:S(2)}, u32[]{:S(2)}) collective-permute-start(bf16[2,72,1152]{2,1,0:T(8,128)(2,1)S(1)} %pad_maximum_fusion.3), channel_id=1, source_target_pairs={{0,12},{4,0},{8,4},{12,8},{1,13},{5,1},{9,5},{13,9},{2,14},{6,2},{... | collective-permute-start | bytes 995336 | tf_op jit(solution)/shard_map/ppermute | solution.py:20
  119.0 6.2 %collective-permute-done.19 = bf16[2,72,1152]{2,1,0:T(8,128)(2,1)S(1)} collective-permute-done((bf16[2,72,1152]{2,1,0:T(8,128)(2,1)S(1)}, bf16[2,72,1152]{2,1,0:T(8,128)(2,1)S(1)}, u32[]{:S(2)}, u32[]{:S(2)}) %collective-permute-start.19) | collective-permute-done | bytes 331808 | tf_op jit(solution)/shard_map/ppermute | solution.py:20
  125.2 3.6 %collective-permute-done.17 = bf16[2,72,1152]{2,1,0:T(8,128)(2,1)S(1)} collective-permute-done((bf16[2,72,1152]{2,1,0:T(8,128)(2,1)S(1)}, bf16[2,72,1152]{2,1,0:T(8,128)(2,1)S(1)}, u32[]{:S(2)}, u32[]{:S(2)}) %collective-permute-start.17) | collective-permute-done | bytes 331808 | tf_op jit(solution)/shard_map/ppermute | solution.py:20
  130.5 2.0 %collective-permute-start.22 = (bf16[2,168,128]{2,1,0:T(8,128)(2,1)S(1)}, bf16[2,168,128]{2,1,0:T(8,128)(2,1)S(1)}, u32[]{:S(2)}, u32[]{:S(2)}) collective-permute-start(bf16[2,168,128]{2,1,0:T(8,128)(2,1)S(1)} %pad_maximum_fusion.13), channel_id=1, source_target_pairs={{0,16},{16,32},{32,48},{48,64},{64,80},{80,96},{96,112},{112,0},{1... | collective-permute-start | bytes 258056 | tf_op jit(solution)/shard_map/ppermute | solution.py:57
  132.5 5.0 %collective-permute-start.23 = (bf16[2,168,128]{2,1,0:T(8,128)(2,1)S(1)}, bf16[2,168,128]{2,1,0:T(8,128)(2,1)S(1)}, u32[]{:S(2)}, u32[]{:S(2)}) collective-permute-start(bf16[2,168,128]{2,1,0:T(8,128)(2,1)S(1)} %pad_maximum_fusion.14), channel_id=1, source_target_pairs={{0,32},{16,48},{32,64},{48,80},{64,96},{80,112},{96,0},{112,16},{1... | collective-permute-start | bytes 258056 | tf_op jit(solution)/shard_map/ppermute | solution.py:57
  140.5 5.8 %collective-permute-done.24 = bf16[2,168,128]{2,1,0:T(8,128)(2,1)S(1)} collective-permute-done((bf16[2,168,128]{2,1,0:T(8,128)(2,1)S(1)}, bf16[2,168,128]{2,1,0:T(8,128)(2,1)S(1)}, u32[]{:S(2)}, u32[]{:S(2)}) %collective-permute-start.24) | collective-permute-done | bytes 86048 | tf_op jit(solution)/shard_map/ppermute | solution.py:57
  147.7 2.2 %collective-permute-start.26 = (bf16[168,128]{1,0:T(8,128)(2,1)S(1)}, bf16[168,128]{1,0:T(8,128)(2,1)S(1)}, u32[]{:S(2)}, u32[]{:S(2)}) collective-permute-start(bf16[168,128]{1,0:T(8,128)(2,1)S(1)} %fusion.27), channel_id=1, source_target_pairs={{0,128},{128,0},{1,129},{129,1},{2,130},{130,2},{3,131},{131,3},{4... | collective-permute-start | bytes 129032 | tf_op jit(solution)/shard_map/ppermute | solution.py:25
  149.8 3.5 %collective-permute-done.26 = bf16[168,128]{1,0:T(8,128)(2,1)S(1)} collective-permute-done((bf16[168,128]{1,0:T(8,128)(2,1)S(1)}, bf16[168,128]{1,0:T(8,128)(2,1)S(1)}, u32[]{:S(2)}, u32[]{:S(2)}) %collective-permute-start.26) | collective-permute-done | bytes 43040 | tf_op jit(solution)/shard_map/ppermute | solution.py:25
  153.9 4.3 %collective-permute-start.27 = (bf16[168,128]{1,0:T(8,128)(2,1)S(1)}, bf16[168,128]{1,0:T(8,128)(2,1)S(1)}, u32[]{:S(2)}, u32[]{:S(2)}) collective-permute-start(bf16[168,128]{1,0:T(8,128)(2,1)S(1)} %get-tuple-element.33), channel_id=1, source_target_pairs={{0,64},{16,80},{32,96},{48,112},{64,0},{80,16},{96,32},{112,48},{1... | collective-permute-start | bytes 129032 | tf_op jit(solution)/shard_map/ppermute | solution.py:57
  160.0 3.2 %collective-permute-start.31 = (bf16[2,168,128]{2,1,0:T(8,128)(2,1)S(1)}, bf16[2,168,128]{2,1,0:T(8,128)(2,1)S(1)}, u32[]{:S(2)}, u32[]{:S(2)}) collective-permute-start(bf16[2,168,128]{2,1,0:T(8,128)(2,1)S(1)} %pad_maximum_fusion.16), channel_id=1, source_target_pairs={{0,48},{16,64},{32,80},{48,96},{64,112},{80,0},{96,16},{112,32},{1... | collective-permute-start | bytes 258056 | tf_op jit(solution)/shard_map/ppermute | solution.py:57
  165.5 4.5 %collective-permute-done.31 = bf16[2,168,128]{2,1,0:T(8,128)(2,1)S(1)} collective-permute-done((bf16[2,168,128]{2,1,0:T(8,128)(2,1)S(1)}, bf16[2,168,128]{2,1,0:T(8,128)(2,1)S(1)}, u32[]{:S(2)}, u32[]{:S(2)}) %collective-permute-start.31) | collective-permute-done | bytes 86048 | tf_op jit(solution)/shard_map/ppermute | solution.py:57
  174.3 9.0 %collective-permute-done.34 = bf16[2,72,1152]{2,1,0:T(8,128)(2,1)S(1)} collective-permute-done((bf16[2,72,1152]{2,1,0:T(8,128)(2,1)S(1)}, bf16[2,72,1152]{2,1,0:T(8,128)(2,1)S(1)}, u32[]{:S(2)}, u32[]{:S(2)}) %collective-permute-start.34) | collective-permute-done | bytes 331808 | tf_op jit(solution)/shard_map/ppermute | solution.py:20
  183.9 2.9 %collective-permute-start.36 = (bf16[2,32,1152]{2,1,0:T(8,128)(2,1)S(1)}, bf16[2,32,1152]{2,1,0:T(8,128)(2,1)S(1)}, u32[]{:S(2)}, u32[]{:S(2)}) collective-permute-start(bf16[2,32,1152]{2,1,0:T(8,128)(2,1)S(1)} %slice.252), channel_id=1, source_target_pairs={{0,12},{4,0},{8,4},{12,8},{1,13},{5,1},{9,5},{13,9},{2,14},{6,2},{... | collective-permute-start | bytes 442376 | tf_op jit(solution)/shard_map/ppermute | solution.py:20
  186.8 2.6 %collective-permute-done.36 = bf16[2,32,1152]{2,1,0:T(8,128)(2,1)S(1)} collective-permute-done((bf16[2,32,1152]{2,1,0:T(8,128)(2,1)S(1)}, bf16[2,32,1152]{2,1,0:T(8,128)(2,1)S(1)}, u32[]{:S(2)}, u32[]{:S(2)}) %collective-permute-start.36) | collective-permute-done | bytes 147488 | tf_op jit(solution)/shard_map/ppermute | solution.py:20
  (172 shorter events, 48.0 us)
Async XLA Ops:
  5.9 6.0 %collective-permute-start.3 = (bf16[48,1152]{1,0:T(8,128)(2,1)S(1)}, bf16[48,1152]{1,0:T(8,128)(2,1)S(1)}, u32[]{:S(2)}, u32[]{:S(2)}) collective-permute-start(bf16[48,1152]{1,0:T(8,128)(2,1)S(1)} %fusion.25), channel_id=1, source_target_pairs={{0,2},{2,0},{1,3},{3,1},{4,6},{6,4},{5,7},{7,5},{8,10},{10,8},{9,1... | collective-permute-start | bytes 331784 | tf_op jit(solution)/shard_map/ppermute | solution.py:25
  7.6 5.8 %collective-permute-start.1 = (bf16[48,1152]{1,0:T(8,128)(2,1)S(1)}, bf16[48,1152]{1,0:T(8,128)(2,1)S(1)}, u32[]{:S(2)}, u32[]{:S(2)}) collective-permute-start(bf16[48,1152]{1,0:T(8,128)(2,1)S(1)} %fusion.24), channel_id=1, source_target_pairs={{0,2},{2,0},{1,3},{3,1},{4,6},{6,4},{5,7},{7,5},{8,10},{10,8},{9,1... | collective-permute-start | bytes 331784 | tf_op jit(solution)/shard_map/ppermute | solution.py:25
  15.2 7.0 %collective-permute-start.4 = (bf16[48,1152]{1,0:T(8,128)(2,1)S(1)}, bf16[48,1152]{1,0:T(8,128)(2,1)S(1)}, u32[]{:S(2)}, u32[]{:S(2)}) collective-permute-start(bf16[48,1152]{1,0:T(8,128)(2,1)S(1)} %fusion.35), channel_id=1, source_target_pairs={{0,1},{1,0},{2,3},{3,2},{4,5},{5,4},{6,7},{7,6},{8,9},{9,8},{10,11... | collective-permute-start | bytes 331784 | tf_op jit(solution)/shard_map/ppermute | solution.py:25
  15.2 35.0 %all-to-all-start = ((bf16[16,48,1152]{2,1,0:T(8,128)(2,1)}), bf16[16,48,1152]{2,1,0:T(8,128)(2,1)S(1)}, u32[]{:S(2)}, u32[]{:S(2)}) async-start(bf16[16,48,1152]{2,1,0:T(8,128)(2,1)} %broadcast_in_dim.4), calls=%async_computation | async-start | bytes 3538944 | tf_op jit(solution)/shard_map/all_to_all | solution.py:190
  22.3 14.3 %collective-permute-start.7 = (bf16[96,1152]{1,0:T(8,128)(2,1)S(1)}, bf16[96,1152]{1,0:T(8,128)(2,1)S(1)}, u32[]{:S(2)}, u32[]{:S(2)}) collective-permute-start(bf16[96,1152]{1,0:T(8,128)(2,1)S(1)} %pad_maximum_fusion.8), channel_id=1, source_target_pairs={{0,48},{16,64},{32,80},{48,96},{64,112},{80,0},{96,16},{112,32},{1... | collective-permute-start | bytes 663560 | tf_op jit(solution)/shard_map/ppermute | solution.py:57
  28.2 10.2 %collective-permute-start.5 = (bf16[96,1152]{1,0:T(8,128)(2,1)S(1)}, bf16[96,1152]{1,0:T(8,128)(2,1)S(1)}, u32[]{:S(2)}, u32[]{:S(2)}) collective-permute-start(bf16[96,1152]{1,0:T(8,128)(2,1)S(1)} %pad_maximum_fusion.8), channel_id=1, source_target_pairs={{0,16},{16,32},{32,48},{48,64},{64,80},{80,96},{96,112},{112,0},{1... | collective-permute-start | bytes 663560 | tf_op jit(solution)/shard_map/ppermute | solution.py:57
  29.2 13.0 %collective-permute-start.6 = (bf16[96,1152]{1,0:T(8,128)(2,1)S(1)}, bf16[96,1152]{1,0:T(8,128)(2,1)S(1)}, u32[]{:S(2)}, u32[]{:S(2)}) collective-permute-start(bf16[96,1152]{1,0:T(8,128)(2,1)S(1)} %pad_maximum_fusion.8), channel_id=1, source_target_pairs={{0,32},{16,48},{32,64},{48,80},{64,96},{80,112},{96,0},{112,16},{1... | collective-permute-start | bytes 663560 | tf_op jit(solution)/shard_map/ppermute | solution.py:57
  36.6 7.5 %collective-permute-start.8 = (bf16[48,1152]{1,0:T(8,128)(2,1)S(1)}, bf16[48,1152]{1,0:T(8,128)(2,1)S(1)}, u32[]{:S(2)}, u32[]{:S(2)}) collective-permute-start(bf16[48,1152]{1,0:T(8,128)(2,1)S(1)} %slice_select_fusion), channel_id=1, source_target_pairs={{0,16},{16,32},{32,48},{48,64},{64,80},{80,96},{96,112},{112,0},{1... | collective-permute-start | bytes 331784 | tf_op jit(solution)/shard_map/ppermute | solution.py:57
  58.3 4.6 %collective-permute-start.10 = (bf16[336,1152]{1,0:T(8,128)(2,1)S(1)}, bf16[336,1152]{1,0:T(8,128)(2,1)S(1)}, u32[]{:S(2)}, u32[]{:S(2)}) collective-permute-start(bf16[336,1152]{1,0:T(8,128)(2,1)S(1)} %slice.226), channel_id=1, source_target_pairs={{0,1},{1,0},{2,3},{3,2},{4,5},{5,4},{6,7},{7,6},{8,9},{9,8},{10,11... | collective-permute-start | bytes 2322440 | tf_op jit(solution)/shard_map/ppermute | solution.py:25
  63.8 4.7 %collective-permute-start.11 = (bf16[48,1152]{1,0:T(8,128)(2,1)S(1)}, bf16[48,1152]{1,0:T(8,128)(2,1)S(1)}, u32[]{:S(2)}, u32[]{:S(2)}) collective-permute-start(bf16[48,1152]{1,0:T(8,128)(2,1)S(1)} %add_convert_fusion.3), channel_id=1, source_target_pairs={{0,112},{16,0},{32,16},{48,32},{64,48},{80,64},{96,80},{112,96},{1... | collective-permute-start | bytes 331784 | tf_op jit(solution)/shard_map/ppermute | solution.py:57
  63.9 31.9 %all-to-all-start.1 = ((bf16[16,48,1152]{2,1,0:T(8,128)(2,1)}), bf16[16,48,1152]{2,1,0:T(8,128)(2,1)S(1)}, u32[]{:S(2)}, u32[]{:S(2)}) async-start(bf16[16,48,1152]{2,1,0:T(8,128)(2,1)} %bitcast.168), calls=%async_computation.1 | async-start | bytes 3538944 | tf_op jit(solution)/shard_map/all_to_all | solution.py:208
  70.9 12.7 %collective-permute-start.12 = (bf16[96,1152]{1,0:T(8,128)(2,1)}, bf16[96,1152]{1,0:T(8,128)(2,1)}, u32[]{:S(2)}, u32[]{:S(2)}) collective-permute-start(bf16[96,1152]{1,0:T(8,128)(2,1)} %get-tuple-element.34), channel_id=1, source_target_pairs={{0,80},{16,96},{32,112},{48,0},{64,16},{80,32},{96,48},{112,64},{1... | collective-permute-start | bytes 663560 | tf_op jit(solution)/shard_map/ppermute | solution.py:57
  76.7 12.2 %collective-permute-start.13 = (bf16[96,1152]{1,0:T(8,128)(2,1)S(1)}, bf16[96,1152]{1,0:T(8,128)(2,1)}, u32[]{:S(2)}, u32[]{:S(2)}) collective-permute-start(bf16[96,1152]{1,0:T(8,128)(2,1)S(1)} %get-tuple-element.36), channel_id=1, source_target_pairs={{0,96},{16,112},{32,0},{48,16},{64,32},{80,48},{96,64},{112,80},{1... | collective-permute-start | bytes 663560 | tf_op jit(solution)/shard_map/ppermute | solution.py:57
  78.2 16.2 %collective-permute-start.14 = (bf16[96,1152]{1,0:T(8,128)(2,1)S(1)}, bf16[96,1152]{1,0:T(8,128)(2,1)}, u32[]{:S(2)}, u32[]{:S(2)}) collective-permute-start(bf16[96,1152]{1,0:T(8,128)(2,1)S(1)} %get-tuple-element.35), channel_id=1, source_target_pairs={{0,112},{16,0},{32,16},{48,32},{64,48},{80,64},{96,80},{112,96},{1... | collective-permute-start | bytes 663560 | tf_op jit(solution)/shard_map/ppermute | solution.py:57
  108.2 10.5 %collective-permute-start.16 = (bf16[2,40,1152]{2,1,0:T(8,128)(2,1)S(1)}, bf16[2,40,1152]{2,1,0:T(8,128)(2,1)S(1)}, u32[]{:S(2)}, u32[]{:S(2)}) collective-permute-start(bf16[2,40,1152]{2,1,0:T(8,128)(2,1)S(1)} %fusion.19), channel_id=1, source_target_pairs={{0,4},{4,8},{8,12},{12,0},{1,5},{5,9},{9,13},{13,1},{2,6},{6,10},{... | collective-permute-start | bytes 552968 | tf_op jit(solution)/shard_map/ppermute | solution.py:20
  108.3 6.6 %collective-permute-start.18 = (bf16[2,32,1152]{2,1,0:T(8,128)(2,1)S(1)}, bf16[2,32,1152]{2,1,0:T(8,128)(2,1)S(1)}, u32[]{:S(2)}, u32[]{:S(2)}) collective-permute-start(bf16[2,32,1152]{2,1,0:T(8,128)(2,1)S(1)} %pad_maximum_fusion.10), channel_id=1, source_target_pairs={{0,12},{4,0},{8,4},{12,8},{1,13},{5,1},{9,5},{13,9},{2,14},{6,2},{... | collective-permute-start | bytes 442376 | tf_op jit(solution)/shard_map/ppermute | solution.py:20
  115.0 10.2 %collective-permute-start.19 = (bf16[2,72,1152]{2,1,0:T(8,128)(2,1)S(1)}, bf16[2,72,1152]{2,1,0:T(8,128)(2,1)S(1)}, u32[]{:S(2)}, u32[]{:S(2)}) collective-permute-start(bf16[2,72,1152]{2,1,0:T(8,128)(2,1)S(1)} %pad_maximum_fusion.3), channel_id=1, source_target_pairs={{0,12},{4,0},{8,4},{12,8},{1,13},{5,1},{9,5},{13,9},{2,14},{6,2},{... | collective-permute-start | bytes 995336 | tf_op jit(solution)/shard_map/ppermute | solution.py:20
  118.8 9.9 %collective-permute-start.17 = (bf16[2,72,1152]{2,1,0:T(8,128)(2,1)S(1)}, bf16[2,72,1152]{2,1,0:T(8,128)(2,1)S(1)}, u32[]{:S(2)}, u32[]{:S(2)}) collective-permute-start(bf16[2,72,1152]{2,1,0:T(8,128)(2,1)S(1)} %pad_maximum_fusion.2), channel_id=1, source_target_pairs={{0,4},{4,8},{8,12},{12,0},{1,5},{5,9},{9,13},{13,1},{2,6},{6,10},{... | collective-permute-start | bytes 995336 | tf_op jit(solution)/shard_map/ppermute | solution.py:20
  130.5 10.0 %collective-permute-start.22 = (bf16[2,168,128]{2,1,0:T(8,128)(2,1)S(1)}, bf16[2,168,128]{2,1,0:T(8,128)(2,1)S(1)}, u32[]{:S(2)}, u32[]{:S(2)}) collective-permute-start(bf16[2,168,128]{2,1,0:T(8,128)(2,1)S(1)} %pad_maximum_fusion.13), channel_id=1, source_target_pairs={{0,16},{16,32},{32,48},{48,64},{64,80},{80,96},{96,112},{112,0},{1... | collective-permute-start | bytes 258056 | tf_op jit(solution)/shard_map/ppermute | solution.py:57
  132.5 8.0 %collective-permute-start.23 = (bf16[2,168,128]{2,1,0:T(8,128)(2,1)S(1)}, bf16[2,168,128]{2,1,0:T(8,128)(2,1)S(1)}, u32[]{:S(2)}, u32[]{:S(2)}) collective-permute-start(bf16[2,168,128]{2,1,0:T(8,128)(2,1)S(1)} %pad_maximum_fusion.14), channel_id=1, source_target_pairs={{0,32},{16,48},{32,64},{48,80},{64,96},{80,112},{96,0},{112,16},{1... | collective-permute-start | bytes 258056 | tf_op jit(solution)/shard_map/ppermute | solution.py:57
  137.6 8.7 %collective-permute-start.24 = (bf16[2,168,128]{2,1,0:T(8,128)(2,1)S(1)}, bf16[2,168,128]{2,1,0:T(8,128)(2,1)S(1)}, u32[]{:S(2)}, u32[]{:S(2)}) collective-permute-start(bf16[2,168,128]{2,1,0:T(8,128)(2,1)S(1)} %pad_maximum_fusion.15), channel_id=1, source_target_pairs={{0,48},{16,64},{32,80},{48,96},{64,112},{80,0},{96,16},{112,32},{1... | collective-permute-start | bytes 258056 | tf_op jit(solution)/shard_map/ppermute | solution.py:57
  138.7 8.2 %collective-permute-start.20 = (bf16[168,128]{1,0:T(8,128)(2,1)S(1)}, bf16[168,128]{1,0:T(8,128)(2,1)S(1)}, u32[]{:S(2)}, u32[]{:S(2)}) collective-permute-start(bf16[168,128]{1,0:T(8,128)(2,1)S(1)} %get-tuple-element.43), channel_id=1, source_target_pairs={{0,64},{16,80},{32,96},{48,112},{64,0},{80,16},{96,32},{112,48},{1... | collective-permute-start | bytes 129032 | tf_op jit(solution)/shard_map/ppermute | solution.py:57
  147.7 5.6 %collective-permute-start.26 = (bf16[168,128]{1,0:T(8,128)(2,1)S(1)}, bf16[168,128]{1,0:T(8,128)(2,1)S(1)}, u32[]{:S(2)}, u32[]{:S(2)}) collective-permute-start(bf16[168,128]{1,0:T(8,128)(2,1)S(1)} %fusion.27), channel_id=1, source_target_pairs={{0,128},{128,0},{1,129},{129,1},{2,130},{130,2},{3,131},{131,3},{4... | collective-permute-start | bytes 129032 | tf_op jit(solution)/shard_map/ppermute | solution.py:25
  153.9 4.3 %collective-permute-start.28 = (bf16[168,128]{1,0:T(8,128)(2,1)S(1)}, bf16[168,128]{1,0:T(8,128)(2,1)S(1)}, u32[]{:S(2)}, u32[]{:S(2)}) collective-permute-start(bf16[168,128]{1,0:T(8,128)(2,1)S(1)} %get-tuple-element.33), channel_id=1, source_target_pairs={{0,1},{1,0},{2,3},{3,2},{4,5},{5,4},{6,7},{7,6},{8,9},{9,8},{10,11... | collective-permute-start | bytes 129032 | tf_op jit(solution)/shard_map/ppermute | solution.py:25
  153.9 10.5 %collective-permute-start.27 = (bf16[168,128]{1,0:T(8,128)(2,1)S(1)}, bf16[168,128]{1,0:T(8,128)(2,1)S(1)}, u32[]{:S(2)}, u32[]{:S(2)}) collective-permute-start(bf16[168,128]{1,0:T(8,128)(2,1)S(1)} %get-tuple-element.33), channel_id=1, source_target_pairs={{0,64},{16,80},{32,96},{48,112},{64,0},{80,16},{96,32},{112,48},{1... | collective-permute-start | bytes 129032 | tf_op jit(solution)/shard_map/ppermute | solution.py:57
  158.2 6.2 %collective-permute-start.29 = (bf16[2,168,128]{2,1,0:T(8,128)(2,1)S(1)}, bf16[2,168,128]{2,1,0:T(8,128)(2,1)S(1)}, u32[]{:S(2)}, u32[]{:S(2)}) collective-permute-start(bf16[2,168,128]{2,1,0:T(8,128)(2,1)S(1)} %pad_maximum_fusion.16), channel_id=1, source_target_pairs={{0,16},{16,32},{32,48},{48,64},{64,80},{80,96},{96,112},{112,0},{1... | collective-permute-start | bytes 258056 | tf_op jit(solution)/shard_map/ppermute | solution.py:57
  158.9 6.7 %collective-permute-start.30 = (bf16[2,168,128]{2,1,0:T(8,128)(2,1)S(1)}, bf16[2,168,128]{2,1,0:T(8,128)(2,1)S(1)}, u32[]{:S(2)}, u32[]{:S(2)}) collective-permute-start(bf16[2,168,128]{2,1,0:T(8,128)(2,1)S(1)} %pad_maximum_fusion.16), channel_id=1, source_target_pairs={{0,32},{16,48},{32,64},{48,80},{64,96},{80,112},{96,0},{112,16},{1... | collective-permute-start | bytes 258056 | tf_op jit(solution)/shard_map/ppermute | solution.py:57
  160.0 10.0 %collective-permute-start.31 = (bf16[2,168,128]{2,1,0:T(8,128)(2,1)S(1)}, bf16[2,168,128]{2,1,0:T(8,128)(2,1)S(1)}, u32[]{:S(2)}, u32[]{:S(2)}) collective-permute-start(bf16[2,168,128]{2,1,0:T(8,128)(2,1)S(1)} %pad_maximum_fusion.16), channel_id=1, source_target_pairs={{0,48},{16,64},{32,80},{48,96},{64,112},{80,0},{96,16},{112,32},{1... | collective-permute-start | bytes 258056 | tf_op jit(solution)/shard_map/ppermute | solution.py:57
  172.0 11.9 %collective-permute-start.33 = (bf16[2,72,1152]{2,1,0:T(8,128)(2,1)S(1)}, bf16[2,72,1152]{2,1,0:T(8,128)(2,1)S(1)}, u32[]{:S(2)}, u32[]{:S(2)}) collective-permute-start(bf16[2,72,1152]{2,1,0:T(8,128)(2,1)S(1)} %bitcast.174), channel_id=1, source_target_pairs={{0,12},{4,0},{8,4},{12,8},{1,13},{5,1},{9,5},{13,9},{2,14},{6,2},{... | collective-permute-start | bytes 995336 | tf_op jit(solution)/shard_map/ppermute | solution.py:20
  172.2 11.2 %collective-permute-start.34 = (bf16[2,72,1152]{2,1,0:T(8,128)(2,1)S(1)}, bf16[2,72,1152]{2,1,0:T(8,128)(2,1)S(1)}, u32[]{:S(2)}, u32[]{:S(2)}) collective-permute-start(bf16[2,72,1152]{2,1,0:T(8,128)(2,1)S(1)} %bitcast.175), channel_id=1, source_target_pairs={{0,4},{4,8},{8,12},{12,0},{1,5},{5,9},{9,13},{13,1},{2,6},{6,10},{... | collective-permute-start | bytes 995336 | tf_op jit(solution)/shard_map/ppermute | solution.py:20
  183.4 7.3 %collective-permute-start.35 = (bf16[2,40,1152]{2,1,0:T(8,128)(2,1)S(1)}, bf16[2,40,1152]{2,1,0:T(8,128)(2,1)S(1)}, u32[]{:S(2)}, u32[]{:S(2)}) collective-permute-start(bf16[2,40,1152]{2,1,0:T(8,128)(2,1)S(1)} %slice.250), channel_id=1, source_target_pairs={{0,4},{4,8},{8,12},{12,0},{1,5},{5,9},{9,13},{13,1},{2,6},{6,10},{... | collective-permute-start | bytes 552968 | tf_op jit(solution)/shard_map/ppermute | solution.py:20
  183.9 5.5 %collective-permute-start.36 = (bf16[2,32,1152]{2,1,0:T(8,128)(2,1)S(1)}, bf16[2,32,1152]{2,1,0:T(8,128)(2,1)S(1)}, u32[]{:S(2)}, u32[]{:S(2)}) collective-permute-start(bf16[2,32,1152]{2,1,0:T(8,128)(2,1)S(1)} %slice.252), channel_id=1, source_target_pairs={{0,12},{4,0},{8,4},{12,8},{1,13},{5,1},{9,5},{13,9},{2,14},{6,2},{... | collective-permute-start | bytes 442376 | tf_op jit(solution)/shard_map/ppermute | solution.py:20
  (21 other events, 112.0 us)
